TPU v7x, 256 devices: a whole 4x4x8 slice. The times are simulated.
256 devices in a mesh: fsdp: 32 (over z, x_hi, core), tp: 8 (over y, x_lo).
Axes of the slice: x: 4 (x_hi: 2, x_lo: 2; x = x_hi * 2 + x_lo), y: 4, z: 8, core: 2. Of those that a mesh axis runs over, the one named last changes fastest.
Arguments:
- activations: bfloat16 [32768, 4096], P('fsdp', 'tp'), may hold values from -6 to 6
- cotangent: bfloat16 [32768, 8192], P('fsdp', 'tp'), may hold values from -0.03125 to 0.03125
- weight: bfloat16 [4096, 8192], P('fsdp', 'tp'), may hold values from -0.09375 to 0.09375
- queries: bfloat16 [512, 4, 8, 4, 128], P('fsdp', None, 'tp'), may hold values from -200 to 200
- new_keys: bfloat16 [512, 4, 8, 128], P('fsdp', None, 'tp'), may hold values from -6 to 6
- new_values: bfloat16 [512, 4, 8, 128], P('fsdp', None, 'tp'), may hold values from -24 to 24
- key_cache: bfloat16 [512, 8, 512, 128], P('fsdp', 'tp'), may hold values from -6 to 6
- value_cache: bfloat16 [512, 8, 512, 128], P('fsdp', 'tp'), may hold values from -24 to 24
- cache_lengths: int32 [512], P('fsdp'), may hold values from 2 to 512, as said below
Outputs:
- grad_weight: float32 [4096, 8192], P('fsdp', 'tp')
- decoded: bfloat16 [512, 4, 8192], P('fsdp', None, 'tp')
Inputs may be any that keep to these rules, and one draw needn't show every extreme that they name: `cache_lengths`: some row holds exactly 512 cached positions and some row exactly 2.
All inputs are finite; a program needn't handle non-finite values.
Results may differ from a plain program's by a relative error of at most 0.025.
Values may be sent and summed in bfloat16 or wider, within the bound.
No kernel may reach another device: no remote copies, remote signals or barrier semaphores. Data moves between devices by JAX's collectives and lax.ppermute only.
A program may use at most 128 MiB of HBM per device.

v0:
```python
import functools

import jax
import jax.numpy as jnp
from jax import lax
from jax.experimental import pallas as pl
from jax.experimental.pallas import tpu as pltpu
from jax.sharding import Mesh, PartitionSpec as P

QB = 128
NZ = 8
NY = 4

learn_rate = 0.01
scale_limit = 448.0
epsilon = 1e-06

F32 = jnp.float32
BF16 = jnp.bfloat16
NT = (((1,), (1,)), ((), ()))


def shift(x, axis, size, step):
    return lax.ppermute(x, axis, [(i, (i + step) % size) for i in range(size)])


def swap(x, axis):
    return lax.ppermute(x, axis, [(0, 1), (1, 0)])


def pick(x, index, axis=0):
    return lax.dynamic_index_in_dim(x, index, axis, keepdims=False)


def attend_kernel(steps, len_ref, q_ref, nk_ref, nv_ref, k_ref, v_ref, out_ref):
    rows, count, head = q_ref.shape
    factor = head ** (-0.5)
    first = pl.program_id(0) * rows
    places = lax.broadcasted_iota(jnp.int32, (count, k_ref.shape[1]), 1)
    step = lax.broadcasted_iota(jnp.int32, (count, nk_ref.shape[1]), 0) % steps
    later = lax.broadcasted_iota(jnp.int32, (count, nk_ref.shape[1]), 1) > step
    for r in range(rows):
        q = q_ref[r]
        old = lax.dot_general(q, k_ref[r], NT, preferred_element_type=F32) * factor
        new = lax.dot_general(q, nk_ref[r], NT, preferred_element_type=F32) * factor
        old = jnp.where(places < len_ref[first + r], old, -jnp.inf)
        new = jnp.where(later, -jnp.inf, new)
        top = jnp.maximum(
            jnp.max(old, axis=1, keepdims=True), jnp.max(new, axis=1, keepdims=True)
        )
        old, new = jnp.exp(old - top), jnp.exp(new - top)
        total = jnp.sum(old, axis=1, keepdims=True) + jnp.sum(new, axis=1, keepdims=True)
        old, new = (old / total).astype(BF16), (new / total).astype(BF16)
        mixed = jnp.dot(old, v_ref[r], preferred_element_type=F32)
        mixed = mixed + jnp.dot(new, nv_ref[r], preferred_element_type=F32)
        out_ref[r] = mixed.astype(BF16)


def attend(queries, new_keys, new_values, key_cache, value_cache, cache_lengths):
    rows, steps, _, heads, size = queries.shape
    cache = key_cache.shape[2]
    tile = 4
    q = queries[:, :, 0].transpose(0, 2, 1, 3).reshape(rows, heads * steps, size)
    pad = ((0, 0), (0, 16 - steps), (0, 0))
    nk, nv = jnp.pad(new_keys[:, :, 0], pad), jnp.pad(new_values[:, :, 0], pad)

    def block(height):
        return pl.BlockSpec((tile, height, size), lambda i: (i, 0, 0))

    return pl.pallas_call(
        functools.partial(attend_kernel, steps),
        grid=(rows // tile,),
        out_shape=jax.ShapeDtypeStruct((rows, heads * steps, size), BF16),
        in_specs=[pl.BlockSpec(memory_space=pltpu.SMEM)]
        + [block(heads * steps), block(16), block(16), block(cache), block(cache)],
        out_specs=block(heads * steps),
        cost_estimate=pl.CostEstimate(
            flops=4 * rows * heads * steps * cache * size,
            bytes_accessed=4 * rows * cache * size,
            transcendentals=rows * heads * steps * cache,
        ),
    )(cache_lengths, q, nk, nv, key_cache[:, 0], value_cache[:, 0])


def grad_kernel(names, core_ref, *refs):
    lefts = sorted({left for left, _ in names})
    rights = sorted({right for _, right in names})
    left_refs = dict(zip(lefts, refs))
    right_refs = dict(zip(rights, refs[len(lefts) :]))
    keep_ref, send_ref = refs[-2:]
    own = core_ref[0] == 0
    columns = keep_ref.shape[0]
    for n, (left, right) in enumerate(names):
        part = jnp.dot(
            left_refs[left][...], right_refs[right][...], preferred_element_type=F32
        ).astype(BF16)
        for v in range(columns):
            for w in range(2):
                first = part[2 * w * QB : (2 * w + 1) * QB, v * QB : (v + 1) * QB]
                second = part[(2 * w + 1) * QB : (2 * w + 2) * QB, v * QB : (v + 1) * QB]
                rows = slice((2 * n + w) * QB, (2 * n + w + 1) * QB)
                keep_ref[v, rows] = jnp.where(own, first, second)
                send_ref[v, rows] = jnp.where(own, second, first)


def grad_parts(core, names, lefts, rights):
    left_names = sorted({left for left, _ in names})
    right_names = sorted({right for _, right in names})
    height, depth = lefts[0].shape
    breadth = rights[0].shape[1]
    tile = 2 * QB
    shape = jax.ShapeDtypeStruct((breadth // QB, len(names) * height // 2, QB), BF16)
    out = pl.BlockSpec((tile // QB, shape.shape[1], QB), lambda i: (i, 0, 0))
    return pl.pallas_call(
        functools.partial(grad_kernel, names),
        grid=(breadth // tile,),
        out_shape=(shape, shape),
        in_specs=[pl.BlockSpec(memory_space=pltpu.SMEM)]
        + [pl.BlockSpec((height, depth), lambda i: (0, 0))] * len(left_names)
        + [pl.BlockSpec((depth, tile), lambda i: (0, i))] * len(right_names),
        out_specs=(out, out),
        compiler_params=pltpu.CompilerParams(vmem_limit_bytes=40 * 2**20),
        cost_estimate=pl.CostEstimate(
            flops=2 * len(names) * height * depth * breadth,
            bytes_accessed=2 * (len(left_names) * height * depth + len(names) * height * breadth),
            transcendentals=0,
        ),
    )(
        core.reshape(1),
        *[lefts[n] for n in left_names],
        *[rights[n] for n in right_names],
    )


def project_kernel(own_ref, scale_ref, *refs):
    left_refs, (quant_ref, quant_other_ref, out_ref) = refs[:NY], refs[NY:]
    rows = left_refs[0].shape[0]
    total = jnp.zeros((rows, 2 * QB), F32)
    for k in range(NY):
        for j, quant in enumerate((quant_ref, quant_other_ref)):
            right = jnp.concatenate([quant[k, 0], quant[k, 1]], axis=1)
            product = jnp.dot(
                left_refs[k][:, j * QB : (j + 1) * QB], right, preferred_element_type=F32
            )
            total = total + product * scale_ref[2 * k + j : 2 * k + j + 1, :]
    total = total.astype(BF16)
    swapped = own_ref[0] == 1
    first, second = total[:, :QB], total[:, QB:]
    low, high = jnp.where(swapped, second, first), jnp.where(swapped, first, second)
    count = out_ref.shape[3]
    for v in range(out_ref.shape[0]):
        for w in range(2):
            at = (2 * v + w) * count
            out_ref[v, w, 0] = low[at : at + count]
            out_ref[v, w, 1] = high[at : at + count]


def project(xl, lefts, quantized, quantized_other, scales, count):
    tile = 2
    whole = pl.BlockSpec(quantized.shape, lambda i: (0, 0, 0, 0))
    return pl.pallas_call(
        project_kernel,
        grid=(NZ // tile,),
        out_shape=jax.ShapeDtypeStruct((NZ, 2, 2, count, QB), BF16),
        in_specs=[
            pl.BlockSpec(memory_space=pltpu.SMEM),
            pl.BlockSpec(scales.shape, lambda i: (0, 0)),
        ]
        + [pl.BlockSpec((tile * 2 * count, 2 * QB), lambda i: (i, 0))] * NY
        + [whole, whole],
        out_specs=pl.BlockSpec((tile, 2, 2, count, QB), lambda i: (i, 0, 0, 0, 0)),
        cost_estimate=pl.CostEstimate(
            flops=2 * NZ * 2 * count * 2 * QB * 8 * QB,
            bytes_accessed=4 * 2**20,
            transcendentals=0,
        ),
    )(xl.reshape(1), scales, *lefts, quantized, quantized_other)


def gather_z(x, z):
    half = x.shape[0] // 2
    down, up = [x], [x]
    for k in range(3):
        down.append(shift(down[-1], "z", NZ, 1))
        up.append(shift(up[-1], "z", NZ, -1))
    far = jnp.concatenate(
        [shift(down[3][:half], "z", NZ, 1), shift(up[3][half:], "z", NZ, -1)], axis=0
    )
    ring = [x, up[1], up[2], up[3], far, down[3], down[2], down[1]]
    ring = jnp.stack(ring + ring, axis=0)
    return lax.dynamic_slice_in_dim(ring, NZ - z, NZ, axis=0)


def gather_y(x):
    half = x.shape[0] // 2
    down = shift(x, "y", NY, 1)
    up = shift(x, "y", NY, -1)
    far_a = shift(down[:half], "y", NY, 1)
    far_b = shift(up[half:], "y", NY, -1)
    return x, down, jnp.concatenate([far_a, far_b], axis=0), up


def scatter_z(keep, got, z):
    half = keep.shape[1] // 2

    def block(k):
        index = (z + k) % NZ
        return pick(keep, index).astype(F32) + pick(got, index).astype(F32)

    far = block(4).astype(BF16)
    fwd = shift(far[:half], "z", NZ, 1).astype(F32)
    bwd = shift(far[half:], "z", NZ, -1).astype(F32)
    mine = block(3)
    fwd = jnp.concatenate([mine[:half] + fwd, mine[half:]], axis=0)
    mine = block(-3)
    bwd = jnp.concatenate([mine[:half], mine[half:] + bwd], axis=0)
    for k in (2, 1):
        fwd = block(k) + shift(fwd.astype(BF16), "z", NZ, 1).astype(F32)
        bwd = block(-k) + shift(bwd.astype(BF16), "z", NZ, -1).astype(F32)
    fwd = shift(fwd.astype(BF16), "z", NZ, 1).astype(F32)
    bwd = shift(bwd.astype(BF16), "z", NZ, -1).astype(F32)
    return block(0) + fwd + bwd


def per_device(
    activations,
    cotangent,
    weight,
    queries,
    new_keys,
    new_values,
    key_cache,
    value_cache,
    cache_lengths,
):
    z, xh, core, y, xl = (lax.axis_index(a) for a in ("z", "xh", "c", "y", "xl"))
    cot_other = swap(cotangent, "xl")
    acts = gather_y(activations.T)

    blocks = weight.reshape(QB, NZ, QB).transpose(1, 0, 2)
    blocks = lax.all_to_all(blocks, "z", 0, 0, tiled=True)
    blocks = blocks.reshape(NY, 2, QB, QB)
    kept, sent = pick(blocks, xl, 1), pick(blocks, 1 - xl, 1)
    blocks = jnp.stack([kept, swap(sent, "xl")], axis=1)
    weight_here = jnp.stack([pick(blocks, (y - k) % NY) for k in range(NY)], axis=0)

    attended = attend(queries, new_keys, new_values, key_cache, value_cache, cache_lengths)
    local_rows, local_steps = queries.shape[0], queries.shape[1]
    count = local_rows * local_steps
    heads = attended.reshape(local_rows, 2, 2, local_steps, QB).transpose(1, 2, 0, 3, 4)
    heads = heads.reshape(2, 2, count, QB)
    heads = jnp.concatenate([pick(heads, core, 1), pick(heads, 1 - core, 1)], axis=-1)
    kept, sent = pick(heads, xh), pick(heads, 1 - xh)
    got = swap(sent, "xh")
    mixed = jnp.concatenate(
        [jnp.where(xh == 0, kept, got), jnp.where(xh == 0, got, kept)], axis=0
    )
    mixed = gather_z(mixed, z).reshape(NZ * 2 * count, 2 * QB)
    lefts = gather_y(mixed)

    chunks = [
        [(0, 0), (1, 0), (3, 0)],
        [(2, 0), (0, 1), (1, 1), (2, 1), (3, 1)],
    ]
    sums = {}
    for names in chunks:
        keep, send = grad_parts(core, names, acts, (cotangent, cot_other))
        part = scatter_z(keep, swap(send, "c"), z).reshape(len(names), 2, QB, QB)
        kept, sent = pick(part, xh, 1), pick(part, 1 - xh, 1)
        part = kept + swap(sent.astype(BF16), "xh").astype(F32)
        sums.update({name: part[n] for n, name in enumerate(names)})
    grad = jnp.stack(
        [jnp.stack([sums[k, h] for h in range(2)], axis=0) for k in range(NY)], axis=0
    )

    blocks = grad.astype(BF16)
    blocks = jnp.stack([pick(blocks, (y - k) % NY) for k in range(NY)], axis=0)
    kept, got = blocks[:, 0], swap(blocks[:, 1], "xl")
    first = jnp.where(xl == 0, kept, got)
    second = jnp.where(xl == 0, got, kept)
    blocks = jnp.stack([first, second], axis=1).reshape(NZ, QB, QB)
    blocks = lax.all_to_all(blocks, "z", 0, 0, tiled=True)
    grad_weight = blocks.transpose(1, 0, 2).reshape(QB, NZ * QB).astype(F32)

    updated = weight_here.astype(F32) - learn_rate * grad
    largest = jnp.max(jnp.abs(updated), axis=(2, 3))
    scales = ((largest + epsilon) / scale_limit).astype(BF16)
    quantized = (updated / scales.astype(F32)[:, :, None, None]).astype(BF16)
    quantized_other, scales_other = swap(quantized, "c"), swap(scales, "c")

    both = jnp.stack([scales, scales_other], axis=1).astype(F32).reshape(2 * NY, 2, 1)
    both = jnp.broadcast_to(both, (2 * NY, 2, QB)).reshape(2 * NY, 2 * QB)
    out = project(xl, lefts, quantized, quantized_other, both, count)
    out = out.reshape(NZ * 4, count, QB)
    out = lax.all_to_all(out, ("z", "xh", "xl"), 0, 0, tiled=True)
    out = out.reshape(NZ, 4, count, QB).astype(F32).sum(axis=1).astype(BF16)
    decoded = out.transpose(1, 0, 2).reshape(local_rows, local_steps, NZ * QB)
    return (grad_weight, decoded)


def solution(mesh):
    inner = Mesh(mesh.devices.reshape(8, 2, 2, 4, 2), ("z", "xh", "c", "y", "xl"))
    fsdp, tp = ("z", "xh", "c"), ("y", "xl")
    return jax.shard_map(
        per_device,
        mesh=inner,
        in_specs=(
            P(fsdp, tp),
            P(fsdp, tp),
            P(fsdp, tp),
            P(fsdp, None, tp, None, None),
            P(fsdp, None, tp, None),
            P(fsdp, None, tp, None),
            P(fsdp, tp, None, None),
            P(fsdp, tp, None, None),
            P(fsdp),
        ),
        out_specs=(P(fsdp, tp), P(fsdp, None, tp)),
        check_vma=False,
    )
```

profile of v0, /device:TPU:1, one launch (start us, length us, event | category | flops | bytes accessed | tf_op | source)
XLA Modules:
  0.0 247.6 jit_solution(14268205111539991541)
XLA Ops:
  9.1 7.9 %shard_map.106 = bf16[16,16,128]{2,1,0:T(8,128)(2,1)} custom-call(s32[16]{0:T(128)} %len_ref.1, bf16[16,16,128]{2,1,0:T(8,128)(2,1)} %bitcast.216, bf16[16,16,128]{2,1,0:T(8,128)(2,1)} %pad.7.nk_ref, bf16[16,16,128]{2,1,0:T(8,128)(2,1)} %pad.8.nv_ref, bf16[16,512,128]{2,1,0:T(8,128)(2,1)} %bitcast.204, bf16[16,512,128]{2,1,0:T(8,128)(2,1)} %bitcast.205), custom_call_target="tpu_custom_call" | custom-call | flops 67108864 | bytes 4194304 | tf_op jit(solution)/shard_map/pallas_call | solution.py:70
  17.9 2.5 %collective-permute-start.28 = (bf16[64,256]{1,0:T(8,128)(2,1)S(1)}, bf16[64,256]{1,0:T(8,128)(2,1)S(1)}, u32[]{:S(2)}, u32[]{:S(2)}) collective-permute-start(bf16[64,256]{1,0:T(8,128)(2,1)S(1)} %fusion.32), channel_id=1, source_target_pairs={{0,16},{16,0},{1,17},{17,1},{2,18},{18,2},{3,19},{19,3},{4,20},{20... | collective-permute-start | bytes 98312 | tf_op jit(solution)/shard_map/ppermute | solution.py:28
  21.3 8.2 %all-to-all-start.1 = ((bf16[8,128,128]{2,1,0:T(8,128)(2,1)}), bf16[8,128,128]{2,1,0:T(8,128)(2,1)}, u32[]{:S(2)}, u32[]{:S(2)}) async-start(bf16[8,128,128]{2,1,0:T(8,128)(2,1)} %bitcast_bitcast_fusion), calls=%async_computation.1 | async-start | bytes 524288 | tf_op jit(solution)/shard_map/all_to_all | solution.py:241
  29.4 25.4 %collective-permute-done.28 = bf16[64,256]{1,0:T(8,128)(2,1)S(1)} collective-permute-done((bf16[64,256]{1,0:T(8,128)(2,1)S(1)}, bf16[64,256]{1,0:T(8,128)(2,1)S(1)}, u32[]{:S(2)}, u32[]{:S(2)}) %collective-permute-start.28) | collective-permute-done | bytes 32800 | tf_op jit(solution)/shard_map/ppermute | solution.py:28
  54.8 5.6 %collective-permute-start.29 = (bf16[128,256]{1,0:T(8,128)(2,1)S(1)}, bf16[128,256]{1,0:T(8,128)(2,1)S(1)}, u32[]{:S(2)}, u32[]{:S(2)}) collective-permute-start(bf16[128,256]{1,0:T(8,128)(2,1)S(1)} %pad_maximum_fusion.10), channel_id=1, source_target_pairs={{0,224},{32,0},{64,32},{96,64},{128,96},{160,128},{192,160},{224,1... | collective-permute-start | bytes 196616 | tf_op jit(solution)/shard_map/ppermute | solution.py:24
  61.8 3.0 %collective-permute-start.30 = (bf16[128,256]{1,0:T(8,128)(2,1)S(1)}, bf16[128,256]{1,0:T(8,128)(2,1)S(1)}, u32[]{:S(2)}, u32[]{:S(2)}) collective-permute-start(bf16[128,256]{1,0:T(8,128)(2,1)S(1)} %collective-permute-done.29), channel_id=1, source_target_pairs={{0,224},{32,0},{64,32},{96,64},{128,96},{160,128},{192,160},{224,1... | collective-permute-start | bytes 196616 | tf_op jit(solution)/shard_map/ppermute | solution.py:24
  66.1 3.0 %collective-permute-start.31 = (bf16[128,256]{1,0:T(8,128)(2,1)S(1)}, bf16[128,256]{1,0:T(8,128)(2,1)S(1)}, u32[]{:S(2)}, u32[]{:S(2)}) collective-permute-start(bf16[128,256]{1,0:T(8,128)(2,1)S(1)} %collective-permute-done.30), channel_id=1, source_target_pairs={{0,224},{32,0},{64,32},{96,64},{128,96},{160,128},{192,160},{224,1... | collective-permute-start | bytes 196616 | tf_op jit(solution)/shard_map/ppermute | solution.py:24
  70.6 3.1 %collective-permute-start.36 = (bf16[64,256]{1,0:T(8,128)(2,1)S(1)}, bf16[64,256]{1,0:T(8,128)(2,1)S(1)}, u32[]{:S(2)}, u32[]{:S(2)}) collective-permute-start(bf16[64,256]{1,0:T(8,128)(2,1)S(1)} %slice.189), channel_id=1, source_target_pairs={{0,224},{32,0},{64,32},{96,64},{128,96},{160,128},{192,160},{224,1... | collective-permute-start | bytes 98312 | tf_op jit(solution)/shard_map/ppermute | solution.py:24
  74.8 3.4 %collective-permute-done.35 = bf16[64,256]{1,0:T(8,128)(2,1)S(1)} collective-permute-done((bf16[64,256]{1,0:T(8,128)(2,1)S(1)}, bf16[64,256]{1,0:T(8,128)(2,1)S(1)}, u32[]{:S(2)}, u32[]{:S(2)}) %collective-permute-start.35) | collective-permute-done | bytes 32800 | tf_op jit(solution)/shard_map/ppermute | solution.py:24
  80.3 4.3 %shard_map.104 = (bf16[8,768,128]{2,1,0:T(8,128)(2,1)S(1)}, bf16[8,768,128]{2,1,0:T(8,128)(2,1)S(1)}) custom-call(s32[1]{0:T(128)} %bitcast.core_ref, bf16[512,1024]{1,0:T(8,128)(2,1)S(1)} %bitcast.202, bf16[512,1024]{1,0:T(8,128)(2,1)S(1)} %collective-permute-done.refs_1_, bf16[512,1024]{1,0:T(8,128)(2,1)S(1)} %collective-permute-done.1.refs_2_.refs_3_, ...), custom_call_target="tpu_custom_call" | custom-call | flops 3221225472 | bytes 6291456 | tf_op jit(solution)/shard_map/pallas_call | solution.py:114
  84.6 7.6 %collective-permute-start.2 = (bf16[8,768,128]{2,1,0:T(8,128)(2,1)S(1)}, bf16[8,768,128]{2,1,0:T(8,128)(2,1)S(1)}, u32[]{:S(2)}, u32[]{:S(2)}) collective-permute-start(bf16[8,768,128]{2,1,0:T(8,128)(2,1)S(1)} %get-tuple-element.7), channel_id=1, source_target_pairs={{0,8},{8,0},{1,9},{9,1},{2,10},{10,2},{3,11},{11,3},{4,12},{12,4},... | collective-permute-start | bytes 4718600 | tf_op jit(solution)/shard_map/ppermute | solution.py:28
  93.7 8.3 %shard_map.105 = (bf16[8,1280,128]{2,1,0:T(8,128)(2,1)S(1)}, bf16[8,1280,128]{2,1,0:T(8,128)(2,1)}) custom-call(s32[1]{0:T(128)} %bitcast.core_ref, bf16[512,1024]{1,0:T(8,128)(2,1)S(1)} %bitcast.203, bf16[512,1024]{1,0:T(8,128)(2,1)S(1)} %copy-done.5, bf16[512,1024]{1,0:T(8,128)(2,1)S(1)} %pad_maximum_fusion.refs_2_, bf16[512,1024]{1,0:T(8,128)(2,1)S(1)} %copy-done.7, ...), custom_call_target="tpu_custom_call" | custom-call | flops 5368709120 | bytes 9437184 | tf_op jit(solution)/shard_map/pallas_call | solution.py:114
  102.0 5.6 %collective-permute-start.15 = (bf16[8,1280,128]{2,1,0:T(8,128)(2,1)}, bf16[8,1280,128]{2,1,0:T(8,128)(2,1)}, u32[]{:S(2)}, u32[]{:S(2)}) collective-permute-start(bf16[8,1280,128]{2,1,0:T(8,128)(2,1)} %get-tuple-element.9), channel_id=1, source_target_pairs={{0,8},{8,0},{1,9},{9,1},{2,10},{10,2},{3,11},{11,3},{4,12},{12,4},... | collective-permute-start | bytes 7864328 | tf_op jit(solution)/shard_map/ppermute | solution.py:28
  107.9 2.7 %collective-permute-start.7 = (bf16[384,128]{1,0:T(8,128)(2,1)S(1)}, bf16[384,128]{1,0:T(8,128)(2,1)S(1)}, u32[]{:S(2)}, u32[]{:S(2)}) collective-permute-start(bf16[384,128]{1,0:T(8,128)(2,1)S(1)} %get-tuple-element.51), channel_id=1, source_target_pairs={{0,224},{32,0},{64,32},{96,64},{128,96},{160,128},{192,160},{224,1... | collective-permute-start | bytes 294920 | tf_op jit(solution)/shard_map/ppermute | solution.py:24
  110.6 2.9 %collective-permute-done.3 = bf16[384,128]{1,0:T(8,128)(2,1)S(1)} collective-permute-done((bf16[384,128]{1,0:T(8,128)(2,1)S(1)}, bf16[384,128]{1,0:T(8,128)(2,1)S(1)}, u32[]{:S(2)}, u32[]{:S(2)}) %collective-permute-start.3) | collective-permute-done | bytes 98336 | tf_op jit(solution)/shard_map/ppermute | solution.py:24
  114.4 2.7 %collective-permute-start.8 = (bf16[768,128]{1,0:T(8,128)(2,1)}, bf16[768,128]{1,0:T(8,128)(2,1)}, u32[]{:S(2)}, u32[]{:S(2)}) collective-permute-start(bf16[768,128]{1,0:T(8,128)(2,1)} %pad_maximum_fusion.9), channel_id=1, source_target_pairs={{0,224},{32,0},{64,32},{96,64},{128,96},{160,128},{192,160},{224,1... | collective-permute-start | bytes 589832 | tf_op jit(solution)/shard_map/ppermute | solution.py:24
  117.1 3.5 %collective-permute-done.4 = bf16[768,128]{1,0:T(8,128)(2,1)S(1)} collective-permute-done((bf16[768,128]{1,0:T(8,128)(2,1)S(1)}, bf16[768,128]{1,0:T(8,128)(2,1)S(1)}, u32[]{:S(2)}, u32[]{:S(2)}) %collective-permute-start.4) | collective-permute-done | bytes 196640 | tf_op jit(solution)/shard_map/ppermute | solution.py:24
  121.4 2.7 %collective-permute-start.39 = (bf16[1024,256]{1,0:T(8,128)(2,1)S(1)}, bf16[1024,256]{1,0:T(8,128)(2,1)}, u32[]{:S(2)}, u32[]{:S(2)}) collective-permute-start(bf16[1024,256]{1,0:T(8,128)(2,1)S(1)} %bitcast.209), channel_id=1, source_target_pairs={{0,6},{2,0},{4,2},{6,4},{1,7},{3,1},{5,3},{7,5},{8,14},{10,8},{12,... | collective-permute-start | bytes 1572872 | tf_op jit(solution)/shard_map/ppermute | solution.py:24
  131.9 4.7 %collective-permute-done.16 = bf16[640,128]{1,0:T(8,128)(2,1)S(1)} collective-permute-done((bf16[640,128]{1,0:T(8,128)(2,1)S(1)}, bf16[640,128]{1,0:T(8,128)(2,1)S(1)}, u32[]{:S(2)}, u32[]{:S(2)}) %collective-permute-start.16) | collective-permute-done | bytes 163872 | tf_op jit(solution)/shard_map/ppermute | solution.py:24
  136.7 9.6 %collective-permute-start.20 = (bf16[640,128]{1,0:T(8,128)(2,1)S(1)}, bf16[640,128]{1,0:T(8,128)(2,1)S(1)}, u32[]{:S(2)}, u32[]{:S(2)}) collective-permute-start(bf16[640,128]{1,0:T(8,128)(2,1)S(1)} %get-tuple-element.36), channel_id=1, source_target_pairs={{0,224},{32,0},{64,32},{96,64},{128,96},{160,128},{192,160},{224,1... | collective-permute-start | bytes 491528 | tf_op jit(solution)/shard_map/ppermute | solution.py:24
  146.4 4.1 %collective-permute-done.20 = bf16[640,128]{1,0:T(8,128)(2,1)S(1)} collective-permute-done((bf16[640,128]{1,0:T(8,128)(2,1)S(1)}, bf16[640,128]{1,0:T(8,128)(2,1)S(1)}, u32[]{:S(2)}, u32[]{:S(2)}) %collective-permute-start.20) | collective-permute-done | bytes 163872 | tf_op jit(solution)/shard_map/ppermute | solution.py:24
  150.5 7.1 %collective-permute-done.17 = bf16[1280,128]{1,0:T(8,128)(2,1)S(1)} collective-permute-done((bf16[1280,128]{1,0:T(8,128)(2,1)S(1)}, bf16[1280,128]{1,0:T(8,128)(2,1)S(1)}, u32[]{:S(2)}, u32[]{:S(2)}) %collective-permute-start.17) | collective-permute-done | bytes 327712 | tf_op jit(solution)/shard_map/ppermute | solution.py:24
  165.1 2.7 %collective-permute-start.10 = (bf16[768,128]{1,0:T(8,128)(2,1)S(1)}, bf16[768,128]{1,0:T(8,128)(2,1)S(1)}, u32[]{:S(2)}, u32[]{:S(2)}) collective-permute-start(bf16[768,128]{1,0:T(8,128)(2,1)S(1)} %fusion.6), channel_id=1, source_target_pairs={{0,224},{32,0},{64,32},{96,64},{128,96},{160,128},{192,160},{224,1... | collective-permute-start | bytes 589832 | tf_op jit(solution)/shard_map/ppermute | solution.py:24
  169.6 2.3 collective-permute-done.10
  182.2 5.0 %collective-permute-done.23 = bf16[1280,128]{1,0:T(8,128)(2,1)S(1)} collective-permute-done((bf16[1280,128]{1,0:T(8,128)(2,1)S(1)}, bf16[1280,128]{1,0:T(8,128)(2,1)S(1)}, u32[]{:S(2)}, u32[]{:S(2)}) %collective-permute-start.23) | collective-permute-done | bytes 327712 | tf_op jit(solution)/shard_map/ppermute | solution.py:24
  189.6 4.6 %collective-permute-done.24 = bf16[5,128,128]{2,1,0:T(8,128)(2,1)S(1)} collective-permute-done((bf16[5,128,128]{2,1,0:T(8,128)(2,1)S(1)}, bf16[5,128,128]{2,1,0:T(8,128)(2,1)S(1)}, u32[]{:S(2)}, u32[]{:S(2)}) %collective-permute-start.24) | collective-permute-done | bytes 163872 | tf_op jit(solution)/shard_map/ppermute | solution.py:28
  195.9 10.8 %collective-permute-start.27 = (bf16[4,2]{1,0:T(4,128)(2,1)S(1)}, bf16[4,2]{1,0:T(4,128)(2,1)S(1)}, u32[]{:S(2)}, u32[]{:S(2)}) collective-permute-start(bf16[4,2]{1,0:T(4,128)(2,1)S(1)} %get-tuple-element.17), channel_id=1, source_target_pairs={{0,8},{8,0},{1,9},{9,1},{2,10},{10,2},{3,11},{11,3},{4,12},{12,4},... | collective-permute-start | bytes 56 | tf_op jit(solution)/shard_map/ppermute | solution.py:28
  207.5 4.1 %all-to-all-start = ((bf16[8,128,128]{2,1,0:T(8,128)(2,1)}), bf16[8,128,128]{2,1,0:T(8,128)(2,1)S(1)}, u32[]{:S(2)}, u32[]{:S(2)}) async-start(bf16[8,128,128]{2,1,0:T(8,128)(2,1)} %bitcast.38), calls=%async_computation | async-start | bytes 524288 | tf_op jit(solution)/shard_map/all_to_all | solution.py:282
  211.8 2.9 %collective-permute-start.41 = (bf16[4,2,128,128]{3,2,1,0:T(8,128)(2,1)S(1)}, bf16[4,2,128,128]{3,2,1,0:T(8,128)(2,1)S(1)}, u32[]{:S(2)}, u32[]{:S(2)}) collective-permute-start(bf16[4,2,128,128]{3,2,1,0:T(8,128)(2,1)S(1)} %divide_convert_fusion.refs_4_), channel_id=1, source_target_pairs={{0,8},{8,0},{1,9},{9,1},{2,10},{10,2},{3,11},{11,3},{4,12},{12,4},... | collective-permute-start | bytes 786440 | tf_op jit(solution)/shard_map/ppermute | solution.py:28
  216.6 4.6 %shard_map.107 = bf16[8,2,2,64,128]{4,3,2,1,0:T(8,128)(2,1)} custom-call(s32[1]{0:T(128)} %bitcast.41.own_ref, f32[8,256]{1,0:T(8,128)} %broadcast_bitcast_fusion.scale_ref, bf16[1024,256]{1,0:T(8,128)(2,1)} %bitcast.210, bf16[1024,256]{1,0:T(8,128)(2,1)} %collective-permute-done.37.refs_1_, bf16[1024,256]{1,0:T(8,128)(2,1)} %pad_maximum_fusion.2.refs_2_, ...), custom_call_target="tpu_custom_call" | custom-call | flops 536870912 | bytes 4194304 | tf_op jit(solution)/shard_map/pallas_call | solution.py:161
  221.2 8.8 %all-to-all-start.2 = ((bf16[32,64,128]{2,1,0:T(8,128)(2,1)}), bf16[32,64,128]{2,1,0:T(8,128)(2,1)S(1)}, u32[]{:S(2)}, u32[]{:S(2)}) async-start(bf16[32,64,128]{2,1,0:T(8,128)(2,1)} %bitcast.207), calls=%async_computation.2 | async-start | bytes 1048576 | tf_op jit(solution)/shard_map/all_to_all | solution.py:295
  231.2 15.3 %all-to-all-done.2 = bf16[32,64,128]{2,1,0:T(8,128)(2,1)S(1)} async-done(((bf16[32,64,128]{2,1,0:T(8,128)(2,1)}), bf16[32,64,128]{2,1,0:T(8,128)(2,1)S(1)}, u32[]{:S(2)}, u32[]{:S(2)}) %all-to-all-start.2) | async-done | bytes 524320 | tf_op jit(solution)/shard_map/all_to_all | solution.py:295
  (193 shorter events, 57.0 us)
Async XLA Ops:
  2.2 77.7 %collective-permute-start = (bf16[512,1024]{1,0:T(8,128)(2,1)S(1)}, bf16[512,1024]{1,0:T(8,128)(2,1)S(1)}, u32[]{:S(2)}, u32[]{:S(2)}) collective-permute-start(bf16[512,1024]{1,0:T(8,128)(2,1)S(1)} %bitcast.200), channel_id=1, source_target_pairs={{0,2},{2,4},{4,6},{6,0},{1,3},{3,5},{5,7},{7,1},{8,10},{10,12},{12... | collective-permute-start | bytes 3145736 | tf_op jit(solution)/shard_map/ppermute | solution.py:24
  4.4 73.9 %collective-permute-start.1 = (bf16[512,1024]{1,0:T(8,128)(2,1)S(1)}, bf16[512,1024]{1,0:T(8,128)(2,1)S(1)}, u32[]{:S(2)}, u32[]{:S(2)}) collective-permute-start(bf16[512,1024]{1,0:T(8,128)(2,1)S(1)} %bitcast.201), channel_id=1, source_target_pairs={{0,6},{2,0},{4,2},{6,4},{1,7},{3,1},{5,3},{7,5},{8,14},{10,8},{12,... | collective-permute-start | bytes 3145736 | tf_op jit(solution)/shard_map/ppermute | solution.py:24
  6.0 86.5 %collective-permute-start.14 = (bf16[1024,1024]{1,0:T(8,128)(2,1)}, bf16[1024,1024]{1,0:T(8,128)(2,1)}, u32[]{:S(2)}, u32[]{:S(2)}) collective-permute-start(bf16[1024,1024]{1,0:T(8,128)(2,1)} %refs_4_.1), channel_id=1, source_target_pairs={{0,1},{1,0},{2,3},{3,2},{4,5},{5,4},{6,7},{7,6},{8,9},{9,8},{10,11... | collective-permute-start | bytes 6291464 | tf_op jit(solution)/shard_map/ppermute | solution.py:28
  17.9 36.9 %collective-permute-start.28 = (bf16[64,256]{1,0:T(8,128)(2,1)S(1)}, bf16[64,256]{1,0:T(8,128)(2,1)S(1)}, u32[]{:S(2)}, u32[]{:S(2)}) collective-permute-start(bf16[64,256]{1,0:T(8,128)(2,1)S(1)} %fusion.32), channel_id=1, source_target_pairs={{0,16},{16,0},{1,17},{17,1},{2,18},{18,2},{3,19},{19,3},{4,20},{20... | collective-permute-start | bytes 98312 | tf_op jit(solution)/shard_map/ppermute | solution.py:28
  21.3 102.8 %all-to-all-start.1 = ((bf16[8,128,128]{2,1,0:T(8,128)(2,1)}), bf16[8,128,128]{2,1,0:T(8,128)(2,1)}, u32[]{:S(2)}, u32[]{:S(2)}) async-start(bf16[8,128,128]{2,1,0:T(8,128)(2,1)} %bitcast_bitcast_fusion), calls=%async_computation.1 | async-start | bytes 524288 | tf_op jit(solution)/shard_map/all_to_all | solution.py:241
  54.8 7.0 %collective-permute-start.29 = (bf16[128,256]{1,0:T(8,128)(2,1)S(1)}, bf16[128,256]{1,0:T(8,128)(2,1)S(1)}, u32[]{:S(2)}, u32[]{:S(2)}) collective-permute-start(bf16[128,256]{1,0:T(8,128)(2,1)S(1)} %pad_maximum_fusion.10), channel_id=1, source_target_pairs={{0,224},{32,0},{64,32},{96,64},{128,96},{160,128},{192,160},{224,1... | collective-permute-start | bytes 196616 | tf_op jit(solution)/shard_map/ppermute | solution.py:24
  78.3 14.0 %collective-permute-start.13 = (bf16[256,1024]{1,0:T(8,128)(2,1)S(1)}, bf16[256,1024]{1,0:T(8,128)(2,1)S(1)}, u32[]{:S(2)}, u32[]{:S(2)}) collective-permute-start(bf16[256,1024]{1,0:T(8,128)(2,1)S(1)} %slice.172), channel_id=1, source_target_pairs={{0,6},{2,0},{4,2},{6,4},{1,7},{3,1},{5,3},{7,5},{8,14},{10,8},{12,... | collective-permute-start | bytes 1572872 | tf_op jit(solution)/shard_map/ppermute | solution.py:24
  79.9 12.4 %collective-permute-start.12 = (bf16[256,1024]{1,0:T(8,128)(2,1)S(1)}, bf16[256,1024]{1,0:T(8,128)(2,1)S(1)}, u32[]{:S(2)}, u32[]{:S(2)}) collective-permute-start(bf16[256,1024]{1,0:T(8,128)(2,1)S(1)} %slice.171), channel_id=1, source_target_pairs={{0,2},{2,4},{4,6},{6,0},{1,3},{3,5},{5,7},{7,1},{8,10},{10,12},{12... | collective-permute-start | bytes 1572872 | tf_op jit(solution)/shard_map/ppermute | solution.py:24
  84.6 23.0 %collective-permute-start.2 = (bf16[8,768,128]{2,1,0:T(8,128)(2,1)S(1)}, bf16[8,768,128]{2,1,0:T(8,128)(2,1)S(1)}, u32[]{:S(2)}, u32[]{:S(2)}) collective-permute-start(bf16[8,768,128]{2,1,0:T(8,128)(2,1)S(1)} %get-tuple-element.7), channel_id=1, source_target_pairs={{0,8},{8,0},{1,9},{9,1},{2,10},{10,2},{3,11},{11,3},{4,12},{12,4},... | collective-permute-start | bytes 4718600 | tf_op jit(solution)/shard_map/ppermute | solution.py:28
  102.0 27.5 %collective-permute-start.15 = (bf16[8,1280,128]{2,1,0:T(8,128)(2,1)}, bf16[8,1280,128]{2,1,0:T(8,128)(2,1)}, u32[]{:S(2)}, u32[]{:S(2)}) collective-permute-start(bf16[8,1280,128]{2,1,0:T(8,128)(2,1)} %get-tuple-element.9), channel_id=1, source_target_pairs={{0,8},{8,0},{1,9},{9,1},{2,10},{10,2},{3,11},{11,3},{4,12},{12,4},... | collective-permute-start | bytes 7864328 | tf_op jit(solution)/shard_map/ppermute | solution.py:28
  113.6 6.9 %collective-permute-start.4 = (bf16[768,128]{1,0:T(8,128)(2,1)S(1)}, bf16[768,128]{1,0:T(8,128)(2,1)S(1)}, u32[]{:S(2)}, u32[]{:S(2)}) collective-permute-start(bf16[768,128]{1,0:T(8,128)(2,1)S(1)} %pad_maximum_fusion.8), channel_id=1, source_target_pairs={{0,32},{32,64},{64,96},{96,128},{128,160},{160,192},{192,224},{224... | collective-permute-start | bytes 589832 | tf_op jit(solution)/shard_map/ppermute | solution.py:24
  114.4 10.7 %collective-permute-start.8 = (bf16[768,128]{1,0:T(8,128)(2,1)}, bf16[768,128]{1,0:T(8,128)(2,1)}, u32[]{:S(2)}, u32[]{:S(2)}) collective-permute-start(bf16[768,128]{1,0:T(8,128)(2,1)} %pad_maximum_fusion.9), channel_id=1, source_target_pairs={{0,224},{32,0},{64,32},{96,64},{128,96},{160,128},{192,160},{224,1... | collective-permute-start | bytes 589832 | tf_op jit(solution)/shard_map/ppermute | solution.py:24
  121.3 6.0 %collective-permute-start.5 = (bf16[768,128]{1,0:T(8,128)(2,1)}, bf16[768,128]{1,0:T(8,128)(2,1)}, u32[]{:S(2)}, u32[]{:S(2)}) collective-permute-start(bf16[768,128]{1,0:T(8,128)(2,1)} %fusion.7), channel_id=1, source_target_pairs={{0,32},{32,64},{64,96},{96,128},{128,160},{160,192},{192,224},{224... | collective-permute-start | bytes 589832 | tf_op jit(solution)/shard_map/ppermute | solution.py:24
  121.3 40.2 %collective-permute-start.37 = (bf16[1024,256]{1,0:T(8,128)(2,1)S(1)}, bf16[1024,256]{1,0:T(8,128)(2,1)}, u32[]{:S(2)}, u32[]{:S(2)}) collective-permute-start(bf16[1024,256]{1,0:T(8,128)(2,1)S(1)} %bitcast.208), channel_id=1, source_target_pairs={{0,2},{2,4},{4,6},{6,0},{1,3},{3,5},{5,7},{7,1},{8,10},{10,12},{12... | collective-permute-start | bytes 1572872 | tf_op jit(solution)/shard_map/ppermute | solution.py:24
  121.4 38.9 %collective-permute-start.39 = (bf16[1024,256]{1,0:T(8,128)(2,1)S(1)}, bf16[1024,256]{1,0:T(8,128)(2,1)}, u32[]{:S(2)}, u32[]{:S(2)}) collective-permute-start(bf16[1024,256]{1,0:T(8,128)(2,1)S(1)} %bitcast.209), channel_id=1, source_target_pairs={{0,6},{2,0},{4,2},{6,4},{1,7},{3,1},{5,3},{7,5},{8,14},{10,8},{12,... | collective-permute-start | bytes 1572872 | tf_op jit(solution)/shard_map/ppermute | solution.py:24
  125.1 33.6 %collective-permute-start.26 = (bf16[4,128,128]{2,1,0:T(8,128)(2,1)S(1)}, bf16[4,128,128]{2,1,0:T(8,128)(2,1)S(1)}, u32[]{:S(2)}, u32[]{:S(2)}) collective-permute-start(bf16[4,128,128]{2,1,0:T(8,128)(2,1)S(1)} %get-tuple-element.41), channel_id=1, source_target_pairs={{0,1},{1,0},{2,3},{3,2},{4,5},{5,4},{6,7},{7,6},{8,9},{9,8},{10,11... | collective-permute-start | bytes 393224 | tf_op jit(solution)/shard_map/ppermute | solution.py:28
  128.8 35.1 %collective-permute-start.9 = (bf16[768,128]{1,0:T(8,128)(2,1)S(1)}, bf16[768,128]{1,0:T(8,128)(2,1)S(1)}, u32[]{:S(2)}, u32[]{:S(2)}) collective-permute-start(bf16[768,128]{1,0:T(8,128)(2,1)S(1)} %get-tuple-element.24), channel_id=1, source_target_pairs={{0,224},{32,0},{64,32},{96,64},{128,96},{160,128},{192,160},{224,1... | collective-permute-start | bytes 589832 | tf_op jit(solution)/shard_map/ppermute | solution.py:24
  136.7 13.8 %collective-permute-start.20 = (bf16[640,128]{1,0:T(8,128)(2,1)S(1)}, bf16[640,128]{1,0:T(8,128)(2,1)S(1)}, u32[]{:S(2)}, u32[]{:S(2)}) collective-permute-start(bf16[640,128]{1,0:T(8,128)(2,1)S(1)} %get-tuple-element.36), channel_id=1, source_target_pairs={{0,224},{32,0},{64,32},{96,64},{128,96},{160,128},{192,160},{224,1... | collective-permute-start | bytes 491528 | tf_op jit(solution)/shard_map/ppermute | solution.py:24
  150.5 7.1 %collective-permute-start.17 = (bf16[1280,128]{1,0:T(8,128)(2,1)S(1)}, bf16[1280,128]{1,0:T(8,128)(2,1)S(1)}, u32[]{:S(2)}, u32[]{:S(2)}) collective-permute-start(bf16[1280,128]{1,0:T(8,128)(2,1)S(1)} %pad_maximum_fusion.3), channel_id=1, source_target_pairs={{0,32},{32,64},{64,96},{96,128},{128,160},{160,192},{192,224},{224... | collective-permute-start | bytes 983048 | tf_op jit(solution)/shard_map/ppermute | solution.py:24
  157.6 7.5 %collective-permute-start.21 = (bf16[1280,128]{1,0:T(8,128)(2,1)S(1)}, bf16[1280,128]{1,0:T(8,128)(2,1)S(1)}, u32[]{:S(2)}, u32[]{:S(2)}) collective-permute-start(bf16[1280,128]{1,0:T(8,128)(2,1)S(1)} %pad_maximum_fusion.4), channel_id=1, source_target_pairs={{0,224},{32,0},{64,32},{96,64},{128,96},{160,128},{192,160},{224,1... | collective-permute-start | bytes 983048 | tf_op jit(solution)/shard_map/ppermute | solution.py:24
  158.7 9.1 %collective-permute-start.18 = (bf16[1280,128]{1,0:T(8,128)(2,1)S(1)}, bf16[1280,128]{1,0:T(8,128)(2,1)S(1)}, u32[]{:S(2)}, u32[]{:S(2)}) collective-permute-start(bf16[1280,128]{1,0:T(8,128)(2,1)S(1)} %fusion.2), channel_id=1, source_target_pairs={{0,32},{32,64},{64,96},{96,128},{128,160},{160,192},{192,224},{224... | collective-permute-start | bytes 983048 | tf_op jit(solution)/shard_map/ppermute | solution.py:24
  161.3 18.3 %collective-permute-start.40 = (bf16[512,256]{1,0:T(8,128)(2,1)S(1)}, bf16[512,256]{1,0:T(8,128)(2,1)S(1)}, u32[]{:S(2)}, u32[]{:S(2)}) collective-permute-start(bf16[512,256]{1,0:T(8,128)(2,1)S(1)} %slice.191), channel_id=1, source_target_pairs={{0,6},{2,0},{4,2},{6,4},{1,7},{3,1},{5,3},{7,5},{8,14},{10,8},{12,... | collective-permute-start | bytes 786440 | tf_op jit(solution)/shard_map/ppermute | solution.py:24
  162.5 17.2 %collective-permute-start.38 = (bf16[512,256]{1,0:T(8,128)(2,1)S(1)}, bf16[512,256]{1,0:T(8,128)(2,1)S(1)}, u32[]{:S(2)}, u32[]{:S(2)}) collective-permute-start(bf16[512,256]{1,0:T(8,128)(2,1)S(1)} %slice.190), channel_id=1, source_target_pairs={{0,2},{2,4},{4,6},{6,0},{1,3},{3,5},{5,7},{7,1},{8,10},{10,12},{12... | collective-permute-start | bytes 786440 | tf_op jit(solution)/shard_map/ppermute | solution.py:24
  165.1 6.9 %collective-permute-start.10 = (bf16[768,128]{1,0:T(8,128)(2,1)S(1)}, bf16[768,128]{1,0:T(8,128)(2,1)S(1)}, u32[]{:S(2)}, u32[]{:S(2)}) collective-permute-start(bf16[768,128]{1,0:T(8,128)(2,1)S(1)} %fusion.6), channel_id=1, source_target_pairs={{0,224},{32,0},{64,32},{96,64},{128,96},{160,128},{192,160},{224,1... | collective-permute-start | bytes 589832 | tf_op jit(solution)/shard_map/ppermute | solution.py:24
  169.1 7.5 %collective-permute-start.22 = (bf16[1280,128]{1,0:T(8,128)(2,1)S(1)}, bf16[1280,128]{1,0:T(8,128)(2,1)S(1)}, u32[]{:S(2)}, u32[]{:S(2)}) collective-permute-start(bf16[1280,128]{1,0:T(8,128)(2,1)S(1)} %get-tuple-element.19), channel_id=1, source_target_pairs={{0,224},{32,0},{64,32},{96,64},{128,96},{160,128},{192,160},{224,1... | collective-permute-start | bytes 983048 | tf_op jit(solution)/shard_map/ppermute | solution.py:24
  173.1 7.4 %collective-permute-start.11 = (bf16[3,128,128]{2,1,0:T(8,128)(2,1)S(1)}, bf16[3,128,128]{2,1,0:T(8,128)(2,1)S(1)}, u32[]{:S(2)}, u32[]{:S(2)}) collective-permute-start(bf16[3,128,128]{2,1,0:T(8,128)(2,1)S(1)} %fusion.21), channel_id=1, source_target_pairs={{0,16},{16,0},{1,17},{17,1},{2,18},{18,2},{3,19},{19,3},{4,20},{20... | collective-permute-start | bytes 294920 | tf_op jit(solution)/shard_map/ppermute | solution.py:28
  174.6 7.6 %collective-permute-start.19 = (bf16[1280,128]{1,0:T(8,128)(2,1)S(1)}, bf16[1280,128]{1,0:T(8,128)(2,1)S(1)}, u32[]{:S(2)}, u32[]{:S(2)}) collective-permute-start(bf16[1280,128]{1,0:T(8,128)(2,1)S(1)} %get-tuple-element.18), channel_id=1, source_target_pairs={{0,32},{32,64},{64,96},{96,128},{128,160},{160,192},{192,224},{224... | collective-permute-start | bytes 983048 | tf_op jit(solution)/shard_map/ppermute | solution.py:24
  177.7 9.5 %collective-permute-start.23 = (bf16[1280,128]{1,0:T(8,128)(2,1)S(1)}, bf16[1280,128]{1,0:T(8,128)(2,1)S(1)}, u32[]{:S(2)}, u32[]{:S(2)}) collective-permute-start(bf16[1280,128]{1,0:T(8,128)(2,1)S(1)} %fusion.1), channel_id=1, source_target_pairs={{0,224},{32,0},{64,32},{96,64},{128,96},{160,128},{192,160},{224,1... | collective-permute-start | bytes 983048 | tf_op jit(solution)/shard_map/ppermute | solution.py:24
  194.4 12.2 %collective-permute-start.25 = (bf16[4,128,128]{2,1,0:T(8,128)(2,1)S(1)}, bf16[4,128,128]{2,1,0:T(8,128)(2,1)S(1)}, u32[]{:S(2)}, u32[]{:S(2)}) collective-permute-start(bf16[4,128,128]{2,1,0:T(8,128)(2,1)S(1)} %slice_bitcast_fusion.6), channel_id=1, source_target_pairs={{0,1},{1,0},{2,3},{3,2},{4,5},{5,4},{6,7},{7,6},{8,9},{9,8},{10,11... | collective-permute-start | bytes 393224 | tf_op jit(solution)/shard_map/ppermute | solution.py:28
  195.9 18.8 %collective-permute-start.27 = (bf16[4,2]{1,0:T(4,128)(2,1)S(1)}, bf16[4,2]{1,0:T(4,128)(2,1)S(1)}, u32[]{:S(2)}, u32[]{:S(2)}) collective-permute-start(bf16[4,2]{1,0:T(4,128)(2,1)S(1)} %get-tuple-element.17), channel_id=1, source_target_pairs={{0,8},{8,0},{1,9},{9,1},{2,10},{10,2},{3,11},{11,3},{4,12},{12,4},... | collective-permute-start | bytes 56 | tf_op jit(solution)/shard_map/ppermute | solution.py:28
  207.5 13.7 %all-to-all-start = ((bf16[8,128,128]{2,1,0:T(8,128)(2,1)}), bf16[8,128,128]{2,1,0:T(8,128)(2,1)S(1)}, u32[]{:S(2)}, u32[]{:S(2)}) async-start(bf16[8,128,128]{2,1,0:T(8,128)(2,1)} %bitcast.38), calls=%async_computation | async-start | bytes 524288 | tf_op jit(solution)/shard_map/all_to_all | solution.py:282
  221.2 25.4 %all-to-all-start.2 = ((bf16[32,64,128]{2,1,0:T(8,128)(2,1)}), bf16[32,64,128]{2,1,0:T(8,128)(2,1)S(1)}, u32[]{:S(2)}, u32[]{:S(2)}) async-start(bf16[32,64,128]{2,1,0:T(8,128)(2,1)} %bitcast.207), calls=%async_computation.2 | async-start | bytes 1048576 | tf_op jit(solution)/shard_map/all_to_all | solution.py:295
  (33 other events, 427.0 us)
where the time goes:
time: 252 us; the launch traced here: 248 us
  starting transfers between devices  104 us (41%)
  waiting for transfers between devices  89.9 us (36%)
  Pallas kernels  25.1 us (10%)
  local copies, waits for them, and re-layouts  14.3 us (6%)
  other arithmetic  13.2 us (5%)
    ppermute x32, starting transfers between devices, shift(): return lax.ppermute(x, axis, [(i, (i + step) % size) for i in range(size)])  47.8 us
    ppermute x32, waiting for transfers between devices, shift(): return lax.ppermute(x, axis, [(i, (i + step) % size) for i in range(size)])  44.4 us
    ppermute x10, starting transfers between devices, swap(): return lax.ppermute(x, axis, [(0, 1), (1, 0)])  34.8 us
    ppermute x10, waiting for transfers between devices, swap(): return lax.ppermute(x, axis, [(0, 1), (1, 0)])  30.1 us
    all_to_all x1, waiting for transfers between devices, per_device(): out = lax.all_to_all(out, ('z', 'xh', 'xl'), 0, 0, tiled=True)  15.3 us
    pallas_call x2, Pallas kernels, grad_parts(): pl.pallas_call(functools.partial(grad_kernel, names), grid=(breadth // ti...  12.6 us
    all_to_all x2, starting transfers between devices, per_device(): blocks = lax.all_to_all(blocks, 'z', 0, 0, tiled=True)  12.2 us
    all_to_all x1, starting transfers between devices, per_device(): out = lax.all_to_all(out, ('z', 'xh', 'xl'), 0, 0, tiled=True)  8.77 us
  transfers between devices with their start and end apart: 45, of which 21 were waited for; matrix products, arithmetic and copies ran while one was open for 9% of the time, Pallas kernels for 10%

commit v1 on v0

v1 whole, which is shorter than its diff:
```python
import functools

import jax
import jax.numpy as jnp
from jax import lax
from jax.experimental import pallas as pl
from jax.experimental.pallas import tpu as pltpu
from jax.sharding import Mesh, PartitionSpec as P

QB = 128
NZ = 8
NY = 4

learn_rate = 0.01
scale_limit = 448.0
epsilon = 1e-06

F32 = jnp.float32
BF16 = jnp.bfloat16
NT = (((1,), (1,)), ((), ()))


def shift(x, axis, size, step):
    return lax.ppermute(x, axis, [(i, (i + step) % size) for i in range(size)])


def swap(x, axis):
    return lax.ppermute(x, axis, [(0, 1), (1, 0)])


def after(x, *others):
    return lax.optimization_barrier((x, *others))[0]


def pick(x, index, axis=0):
    return lax.dynamic_index_in_dim(x, index, axis, keepdims=False)


def payload_kernel(steps, len_ref, q_ref, nk_ref, nv_ref, k_ref, v_ref, weight_ref, out_ref):
    rows, count, size = q_ref.shape
    breadth = weight_ref.shape[1]
    index = pl.program_id(0)

    @pl.when(index == 0)
    def _():
        for v in range(breadth // QB):
            out_ref[v * QB : (v + 1) * QB] = weight_ref[:, v * QB : (v + 1) * QB]

    factor = size ** (-0.5)
    first = index * rows
    places = lax.broadcasted_iota(jnp.int32, (count, k_ref.shape[1]), 1)
    step = lax.broadcasted_iota(jnp.int32, (count, nk_ref.shape[1]), 0) % steps
    later = lax.broadcasted_iota(jnp.int32, (count, nk_ref.shape[1]), 1) > step
    attended = []
    for r in range(rows):
        q = q_ref[r]
        old = lax.dot_general(q, k_ref[r], NT, preferred_element_type=F32) * factor
        new = lax.dot_general(q, nk_ref[r], NT, preferred_element_type=F32) * factor
        old = jnp.where(places < len_ref[first + r], old, -jnp.inf)
        new = jnp.where(later, -jnp.inf, new)
        top = jnp.maximum(
            jnp.max(old, axis=1, keepdims=True), jnp.max(new, axis=1, keepdims=True)
        )
        old, new = jnp.exp(old - top), jnp.exp(new - top)
        total = jnp.sum(old, axis=1, keepdims=True) + jnp.sum(new, axis=1, keepdims=True)
        old, new = (old / total).astype(BF16), (new / total).astype(BF16)
        mixed = jnp.dot(old, v_ref[r], preferred_element_type=F32)
        attended.append(mixed + jnp.dot(new, nv_ref[r], preferred_element_type=F32))
    for h in range(count // steps):
        block = [mixed[h * steps : (h + 1) * steps] for mixed in attended]
        block = jnp.concatenate(block, axis=0).astype(BF16)
        height = rows * steps
        start = breadth + h * height * pl.num_programs(0) + index * height
        out_ref[pl.ds(pl.multiple_of(start, height), height)] = block


def make_payload(queries, new_keys, new_values, key_cache, value_cache, cache_lengths, weight):
    rows, steps, _, heads, size = queries.shape
    cache = key_cache.shape[2]
    tile = 4
    q = queries[:, :, 0].transpose(0, 2, 1, 3).reshape(rows, heads * steps, size)
    pad = ((0, 0), (0, 16 - steps), (0, 0))
    nk, nv = jnp.pad(new_keys[:, :, 0], pad), jnp.pad(new_values[:, :, 0], pad)
    shape = (weight.shape[1] + heads * rows * steps, QB)

    def block(height):
        return pl.BlockSpec((tile, height, size), lambda i: (i, 0, 0))

    return pl.pallas_call(
        functools.partial(payload_kernel, steps),
        grid=(rows // tile,),
        out_shape=jax.ShapeDtypeStruct(shape, BF16),
        in_specs=[pl.BlockSpec(memory_space=pltpu.SMEM)]
        + [block(heads * steps), block(16), block(16), block(cache), block(cache)]
        + [pl.BlockSpec(weight.shape, lambda i: (0, 0))],
        out_specs=pl.BlockSpec(shape, lambda i: (0, 0)),
        cost_estimate=pl.CostEstimate(flops=2**34, bytes_accessed=2**22, transcendentals=0),
    )(cache_lengths, q, nk, nv, key_cache[:, 0], value_cache[:, 0], weight)


def grad_kernel(names, lefts, rights, core_ref, *refs):
    left_refs = dict(zip(lefts, refs))
    right_refs = dict(zip(rights, refs[len(lefts) :]))
    out_refs = refs[len(lefts) + len(rights) :]
    group = len(names) // (len(out_refs) // 2)
    own = core_ref[0] == 0
    for n, (left, right) in enumerate(names):
        part = jnp.dot(left_refs[left][...], right_refs[right][...], preferred_element_type=F32)
        part = part.astype(BF16)
        half = part.shape[0] // 2
        keep_ref, send_ref = out_refs[n // group * 2 : n // group * 2 + 2]
        for w in range(2):
            start = n % group * half + w * QB
            rows = slice(start, start + QB)
            for v in range(keep_ref.shape[0]):
                columns = slice(v * QB, (v + 1) * QB)
                low = part[2 * w * QB : (2 * w + 1) * QB, columns]
                high = part[(2 * w + 1) * QB : (2 * w + 2) * QB, columns]
                keep_ref[v, rows] = jnp.where(own, low, high)
                send_ref[v, rows] = jnp.where(own, high, low)


def grad_parts(core, names, left_arrays, right_arrays, group):
    lefts = sorted({left for left, _ in names})
    rights = sorted({right for _, right in names})
    height, depth = left_arrays[lefts[0]].shape
    breadth = right_arrays[rights[0]].shape[1]
    tile = 2 * QB
    rows = group * height // 2
    shape = jax.ShapeDtypeStruct((breadth // QB, rows, QB), BF16)
    out = pl.BlockSpec((tile // QB, rows, QB), lambda i: (i, 0, 0))
    copies = 2 * len(names) // group
    return pl.pallas_call(
        functools.partial(grad_kernel, names, lefts, rights),
        grid=(breadth // tile,),
        out_shape=(shape,) * copies,
        in_specs=[pl.BlockSpec(memory_space=pltpu.SMEM)]
        + [pl.BlockSpec((height, depth), lambda i: (0, 0))] * len(lefts)
        + [pl.BlockSpec((depth, tile), lambda i: (0, i))] * len(rights),
        out_specs=(out,) * copies,
        compiler_params=pltpu.CompilerParams(vmem_limit_bytes=40 * 2**20),
        cost_estimate=pl.CostEstimate(
            flops=2**20,
            bytes_accessed=2**10,
            transcendentals=0,
        ),
    )(core.reshape(1), *[left_arrays[n] for n in lefts], *[right_arrays[n] for n in rights])


def project_kernel(scale_ref, *refs):
    left_refs, (quant_ref, quant_other_ref), out_refs = refs[:NY], refs[NY : NY + 2], refs[NY + 2 :]
    tile, _, _, count, _ = left_refs[0].shape
    rows = tile * 2 * count
    total = jnp.zeros((rows, 2 * QB), F32)
    for k in range(NY):
        for j, quant in enumerate((quant_ref, quant_other_ref)):
            right = jnp.concatenate([quant[k, 0], quant[k, 1]], axis=1)
            product = jnp.dot(
                left_refs[k][:, :, j].reshape(rows, QB), right, preferred_element_type=F32
            )
            total = total + product * scale_ref[2 * k + j : 2 * k + j + 1, :]
    total = total.reshape(tile, 2, count, 2 * QB)
    for w in range(2):
        for v in range(2):
            out_refs[2 * w + v][...] = total[:, w, :, v * QB : (v + 1) * QB].astype(
                out_refs[2 * w + v].dtype
            )


def project(lefts, quantized, quantized_other, scales):
    tile = 2
    count = lefts[0].shape[3]
    whole = pl.BlockSpec(quantized.shape, lambda i: (0, 0, 0, 0))
    shape = (NZ, count, QB)
    return pl.pallas_call(
        project_kernel,
        grid=(NZ // tile,),
        out_shape=(jax.ShapeDtypeStruct(shape, F32),) + (jax.ShapeDtypeStruct(shape, BF16),) * 3,
        in_specs=[pl.BlockSpec(scales.shape, lambda i: (0, 0))]
        + [pl.BlockSpec((tile, 2, 2, count, QB), lambda i: (i, 0, 0, 0, 0))] * NY
        + [whole, whole],
        out_specs=(pl.BlockSpec((tile, count, QB), lambda i: (i, 0, 0)),) * 4,
        cost_estimate=pl.CostEstimate(
            flops=2 * NZ * 2 * count * 2 * QB * 8 * QB,
            bytes_accessed=4 * 2**20,
            transcendentals=0,
        ),
    )(scales, *lefts, quantized, quantized_other)


def gather_y(x):
    half = x.shape[0] // 2
    down = shift(x, "y", NY, 1)
    up = shift(x, "y", NY, -1)
    far_a = shift(down[:half], "y", NY, 1)
    far_b = shift(up[half:], "y", NY, -1)
    return x, down, jnp.concatenate([far_a, far_b], axis=0), up


def add_cores(outs):
    return [
        (keep.astype(F32) + swap(send, "c").astype(F32)).astype(BF16)
        for keep, send in zip(outs[::2], outs[1::2])
    ]


def z_block(pieces, index):
    return jnp.concatenate([pick(a, index) for a in pieces], axis=0).astype(F32)


def z_first(pieces, z):
    far = z_block(pieces, (z + 4) % NZ).astype(BF16)
    half = far.shape[0] // 2
    fwd = shift(far[:half], "z", NZ, 1).astype(F32)
    bwd = shift(far[half:], "z", NZ, -1).astype(F32)
    mine = z_block(pieces, (z + 3) % NZ)
    fwd = jnp.concatenate([mine[:half] + fwd, mine[half:]], axis=0)
    mine = z_block(pieces, (z - 3) % NZ)
    bwd = jnp.concatenate([mine[:half], mine[half:] + bwd], axis=0)
    return fwd.astype(BF16), bwd.astype(BF16)


def z_next(pieces, z, k, fwd, bwd):
    fwd = z_block(pieces, (z + k) % NZ) + shift(fwd, "z", NZ, 1).astype(F32)
    bwd = z_block(pieces, (z - k) % NZ) + shift(bwd, "z", NZ, -1).astype(F32)
    return fwd.astype(BF16), bwd.astype(BF16)


def z_last(pieces, z, fwd, bwd):
    fwd, bwd = shift(fwd, "z", NZ, 1), shift(bwd, "z", NZ, -1)
    return z_block(pieces, z) + fwd.astype(F32) + bwd.astype(F32)


def per_device(
    activations,
    cotangent,
    weight,
    queries,
    new_keys,
    new_values,
    key_cache,
    value_cache,
    cache_lengths,
):
    z, xh, core, y, xl = (lax.axis_index(a) for a in ("z", "xh", "c", "y", "xl"))
    cot_other = swap(cotangent, "xl")
    acts = gather_y(activations.T)

    local_rows, local_steps = queries.shape[0], queries.shape[1]
    count = local_rows * local_steps
    payload = make_payload(
        queries, new_keys, new_values, key_cache, value_cache, cache_lengths, weight
    )
    everyone = lax.all_gather(payload, "z", axis=0, tiled=False)

    early = [(0, 0), (1, 0)]
    late = [(2, 0), (3, 0)] + [(k, 1) for k in range(NY)]
    outs = grad_parts(core, early, acts, (after(cotangent, payload),), 1)
    pieces = add_cores(outs)
    cot_other = after(cot_other, *pieces)
    outs = grad_parts(core, late, acts, (cotangent, cot_other), 3)
    part = jnp.concatenate(add_cores(outs), axis=1)
    part = after(part, everyone)
    late_part = lax.psum_scatter(part, "z", scatter_dimension=0, tiled=False)

    blocks = lax.dynamic_slice_in_dim(everyone, z * QB, QB, axis=1).reshape(NY, 2, QB, QB)
    blocks = after(blocks, part)
    kept, sent = pick(blocks, xl, 1), pick(blocks, 1 - xl, 1)
    blocks = jnp.stack([kept, swap(sent, "xl")], axis=1)
    weight_here = jnp.stack([pick(blocks, (y - k) % NY) for k in range(NY)], axis=0)

    heads = everyone[:, NZ * QB :].reshape(NZ, 2, 2, count, QB)
    heads = jnp.stack([pick(heads, core, 2), pick(heads, 1 - core, 2)], axis=2)
    kept, sent = pick(heads, xh, 1), pick(heads, 1 - xh, 1)
    got = swap(after(sent, part), "xh")
    pieces = lax.optimization_barrier((*pieces, part))[:-1]
    ways = z_first(pieces, z)
    ways = z_next(pieces, z, 2, *ways)
    own = jnp.stack([kept, got], axis=1)
    down, up = shift(own, "y", NY, 1), shift(own, "y", NY, -1)
    ways = z_next(pieces, z, 1, *lax.optimization_barrier((*ways, own))[:2])
    far_a = shift(down[: NZ // 2], "y", NY, 1)
    far_b = shift(up[NZ // 2 :], "y", NY, -1)
    early_part = z_last(pieces, z, *lax.optimization_barrier((*ways, down, up))[:2])
    lefts = (own, down, jnp.concatenate([far_a, far_b], axis=0), up)

    sums = {}
    for names, part in ((early, early_part), (late, late_part)):
        part = part.reshape(len(names), 2, QB, QB)
        kept, sent = pick(part, xh, 1), pick(part, 1 - xh, 1)
        part = kept.astype(F32) + swap(sent.astype(BF16), "xh").astype(F32)
        sums.update({name: part[n] for n, name in enumerate(names)})
    grad = jnp.stack(
        [jnp.stack([sums[k, h] for h in range(2)], axis=0) for k in range(NY)], axis=0
    )

    updated = weight_here.astype(F32) - learn_rate * grad
    largest = jnp.max(jnp.abs(updated), axis=(2, 3))
    scales = ((largest + epsilon) / scale_limit).astype(BF16)
    quantized = (updated / scales.astype(F32)[:, :, None, None]).astype(BF16)
    quantized_other, scales_other = swap(quantized, "c"), swap(scales, "c")

    both = jnp.stack([scales, scales_other], axis=1).astype(F32).reshape(2 * NY, 2, 1)
    both = jnp.broadcast_to(both, (2 * NY, 2, QB)).reshape(2 * NY, 2 * QB)
    mine, to_lo, to_hi, to_both = project(lefts, quantized, quantized_other, both)
    out = (
        mine
        + swap(to_lo, "xl").astype(F32)
        + swap(to_hi, "xh").astype(F32)
        + lax.ppermute(to_both, ("xh", "xl"), [(i, 3 - i) for i in range(4)]).astype(F32)
    ).astype(BF16)

    blocks = grad.astype(BF16)
    blocks = jnp.stack([pick(blocks, (y - k) % NY) for k in range(NY)], axis=0)
    kept, got = blocks[:, 0], swap(blocks[:, 1], "xl")
    first = jnp.where(xl == 0, kept, got)
    second = jnp.where(xl == 0, got, kept)
    blocks = jnp.stack([first, second], axis=1).reshape(NZ, QB, QB)
    blocks = jnp.concatenate([out, blocks], axis=1)
    blocks = lax.all_to_all(blocks, "z", 0, 0, tiled=True).transpose(1, 0, 2)
    blocks = blocks.reshape(count + QB, NZ * QB)
    decoded = blocks[:count].reshape(local_rows, local_steps, NZ * QB)
    return (blocks[count:].astype(F32), decoded)


def solution(mesh):
    inner = Mesh(mesh.devices.reshape(8, 2, 2, 4, 2), ("z", "xh", "c", "y", "xl"))
    fsdp, tp = ("z", "xh", "c"), ("y", "xl")
    return jax.shard_map(
        per_device,
        mesh=inner,
        in_specs=(
            P(fsdp, tp),
            P(fsdp, tp),
            P(fsdp, tp),
            P(fsdp, None, tp, None, None),
            P(fsdp, None, tp, None),
            P(fsdp, None, tp, None),
            P(fsdp, tp, None, None),
            P(fsdp, tp, None, None),
            P(fsdp),
        ),
        out_specs=(P(fsdp, tp), P(fsdp, None, tp)),
        check_vma=False,
    )
```

time: 252 us -> 191 us (0.76); the launches traced: 248 us -> 191 us
  starting transfers between devices: 104 us -> 46.8 us
  waiting for transfers between devices: 89.9 us -> 60.3 us
  blocking collectives: 0 us -> 17.6 us
  between operations: 1.58 us -> 14.6 us
  other arithmetic: 13.2 us -> 9.63 us
    ppermute x32 -> x16, starting transfers between devices: 47.8 us -> 26.1 us  [shift(): return lax.ppermute(x, axis, [(i, (i + step) % size) for i in range(size)])]
    all_to_all x3 -> x0, starting transfers between devices: 21 us -> none  [the longest x2 12.2 us: per_device(): blocks = lax.all_to_all(blocks, 'z', 0, 0, tiled=True)]
    all_to_all x0 -> x1, blocking collectives: none -> 17.6 us  [per_device(): blocks = lax.all_to_all(blocks, 'z', 0, 0, tiled=True).transpose(1, 0, 2)]
    ppermute x10 -> x14, starting transfers between devices: 34.8 us -> 19.2 us  [swap(): return lax.ppermute(x, axis, [(0, 1), (1, 0)])]
    all_to_all x3 -> x0, waiting for transfers between devices: 15.3 us -> none  [the longest x1 15.3 us: per_device(): out = lax.all_to_all(out, ('z', 'xh', 'xl'), 0, 0, tiled=True)]
    ppermute x10 -> x14, waiting for transfers between devices: 30.1 us -> 18.7 us  [swap(): return lax.ppermute(x, axis, [(0, 1), (1, 0)])]
    ppermute x32 -> x16, waiting for transfers between devices: 44.4 us -> 33.4 us  [shift(): return lax.ppermute(x, axis, [(i, (i + step) % size) for i in range(size)])]
    reduce_scatter x0 -> x1, waiting for transfers between devices: none -> 5.57 us  [per_device(): late_part = lax.psum_scatter(part, 'z', scatter_dimension=0, tiled=False)]
  transfers between devices with their start and end apart: 45 -> 33, of which waited for: 21 -> 18; matrix products, arithmetic and copies ran while one was open for 9% -> 10% of each run, Pallas kernels for 10% -> 14%
where the time goes in v1:
time: 191 us
  waiting for transfers between devices  60.3 us (32%)
  starting transfers between devices  46.8 us (25%)
  Pallas kernels  26.6 us (14%)
  blocking collectives  17.6 us (9%)
  local copies, waits for them, and re-layouts  15.3 us (8%)
  between operations  14.6 us (8%)
  other arithmetic  9.63 us (5%)
    ppermute x16, waiting for transfers between devices, shift(): return lax.ppermute(x, axis, [(i, (i + step) % size) for i in range(size)])  33.4 us
    ppermute x16, starting transfers between devices, shift(): return lax.ppermute(x, axis, [(i, (i + step) % size) for i in range(size)])  26.1 us
    ppermute x14, starting transfers between devices, swap(): return lax.ppermute(x, axis, [(0, 1), (1, 0)])  19.2 us
    ppermute x14, waiting for transfers between devices, swap(): return lax.ppermute(x, axis, [(0, 1), (1, 0)])  18.7 us
    all_to_all x1, blocking collectives, per_device(): blocks = lax.all_to_all(blocks, 'z', 0, 0, tiled=True).transpose(1, 0, 2)  17.6 us
    pallas_call x2, Pallas kernels, grad_parts(): pl.pallas_call(functools.partial(grad_kernel, names, lefts, rights), grid...  13.6 us
    pallas_call x1, Pallas kernels, make_payload(): pl.pallas_call(functools.partial(payload_kernel, steps), grid=(rows // ti...  8.41 us
    reduce_scatter x1, waiting for transfers between devices, per_device(): late_part = lax.psum_scatter(part, 'z', scatter_dimension=0, tiled=False)  5.57 us
  transfers between devices with their start and end apart: 33, of which 18 were waited for; matrix products, arithmetic and copies ran while one was open for 10% of the time, Pallas kernels for 14%

profile of v1, /device:TPU:1, one launch (start us, length us, event | category | flops | bytes accessed | tf_op | source)
XLA Modules:
  0.0 190.8 jit_solution(2043151862006693083)
XLA Ops:
  8.9 2.2 %collective-permute-start = (bf16[512,1024]{1,0:T(8,128)(2,1)S(1)}, bf16[512,1024]{1,0:T(8,128)(2,1)}, u32[]{:S(2)}, u32[]{:S(2)}) collective-permute-start(bf16[512,1024]{1,0:T(8,128)(2,1)S(1)} %bitcast.101), channel_id=1, source_target_pairs={{0,2},{2,4},{4,6},{6,0},{1,3},{3,5},{5,7},{7,1},{8,10},{10,12},{12... | collective-permute-start | bytes 3145736 | tf_op jit(solution)/shard_map/ppermute | solution.py:24
  16.6 8.4 %shard_map.104 = bf16[1280,128]{1,0:T(8,128)(2,1)} custom-call(s32[16]{0:T(128)} %len_ref.1, bf16[16,16,128]{2,1,0:T(8,128)(2,1)} %bitcast.120, bf16[16,16,128]{2,1,0:T(8,128)(2,1)} %pad.7.nk_ref, bf16[16,16,128]{2,1,0:T(8,128)(2,1)} %pad.8.nv_ref, bf16[16,512,128]{2,1,0:T(8,128)(2,1)} %bitcast.125, bf16[16,512,128]{2,1,0:T(8,128)(2,1)} %bitcast.126, ...), custom_call_target="tpu_custom_call" | custom-call | flops 17179869184 | bytes 4194304 | tf_op jit(solution)/shard_map/pallas_call | solution.py:89
  25.1 8.4 %collective-permute-done.refs_1_ = bf16[512,1024]{1,0:T(8,128)(2,1)} collective-permute-done((bf16[512,1024]{1,0:T(8,128)(2,1)S(1)}, bf16[512,1024]{1,0:T(8,128)(2,1)}, u32[]{:S(2)}, u32[]{:S(2)}) %collective-permute-start) | collective-permute-done | bytes 1048608 | tf_op jit(solution)/shard_map/ppermute | solution.py:24
  33.5 1.9 %slice.88 = bf16[256,1024]{1,0:T(8,128)(2,1)} slice(bf16[512,1024]{1,0:T(8,128)(2,1)} %collective-permute-done.refs_1_), slice={[0:256], [0:1024]} | slice | bytes 1048576 | tf_op jit(solution)/shard_map/slice | solution.py:195
  36.9 1.9 slice.89
  40.4 4.4 %shard_map.105 = (bf16[8,256,128]{2,1,0:T(8,128)(2,1)S(1)}, bf16[8,256,128]{2,1,0:T(8,128)(2,1)S(1)}, bf16[8,256,128]{2,1,0:T(8,128)(2,1)S(1)}, bf16[8,256,128]{2,1,0:T(8,128)(2,1)S(1)}) custom-call(s32[1]{0:T(128)} %bitcast.9.core_ref, bf16[512,1024]{1,0:T(8,128)(2,1)S(1)} %bitcast.103, bf16[512,1024]{1,0:T(8,128)(2,1)} %collective-permute-done.refs_1_, ...), custom_call_target="tpu_custom_call" | custom-call | flops 1048576 | bytes 1024 | tf_op jit(solution)/shard_map/pallas_call | solution.py:133
  44.8 3.4 %collective-permute-start.6 = (bf16[8,256,128]{2,1,0:T(8,128)(2,1)S(1)}, bf16[8,256,128]{2,1,0:T(8,128)(2,1)S(1)}, u32[]{:S(2)}, u32[]{:S(2)}) collective-permute-start(bf16[8,256,128]{2,1,0:T(8,128)(2,1)S(1)} %get-tuple-element.29), channel_id=1, source_target_pairs={{0,8},{8,0},{1,9},{9,1},{2,10},{10,2},{3,11},{11,3},{4,12},{12,4},... | collective-permute-start | bytes 1572872 | tf_op jit(solution)/shard_map/ppermute | solution.py:28
  48.3 2.2 %collective-permute-done.3 = bf16[256,1024]{1,0:T(8,128)(2,1)} collective-permute-done((bf16[256,1024]{1,0:T(8,128)(2,1)}, bf16[256,1024]{1,0:T(8,128)(2,1)}, u32[]{:S(2)}, u32[]{:S(2)}) %collective-permute-start.3) | collective-permute-done | bytes 524320 | tf_op jit(solution)/shard_map/ppermute | solution.py:24
  53.7 3.7 %collective-permute-done.4.refs_5_ = bf16[1024,1024]{1,0:T(8,128)(2,1)} collective-permute-done((bf16[1024,1024]{1,0:T(8,128)(2,1)S(1)}, bf16[1024,1024]{1,0:T(8,128)(2,1)}, u32[]{:S(2)}, u32[]{:S(2)}) %collective-permute-start.4) | collective-permute-done | bytes 2097184 | tf_op jit(solution)/shard_map/ppermute | solution.py:28
  57.4 9.3 %shard_map.106 = (bf16[8,768,128]{2,1,0:T(8,128)(2,1)S(1)}, bf16[8,768,128]{2,1,0:T(8,128)(2,1)S(1)}, bf16[8,768,128]{2,1,0:T(8,128)(2,1)S(1)}, bf16[8,768,128]{2,1,0:T(8,128)(2,1)S(1)}) custom-call(s32[1]{0:T(128)} %bitcast.9.core_ref, bf16[512,1024]{1,0:T(8,128)(2,1)S(1)} %bitcast.104, bf16[512,1024]{1,0:T(8,128)(2,1)} %collective-permute-done.refs_1_, ...), custom_call_target="tpu_custom_call" | custom-call | flops 1048576 | bytes 1024 | tf_op jit(solution)/shard_map/pallas_call | solution.py:133
  66.7 3.5 %collective-permute-start.7 = (bf16[8,768,128]{2,1,0:T(8,128)(2,1)S(1)}, bf16[8,768,128]{2,1,0:T(8,128)(2,1)S(1)}, u32[]{:S(2)}, u32[]{:S(2)}) collective-permute-start(bf16[8,768,128]{2,1,0:T(8,128)(2,1)S(1)} %get-tuple-element.32), channel_id=1, source_target_pairs={{0,8},{8,0},{1,9},{9,1},{2,10},{10,2},{3,11},{11,3},{4,12},{12,4},... | collective-permute-start | bytes 4718600 | tf_op jit(solution)/shard_map/ppermute | solution.py:28
  70.2 2.9 %collective-permute-done.7 = bf16[8,768,128]{2,1,0:T(8,128)(2,1)S(1)} collective-permute-done((bf16[8,768,128]{2,1,0:T(8,128)(2,1)S(1)}, bf16[8,768,128]{2,1,0:T(8,128)(2,1)S(1)}, u32[]{:S(2)}, u32[]{:S(2)}) %collective-permute-start.7) | collective-permute-done | bytes 1572896 | tf_op jit(solution)/shard_map/ppermute | solution.py:28
  73.6 1.8 collective-permute-done.8
  75.8 1.9 pad_maximum_fusion
  79.1 2.8 %collective-permute-start.14 = (bf16[8,2,64,128]{3,2,1,0:T(8,128)(2,1)S(1)}, bf16[8,2,64,128]{3,2,1,0:T(8,128)(2,1)S(1)}, u32[]{:S(2)}, u32[]{:S(2)}) collective-permute-start(bf16[8,2,64,128]{3,2,1,0:T(8,128)(2,1)S(1)} %get-tuple-element.39), channel_id=1, source_target_pairs={{0,16},{16,0},{1,17},{17,1},{2,18},{18,2},{3,19},{19,3},{4,20},{20... | collective-permute-start | bytes 786440 | tf_op jit(solution)/shard_map/ppermute | solution.py:28
  82.0 5.8 %collective-permute-start.12 = (bf16[256,128]{1,0:T(8,128)(2,1)S(1)}, bf16[256,128]{1,0:T(8,128)(2,1)S(1)}, u32[]{:S(2)}, u32[]{:S(2)}) collective-permute-start(bf16[256,128]{1,0:T(8,128)(2,1)S(1)} %get-tuple-element.63), channel_id=1, source_target_pairs={{0,224},{32,0},{64,32},{96,64},{128,96},{160,128},{192,160},{224,1... | collective-permute-start | bytes 196616 | tf_op jit(solution)/shard_map/ppermute | solution.py:24
  89.2 3.4 %collective-permute-start.13 = (bf16[512,128]{1,0:T(8,128)(2,1)S(1)}, bf16[512,128]{1,0:T(8,128)(2,1)S(1)}, u32[]{:S(2)}, u32[]{:S(2)}) collective-permute-start(bf16[512,128]{1,0:T(8,128)(2,1)S(1)} %pad_maximum_fusion.10), channel_id=1, source_target_pairs={{0,224},{32,0},{64,32},{96,64},{128,96},{160,128},{192,160},{224,1... | collective-permute-start | bytes 393224 | tf_op jit(solution)/shard_map/ppermute | solution.py:24
  92.7 4.1 %collective-permute-done.13 = bf16[512,128]{1,0:T(8,128)(2,1)S(1)} collective-permute-done((bf16[512,128]{1,0:T(8,128)(2,1)S(1)}, bf16[512,128]{1,0:T(8,128)(2,1)S(1)}, u32[]{:S(2)}, u32[]{:S(2)}) %collective-permute-start.13) | collective-permute-done | bytes 131104 | tf_op jit(solution)/shard_map/ppermute | solution.py:24
  96.9 4.7 %collective-permute-done.11 = bf16[512,128]{1,0:T(8,128)(2,1)S(1)} collective-permute-done((bf16[512,128]{1,0:T(8,128)(2,1)S(1)}, bf16[512,128]{1,0:T(8,128)(2,1)S(1)}, u32[]{:S(2)}, u32[]{:S(2)}) %collective-permute-start.11) | collective-permute-done | bytes 131104 | tf_op jit(solution)/shard_map/ppermute | solution.py:24
  101.9 2.7 %collective-permute-start.18 = (bf16[8,2,2,64,128]{4,3,2,1,0:T(8,128)(2,1)S(1)}, bf16[8,2,2,64,128]{4,3,2,1,0:T(8,128)(2,1)S(1)}, u32[]{:S(2)}, u32[]{:S(2)}) collective-permute-start(bf16[8,2,2,64,128]{4,3,2,1,0:T(8,128)(2,1)S(1)} %pad_maximum_fusion.2.refs_0_), channel_id=1, source_target_pairs={{0,6},{2,0},{4,2},{6,4},{1,7},{3,1},{5,3},{7,5},{8,14},{10,8},{12,... | collective-permute-start | bytes 1572872 | tf_op jit(solution)/shard_map/ppermute | solution.py:24
  105.9 3.4 %collective-permute-done.16 = bf16[512,128]{1,0:T(8,128)(2,1)S(1)} collective-permute-done((bf16[512,128]{1,0:T(8,128)(2,1)S(1)}, bf16[512,128]{1,0:T(8,128)(2,1)S(1)}, u32[]{:S(2)}, u32[]{:S(2)}) %collective-permute-start.16) | collective-permute-done | bytes 131104 | tf_op jit(solution)/shard_map/ppermute | solution.py:24
  109.4 3.8 %collective-permute-done.15 = bf16[512,128]{1,0:T(8,128)(2,1)S(1)} collective-permute-done((bf16[512,128]{1,0:T(8,128)(2,1)S(1)}, bf16[512,128]{1,0:T(8,128)(2,1)S(1)}, u32[]{:S(2)}, u32[]{:S(2)}) %collective-permute-start.15) | collective-permute-done | bytes 131104 | tf_op jit(solution)/shard_map/ppermute | solution.py:24
  117.9 4.7 %collective-permute-done.19 = bf16[512,128]{1,0:T(8,128)(2,1)S(1)} collective-permute-done((bf16[512,128]{1,0:T(8,128)(2,1)S(1)}, bf16[512,128]{1,0:T(8,128)(2,1)S(1)}, u32[]{:S(2)}, u32[]{:S(2)}) %collective-permute-start.19) | collective-permute-done | bytes 131104 | tf_op jit(solution)/shard_map/ppermute | solution.py:24
  123.1 2.7 %collective-permute-start.25 = (bf16[4,2,2,64,128]{4,3,2,1,0:T(8,128)(2,1)S(1)}, bf16[4,2,2,64,128]{4,3,2,1,0:T(8,128)(2,1)S(1)}, u32[]{:S(2)}, u32[]{:S(2)}) collective-permute-start(bf16[4,2,2,64,128]{4,3,2,1,0:T(8,128)(2,1)S(1)} %slice.100), channel_id=1, source_target_pairs={{0,6},{2,0},{4,2},{6,4},{1,7},{3,1},{5,3},{7,5},{8,14},{10,8},{12,... | collective-permute-start | bytes 786440 | tf_op jit(solution)/shard_map/ppermute | solution.py:24
  127.5 5.6 %reduce-scatter.2.cloned.1.call-done = bf16[1,1536,128]{2,1,0:T(8,128)(2,1)} async-done(((bf16[8,1536,128]{2,1,0:T(8,128)(2,1)}), bf16[1,1536,128]{2,1,0:T(8,128)(2,1)}) %reduce-scatter.2.cloned.1.call-update) | async-done | bytes 393232 | tf_op jit(solution)/shard_map/reduce_scatter | solution.py:264
  134.0 2.3 %collective-permute-start.22 = (bf16[6,128,128]{2,1,0:T(8,128)(2,1)S(1)}, bf16[6,128,128]{2,1,0:T(8,128)(2,1)S(1)}, u32[]{:S(2)}, u32[]{:S(2)}) collective-permute-start(bf16[6,128,128]{2,1,0:T(8,128)(2,1)S(1)} %dynamic-slice_bitcast_fusion), channel_id=1, source_target_pairs={{0,16},{16,0},{1,17},{17,1},{2,18},{18,2},{3,19},{19,3},{4,20},{20... | collective-permute-start | bytes 589832 | tf_op jit(solution)/shard_map/ppermute | solution.py:28
  137.1 4.3 %collective-permute-done.22 = bf16[6,128,128]{2,1,0:T(8,128)(2,1)S(1)} collective-permute-done((bf16[6,128,128]{2,1,0:T(8,128)(2,1)S(1)}, bf16[6,128,128]{2,1,0:T(8,128)(2,1)S(1)}, u32[]{:S(2)}, u32[]{:S(2)}) %collective-permute-start.22) | collective-permute-done | bytes 196640 | tf_op jit(solution)/shard_map/ppermute | solution.py:28
  147.9 4.5 %shard_map.107 = (f32[8,64,128]{2,1,0:T(8,128)}, bf16[8,64,128]{2,1,0:T(8,128)(2,1)}, bf16[8,64,128]{2,1,0:T(8,128)(2,1)}, bf16[8,64,128]{2,1,0:T(8,128)(2,1)}) custom-call(f32[8,256]{1,0:T(8,128)} %broadcast_bitcast_fusion.scale_ref, bf16[8,2,2,64,128]{4,3,2,1,0:T(8,128)(2,1)} %copy-done.1, bf16[8,2,2,64,128]{4,3,2,1,0:T(8,128)(2,1)} %copy-done.4, ...), custom_call_target="tpu_custom_call" | custom-call | flops 536870912 | bytes 4194304 | tf_op jit(solution)/shard_map/pallas_call | solution.py:175
  152.9 2.1 %collective-permute-start.28 = (bf16[8,64,128]{2,1,0:T(8,128)(2,1)}, bf16[8,64,128]{2,1,0:T(8,128)(2,1)S(1)}, u32[]{:S(2)}, u32[]{:S(2)}) collective-permute-start(bf16[8,64,128]{2,1,0:T(8,128)(2,1)} %get-tuple-element.46), channel_id=1, source_target_pairs={{0,16},{16,0},{1,17},{17,1},{2,18},{18,2},{3,19},{19,3},{4,20},{20... | collective-permute-start | bytes 393224 | tf_op jit(solution)/shard_map/ppermute | solution.py:28
  157.0 3.8 %collective-permute-done.28 = bf16[8,64,128]{2,1,0:T(8,128)(2,1)S(1)} collective-permute-done((bf16[8,64,128]{2,1,0:T(8,128)(2,1)}, bf16[8,64,128]{2,1,0:T(8,128)(2,1)S(1)}, u32[]{:S(2)}, u32[]{:S(2)}) %collective-permute-start.28) | collective-permute-done | bytes 131104 | tf_op jit(solution)/shard_map/ppermute | solution.py:28
  160.8 2.5 %collective-permute-done.29 = bf16[8,64,128]{2,1,0:T(8,128)(2,1)S(1)} collective-permute-done((bf16[8,64,128]{2,1,0:T(8,128)(2,1)}, bf16[8,64,128]{2,1,0:T(8,128)(2,1)S(1)}, u32[]{:S(2)}, u32[]{:S(2)}) %collective-permute-start.29) | collective-permute-done | bytes 131104 | tf_op jit(solution)/shard_map/ppermute | solution.py:310
  164.3 17.6 %all_to_all.5 = bf16[8,192,128]{2,1,0:T(8,128)(2,1)S(1)} all-to-all(bf16[8,192,128]{2,1,0:T(8,128)(2,1)S(1)} %pad_maximum_fusion.5), channel_id=1, replica_groups=mesh['z'=8,'xh'=2,'c'=2,'y'=4,'xl'=2] {'z'}, dimensions={0} | all-to-all | bytes 786432 | tf_op jit(solution)/shard_map/all_to_all | solution.py:320
  (126 shorter events, 39.6 us)
Async XLA Ops:
  7.2 70.5 %all-gather.3.cloned.1.call-start = ((), (), s32[]{:S(2)}) async-start(), calls=%async_computation.3 | async-start | bytes 2949120 | tf_op jit(solution)/shard_map/all_gather | solution.py:254
  8.9 24.6 %collective-permute-start = (bf16[512,1024]{1,0:T(8,128)(2,1)S(1)}, bf16[512,1024]{1,0:T(8,128)(2,1)}, u32[]{:S(2)}, u32[]{:S(2)}) collective-permute-start(bf16[512,1024]{1,0:T(8,128)(2,1)S(1)} %bitcast.101), channel_id=1, source_target_pairs={{0,2},{2,4},{4,6},{6,0},{1,3},{3,5},{5,7},{7,1},{8,10},{10,12},{12... | collective-permute-start | bytes 3145736 | tf_op jit(solution)/shard_map/ppermute | solution.py:24
  11.1 25.9 %collective-permute-start.2 = (bf16[512,1024]{1,0:T(8,128)(2,1)S(1)}, bf16[512,1024]{1,0:T(8,128)(2,1)}, u32[]{:S(2)}, u32[]{:S(2)}) collective-permute-start(bf16[512,1024]{1,0:T(8,128)(2,1)S(1)} %bitcast.102), channel_id=1, source_target_pairs={{0,6},{2,0},{4,2},{6,4},{1,7},{3,1},{5,3},{7,5},{8,14},{10,8},{12,... | collective-permute-start | bytes 3145736 | tf_op jit(solution)/shard_map/ppermute | solution.py:24
  12.6 44.8 %collective-permute-start.4 = (bf16[1024,1024]{1,0:T(8,128)(2,1)S(1)}, bf16[1024,1024]{1,0:T(8,128)(2,1)}, u32[]{:S(2)}, u32[]{:S(2)}) collective-permute-start(bf16[1024,1024]{1,0:T(8,128)(2,1)S(1)} %copy-done), channel_id=1, source_target_pairs={{0,1},{1,0},{2,3},{3,2},{4,5},{5,4},{6,7},{7,6},{8,9},{9,8},{10,11... | collective-permute-start | bytes 6291464 | tf_op jit(solution)/shard_map/ppermute | solution.py:28
  25.0 108.0 %reduce-scatter.2.cloned.1.call-start = ((), (), s32[]{:S(2)}) async-start(), calls=%async_computation.2 | async-start | bytes 3538944 | tf_op jit(solution)/shard_map/reduce_scatter | solution.py:264
  35.4 13.0 %collective-permute-start.1 = (bf16[256,1024]{1,0:T(8,128)(2,1)}, bf16[256,1024]{1,0:T(8,128)(2,1)}, u32[]{:S(2)}, u32[]{:S(2)}) collective-permute-start(bf16[256,1024]{1,0:T(8,128)(2,1)} %slice.88), channel_id=1, source_target_pairs={{0,2},{2,4},{4,6},{6,0},{1,3},{3,5},{5,7},{7,1},{8,10},{10,12},{12... | collective-permute-start | bytes 1572872 | tf_op jit(solution)/shard_map/ppermute | solution.py:24
  38.8 11.7 %collective-permute-start.3 = (bf16[256,1024]{1,0:T(8,128)(2,1)}, bf16[256,1024]{1,0:T(8,128)(2,1)}, u32[]{:S(2)}, u32[]{:S(2)}) collective-permute-start(bf16[256,1024]{1,0:T(8,128)(2,1)} %slice.89), channel_id=1, source_target_pairs={{0,6},{2,0},{4,2},{6,4},{1,7},{3,1},{5,3},{7,5},{8,14},{10,8},{12,... | collective-permute-start | bytes 1572872 | tf_op jit(solution)/shard_map/ppermute | solution.py:24
  44.8 7.0 %collective-permute-start.6 = (bf16[8,256,128]{2,1,0:T(8,128)(2,1)S(1)}, bf16[8,256,128]{2,1,0:T(8,128)(2,1)S(1)}, u32[]{:S(2)}, u32[]{:S(2)}) collective-permute-start(bf16[8,256,128]{2,1,0:T(8,128)(2,1)S(1)} %get-tuple-element.29), channel_id=1, source_target_pairs={{0,8},{8,0},{1,9},{9,1},{2,10},{10,2},{3,11},{11,3},{4,12},{12,4},... | collective-permute-start | bytes 1572872 | tf_op jit(solution)/shard_map/ppermute | solution.py:28
  48.2 4.5 %collective-permute-start.5 = (bf16[8,256,128]{2,1,0:T(8,128)(2,1)S(1)}, bf16[8,256,128]{2,1,0:T(8,128)(2,1)S(1)}, u32[]{:S(2)}, u32[]{:S(2)}) collective-permute-start(bf16[8,256,128]{2,1,0:T(8,128)(2,1)S(1)} %get-tuple-element.27), channel_id=1, source_target_pairs={{0,8},{8,0},{1,9},{9,1},{2,10},{10,2},{3,11},{11,3},{4,12},{12,4},... | collective-permute-start | bytes 1572872 | tf_op jit(solution)/shard_map/ppermute | solution.py:28
  66.7 6.5 %collective-permute-start.7 = (bf16[8,768,128]{2,1,0:T(8,128)(2,1)S(1)}, bf16[8,768,128]{2,1,0:T(8,128)(2,1)S(1)}, u32[]{:S(2)}, u32[]{:S(2)}) collective-permute-start(bf16[8,768,128]{2,1,0:T(8,128)(2,1)S(1)} %get-tuple-element.32), channel_id=1, source_target_pairs={{0,8},{8,0},{1,9},{9,1},{2,10},{10,2},{3,11},{11,3},{4,12},{12,4},... | collective-permute-start | bytes 4718600 | tf_op jit(solution)/shard_map/ppermute | solution.py:28
  70.1 5.3 %collective-permute-start.8 = (bf16[8,768,128]{2,1,0:T(8,128)(2,1)S(1)}, bf16[8,768,128]{2,1,0:T(8,128)(2,1)S(1)}, u32[]{:S(2)}, u32[]{:S(2)}) collective-permute-start(bf16[8,768,128]{2,1,0:T(8,128)(2,1)S(1)} %get-tuple-element.34), channel_id=1, source_target_pairs={{0,8},{8,0},{1,9},{9,1},{2,10},{10,2},{3,11},{11,3},{4,12},{12,4},... | collective-permute-start | bytes 4718600 | tf_op jit(solution)/shard_map/ppermute | solution.py:28
  79.1 22.5 %collective-permute-start.14 = (bf16[8,2,64,128]{3,2,1,0:T(8,128)(2,1)S(1)}, bf16[8,2,64,128]{3,2,1,0:T(8,128)(2,1)S(1)}, u32[]{:S(2)}, u32[]{:S(2)}) collective-permute-start(bf16[8,2,64,128]{3,2,1,0:T(8,128)(2,1)S(1)} %get-tuple-element.39), channel_id=1, source_target_pairs={{0,16},{16,0},{1,17},{17,1},{2,18},{18,2},{3,19},{19,3},{4,20},{20... | collective-permute-start | bytes 786440 | tf_op jit(solution)/shard_map/ppermute | solution.py:28
  82.0 7.2 %collective-permute-start.12 = (bf16[256,128]{1,0:T(8,128)(2,1)S(1)}, bf16[256,128]{1,0:T(8,128)(2,1)S(1)}, u32[]{:S(2)}, u32[]{:S(2)}) collective-permute-start(bf16[256,128]{1,0:T(8,128)(2,1)S(1)} %get-tuple-element.63), channel_id=1, source_target_pairs={{0,224},{32,0},{64,32},{96,64},{128,96},{160,128},{192,160},{224,1... | collective-permute-start | bytes 196616 | tf_op jit(solution)/shard_map/ppermute | solution.py:24
  87.9 4.7 %collective-permute-start.10 = (bf16[256,128]{1,0:T(8,128)(2,1)S(1)}, bf16[256,128]{1,0:T(8,128)(2,1)S(1)}, u32[]{:S(2)}, u32[]{:S(2)}) collective-permute-start(bf16[256,128]{1,0:T(8,128)(2,1)S(1)} %get-tuple-element.58), channel_id=1, source_target_pairs={{0,32},{32,64},{64,96},{96,128},{128,160},{160,192},{192,224},{224... | collective-permute-start | bytes 196616 | tf_op jit(solution)/shard_map/ppermute | solution.py:24
  89.2 7.6 %collective-permute-start.13 = (bf16[512,128]{1,0:T(8,128)(2,1)S(1)}, bf16[512,128]{1,0:T(8,128)(2,1)S(1)}, u32[]{:S(2)}, u32[]{:S(2)}) collective-permute-start(bf16[512,128]{1,0:T(8,128)(2,1)S(1)} %pad_maximum_fusion.10), channel_id=1, source_target_pairs={{0,224},{32,0},{64,32},{96,64},{128,96},{160,128},{192,160},{224,1... | collective-permute-start | bytes 393224 | tf_op jit(solution)/shard_map/ppermute | solution.py:24
  92.6 8.9 %collective-permute-start.11 = (bf16[512,128]{1,0:T(8,128)(2,1)S(1)}, bf16[512,128]{1,0:T(8,128)(2,1)S(1)}, u32[]{:S(2)}, u32[]{:S(2)}) collective-permute-start(bf16[512,128]{1,0:T(8,128)(2,1)S(1)} %pad_maximum_fusion.9), channel_id=1, source_target_pairs={{0,32},{32,64},{64,96},{96,128},{128,160},{160,192},{192,224},{224... | collective-permute-start | bytes 393224 | tf_op jit(solution)/shard_map/ppermute | solution.py:24
  101.7 7.7 %collective-permute-start.16 = (bf16[512,128]{1,0:T(8,128)(2,1)S(1)}, bf16[512,128]{1,0:T(8,128)(2,1)S(1)}, u32[]{:S(2)}, u32[]{:S(2)}) collective-permute-start(bf16[512,128]{1,0:T(8,128)(2,1)S(1)} %add_convert_fusion.7), channel_id=1, source_target_pairs={{0,224},{32,0},{64,32},{96,64},{128,96},{160,128},{192,160},{224,1... | collective-permute-start | bytes 393224 | tf_op jit(solution)/shard_map/ppermute | solution.py:24
  101.8 12.3 %collective-permute-start.17 = (bf16[8,2,2,64,128]{4,3,2,1,0:T(8,128)(2,1)S(1)}, bf16[8,2,2,64,128]{4,3,2,1,0:T(8,128)(2,1)S(1)}, u32[]{:S(2)}, u32[]{:S(2)}) collective-permute-start(bf16[8,2,2,64,128]{4,3,2,1,0:T(8,128)(2,1)S(1)} %pad_maximum_fusion.2.refs_0_), channel_id=1, source_target_pairs={{0,2},{2,4},{4,6},{6,0},{1,3},{3,5},{5,7},{7,1},{8,10},{10,12},{12... | collective-permute-start | bytes 1572872 | tf_op jit(solution)/shard_map/ppermute | solution.py:24
  101.9 12.2 %collective-permute-start.18 = (bf16[8,2,2,64,128]{4,3,2,1,0:T(8,128)(2,1)S(1)}, bf16[8,2,2,64,128]{4,3,2,1,0:T(8,128)(2,1)S(1)}, u32[]{:S(2)}, u32[]{:S(2)}) collective-permute-start(bf16[8,2,2,64,128]{4,3,2,1,0:T(8,128)(2,1)S(1)} %pad_maximum_fusion.2.refs_0_), channel_id=1, source_target_pairs={{0,6},{2,0},{4,2},{6,4},{1,7},{3,1},{5,3},{7,5},{8,14},{10,8},{12,... | collective-permute-start | bytes 1572872 | tf_op jit(solution)/shard_map/ppermute | solution.py:24
  104.5 8.6 %collective-permute-start.15 = (bf16[512,128]{1,0:T(8,128)(2,1)S(1)}, bf16[512,128]{1,0:T(8,128)(2,1)S(1)}, u32[]{:S(2)}, u32[]{:S(2)}) collective-permute-start(bf16[512,128]{1,0:T(8,128)(2,1)S(1)} %add_convert_fusion.8), channel_id=1, source_target_pairs={{0,32},{32,64},{64,96},{96,128},{128,160},{160,192},{192,224},{224... | collective-permute-start | bytes 393224 | tf_op jit(solution)/shard_map/ppermute | solution.py:24
  114.0 8.6 %collective-permute-start.19 = (bf16[512,128]{1,0:T(8,128)(2,1)S(1)}, bf16[512,128]{1,0:T(8,128)(2,1)S(1)}, u32[]{:S(2)}, u32[]{:S(2)}) collective-permute-start(bf16[512,128]{1,0:T(8,128)(2,1)S(1)} %add_convert_fusion.6), channel_id=1, source_target_pairs={{0,32},{32,64},{64,96},{96,128},{128,160},{160,192},{192,224},{224... | collective-permute-start | bytes 393224 | tf_op jit(solution)/shard_map/ppermute | solution.py:24
  115.1 7.5 %collective-permute-start.20 = (bf16[512,128]{1,0:T(8,128)(2,1)S(1)}, bf16[512,128]{1,0:T(8,128)(2,1)S(1)}, u32[]{:S(2)}, u32[]{:S(2)}) collective-permute-start(bf16[512,128]{1,0:T(8,128)(2,1)S(1)} %add_convert_fusion.5), channel_id=1, source_target_pairs={{0,224},{32,0},{64,32},{96,64},{128,96},{160,128},{192,160},{224,1... | collective-permute-start | bytes 393224 | tf_op jit(solution)/shard_map/ppermute | solution.py:24
  117.8 5.0 %collective-permute-start.9 = (bf16[4,128,128]{2,1,0:T(8,128)(2,1)S(1)}, bf16[4,128,128]{2,1,0:T(8,128)(2,1)S(1)}, u32[]{:S(2)}, u32[]{:S(2)}) collective-permute-start(bf16[4,128,128]{2,1,0:T(8,128)(2,1)S(1)} %get-tuple-element.84), channel_id=1, source_target_pairs={{0,1},{1,0},{2,3},{3,2},{4,5},{5,4},{6,7},{7,6},{8,9},{9,8},{10,11... | collective-permute-start | bytes 393224 | tf_op jit(solution)/shard_map/ppermute | solution.py:28
  122.7 4.7 %collective-permute-start.21 = (bf16[2,128,128]{2,1,0:T(8,128)(2,1)S(1)}, bf16[2,128,128]{2,1,0:T(8,128)(2,1)S(1)}, u32[]{:S(2)}, u32[]{:S(2)}) collective-permute-start(bf16[2,128,128]{2,1,0:T(8,128)(2,1)S(1)} %fusion.6), channel_id=1, source_target_pairs={{0,16},{16,0},{1,17},{17,1},{2,18},{18,2},{3,19},{19,3},{4,20},{20... | collective-permute-start | bytes 196616 | tf_op jit(solution)/shard_map/ppermute | solution.py:28
  122.9 13.4 %collective-permute-start.24 = (bf16[4,2,2,64,128]{4,3,2,1,0:T(8,128)(2,1)S(1)}, bf16[4,2,2,64,128]{4,3,2,1,0:T(8,128)(2,1)S(1)}, u32[]{:S(2)}, u32[]{:S(2)}) collective-permute-start(bf16[4,2,2,64,128]{4,3,2,1,0:T(8,128)(2,1)S(1)} %slice.99), channel_id=1, source_target_pairs={{0,2},{2,4},{4,6},{6,0},{1,3},{3,5},{5,7},{7,1},{8,10},{10,12},{12... | collective-permute-start | bytes 786440 | tf_op jit(solution)/shard_map/ppermute | solution.py:24
  123.1 13.2 %collective-permute-start.25 = (bf16[4,2,2,64,128]{4,3,2,1,0:T(8,128)(2,1)S(1)}, bf16[4,2,2,64,128]{4,3,2,1,0:T(8,128)(2,1)S(1)}, u32[]{:S(2)}, u32[]{:S(2)}) collective-permute-start(bf16[4,2,2,64,128]{4,3,2,1,0:T(8,128)(2,1)S(1)} %slice.100), channel_id=1, source_target_pairs={{0,6},{2,0},{4,2},{6,4},{1,7},{3,1},{5,3},{7,5},{8,14},{10,8},{12,... | collective-permute-start | bytes 786440 | tf_op jit(solution)/shard_map/ppermute | solution.py:24
  134.0 7.4 %collective-permute-start.22 = (bf16[6,128,128]{2,1,0:T(8,128)(2,1)S(1)}, bf16[6,128,128]{2,1,0:T(8,128)(2,1)S(1)}, u32[]{:S(2)}, u32[]{:S(2)}) collective-permute-start(bf16[6,128,128]{2,1,0:T(8,128)(2,1)S(1)} %dynamic-slice_bitcast_fusion), channel_id=1, source_target_pairs={{0,16},{16,0},{1,17},{17,1},{2,18},{18,2},{3,19},{19,3},{4,20},{20... | collective-permute-start | bytes 589832 | tf_op jit(solution)/shard_map/ppermute | solution.py:28
  142.7 3.6 %collective-permute-start.23 = (bf16[4,2]{1,0:T(4,128)(2,1)S(1)}, bf16[4,2]{1,0:T(4,128)(2,1)S(1)}, u32[]{:S(2)}, u32[]{:S(2)}) collective-permute-start(bf16[4,2]{1,0:T(4,128)(2,1)S(1)} %get-tuple-element.53), channel_id=1, source_target_pairs={{0,8},{8,0},{1,9},{9,1},{2,10},{10,2},{3,11},{11,3},{4,12},{12,4},... | collective-permute-start | bytes 56 | tf_op jit(solution)/shard_map/ppermute | solution.py:28
  144.9 11.4 %collective-permute-start.30 = (bf16[4,128,128]{2,1,0:T(8,128)(2,1)S(1)}, bf16[4,128,128]{2,1,0:T(8,128)(2,1)S(1)}, u32[]{:S(2)}, u32[]{:S(2)}) collective-permute-start(bf16[4,128,128]{2,1,0:T(8,128)(2,1)S(1)} %slice_bitcast_fusion), channel_id=1, source_target_pairs={{0,1},{1,0},{2,3},{3,2},{4,5},{5,4},{6,7},{7,6},{8,9},{9,8},{10,11... | collective-permute-start | bytes 393224 | tf_op jit(solution)/shard_map/ppermute | solution.py:28
  152.4 4.6 %collective-permute-start.27 = (bf16[8,64,128]{2,1,0:T(8,128)(2,1)}, bf16[8,64,128]{2,1,0:T(8,128)(2,1)S(1)}, u32[]{:S(2)}, u32[]{:S(2)}) collective-permute-start(bf16[8,64,128]{2,1,0:T(8,128)(2,1)} %get-tuple-element.45), channel_id=1, source_target_pairs={{0,1},{1,0},{2,3},{3,2},{4,5},{5,4},{6,7},{7,6},{8,9},{9,8},{10,11... | collective-permute-start | bytes 393224 | tf_op jit(solution)/shard_map/ppermute | solution.py:28
  152.9 7.9 %collective-permute-start.28 = (bf16[8,64,128]{2,1,0:T(8,128)(2,1)}, bf16[8,64,128]{2,1,0:T(8,128)(2,1)S(1)}, u32[]{:S(2)}, u32[]{:S(2)}) collective-permute-start(bf16[8,64,128]{2,1,0:T(8,128)(2,1)} %get-tuple-element.46), channel_id=1, source_target_pairs={{0,16},{16,0},{1,17},{17,1},{2,18},{18,2},{3,19},{19,3},{4,20},{20... | collective-permute-start | bytes 393224 | tf_op jit(solution)/shard_map/ppermute | solution.py:28
  154.9 8.3 %collective-permute-start.29 = (bf16[8,64,128]{2,1,0:T(8,128)(2,1)}, bf16[8,64,128]{2,1,0:T(8,128)(2,1)S(1)}, u32[]{:S(2)}, u32[]{:S(2)}) collective-permute-start(bf16[8,64,128]{2,1,0:T(8,128)(2,1)} %get-tuple-element.47), channel_id=1, source_target_pairs={{0,17},{1,16},{16,1},{17,0},{2,19},{3,18},{18,3},{19,2},{4,21},{5,... | collective-permute-start | bytes 393224 | tf_op jit(solution)/shard_map/ppermute | solution.py:310
  (11 other events, 108.5 us)
Sparse Core Ops, SparseCore 0:
  25.1 41.6 all-gather.2
  77.8 55.1 reduce-scatter.1

commit v2 on v1

--- a/solution.py
+++ b/solution.py
@@ -98,67 +98,62 @@
     )(cache_lengths, q, nk, nv, key_cache[:, 0], value_cache[:, 0], weight)
 
 
-def grad_kernel(names, lefts, rights, core_ref, *refs):
+def grad_kernel(groups, lefts, rights, core_ref, *refs):
     left_refs = dict(zip(lefts, refs))
     right_refs = dict(zip(rights, refs[len(lefts) :]))
     out_refs = refs[len(lefts) + len(rights) :]
-    group = len(names) // (len(out_refs) // 2)
     own = core_ref[0] == 0
-    for n, (left, right) in enumerate(names):
-        part = jnp.dot(left_refs[left][...], right_refs[right][...], preferred_element_type=F32)
-        part = part.astype(BF16)
-        half = part.shape[0] // 2
-        keep_ref, send_ref = out_refs[n // group * 2 : n // group * 2 + 2]
-        for w in range(2):
-            start = n % group * half + w * QB
-            rows = slice(start, start + QB)
-            for v in range(keep_ref.shape[0]):
-                columns = slice(v * QB, (v + 1) * QB)
-                low = part[2 * w * QB : (2 * w + 1) * QB, columns]
-                high = part[(2 * w + 1) * QB : (2 * w + 2) * QB, columns]
-                keep_ref[v, rows] = jnp.where(own, low, high)
-                send_ref[v, rows] = jnp.where(own, high, low)
-
-
-def grad_parts(core, names, left_arrays, right_arrays, group):
-    lefts = sorted({left for left, _ in names})
-    rights = sorted({right for _, right in names})
+    for g, names in enumerate(groups):
+        keep_ref, send_ref = out_refs[2 * g : 2 * g + 2]
+        for n, (left, right) in enumerate(names):
+            part = jnp.dot(
+                left_refs[left][...], right_refs[right][...], preferred_element_type=F32
+            ).astype(BF16)
+            for w in range(2):
+                rows = slice((2 * n + w) * QB, (2 * n + w + 1) * QB)
+                for v in range(keep_ref.shape[0]):
+                    columns = slice(v * QB, (v + 1) * QB)
+                    low = part[2 * w * QB : (2 * w + 1) * QB, columns]
+                    high = part[(2 * w + 1) * QB : (2 * w + 2) * QB, columns]
+                    keep_ref[v, rows] = jnp.where(own, low, high)
+                    send_ref[v, rows] = jnp.where(own, high, low)
+
+
+def grad_parts(core, groups, left_arrays, right_arrays, moved):
+    lefts = sorted({left for names in groups for left, _ in names})
+    rights = sorted({right for names in groups for _, right in names})
     height, depth = left_arrays[lefts[0]].shape
     breadth = right_arrays[rights[0]].shape[1]
     tile = 2 * QB
-    rows = group * height // 2
-    shape = jax.ShapeDtypeStruct((breadth // QB, rows, QB), BF16)
-    out = pl.BlockSpec((tile // QB, rows, QB), lambda i: (i, 0, 0))
-    copies = 2 * len(names) // group
+    shapes, outs = [], []
+    for names in groups:
+        rows = len(names) * height // 2
+        shapes += [jax.ShapeDtypeStruct((breadth // QB, rows, QB), BF16)] * 2
+        outs += [pl.BlockSpec((tile // QB, rows, QB), lambda i: (i, 0, 0))] * 2
     return pl.pallas_call(
-        functools.partial(grad_kernel, names, lefts, rights),
+        functools.partial(grad_kernel, groups, lefts, rights),
         grid=(breadth // tile,),
-        out_shape=(shape,) * copies,
+        out_shape=tuple(shapes),
         in_specs=[pl.BlockSpec(memory_space=pltpu.SMEM)]
         + [pl.BlockSpec((height, depth), lambda i: (0, 0))] * len(lefts)
         + [pl.BlockSpec((depth, tile), lambda i: (0, i))] * len(rights),
-        out_specs=(out,) * copies,
+        out_specs=tuple(outs),
         compiler_params=pltpu.CompilerParams(vmem_limit_bytes=40 * 2**20),
-        cost_estimate=pl.CostEstimate(
-            flops=2**20,
-            bytes_accessed=2**10,
-            transcendentals=0,
-        ),
+        cost_estimate=pl.CostEstimate(flops=2**20, bytes_accessed=moved, transcendentals=0),
     )(core.reshape(1), *[left_arrays[n] for n in lefts], *[right_arrays[n] for n in rights])
 
 
-def project_kernel(scale_ref, *refs):
-    left_refs, (quant_ref, quant_other_ref), out_refs = refs[:NY], refs[NY : NY + 2], refs[NY + 2 :]
+def project_kernel(*refs):
+    left_refs, right_refs, out_refs = refs[: NY + 1], refs[NY + 1 : NY + 3], refs[NY + 3 :]
     tile, _, _, count, _ = left_refs[0].shape
     rows = tile * 2 * count
-    total = jnp.zeros((rows, 2 * QB), F32)
-    for k in range(NY):
-        for j, quant in enumerate((quant_ref, quant_other_ref)):
-            right = jnp.concatenate([quant[k, 0], quant[k, 1]], axis=1)
-            product = jnp.dot(
-                left_refs[k][:, :, j].reshape(rows, QB), right, preferred_element_type=F32
-            )
-            total = total + product * scale_ref[2 * k + j : 2 * k + j + 1, :]
+    lower = pl.program_id(0) < pl.num_programs(0) // 2
+    total = 0.0
+    for j, right in enumerate(right_refs):
+        left = [left_ref[:, :, j].reshape(rows, QB) for left_ref in left_refs]
+        left[2:4] = [jnp.where(lower, left[2], left[3])]
+        left = jnp.concatenate(left, axis=1)
+        total = total + jnp.dot(left, right[...], preferred_element_type=F32)
     total = total.reshape(tile, 2, count, 2 * QB)
     for w in range(2):
         for v in range(2):
@@ -167,17 +162,21 @@
             )
 
 
-def project(lefts, quantized, quantized_other, scales):
-    tile = 2
+def project(lefts, right, right_other):
+    tile = 4
     count = lefts[0].shape[3]
-    whole = pl.BlockSpec(quantized.shape, lambda i: (0, 0, 0, 0))
+    whole = pl.BlockSpec(right.shape, lambda i: (0, 0))
     shape = (NZ, count, QB)
+    steps = NZ // tile
+    block = (tile, 2, 2, count, QB)
+    whole_row = pl.BlockSpec(block, lambda i: (i, 0, 0, 0, 0))
+    low_half = pl.BlockSpec(block, lambda i: (jnp.minimum(i, steps // 2 - 1), 0, 0, 0, 0))
+    high_half = pl.BlockSpec(block, lambda i: (jnp.maximum(i - steps // 2, 0), 0, 0, 0, 0))
     return pl.pallas_call(
         project_kernel,
         grid=(NZ // tile,),
         out_shape=(jax.ShapeDtypeStruct(shape, F32),) + (jax.ShapeDtypeStruct(shape, BF16),) * 3,
-        in_specs=[pl.BlockSpec(scales.shape, lambda i: (0, 0))]
-        + [pl.BlockSpec((tile, 2, 2, count, QB), lambda i: (i, 0, 0, 0, 0))] * NY
+        in_specs=[whole_row, whole_row, low_half, high_half, whole_row]
         + [whole, whole],
         out_specs=(pl.BlockSpec((tile, count, QB), lambda i: (i, 0, 0)),) * 4,
         cost_estimate=pl.CostEstimate(
@@ -185,7 +184,7 @@
             bytes_accessed=4 * 2**20,
             transcendentals=0,
         ),
-    )(scales, *lefts, quantized, quantized_other)
+    )(*lefts, right, right_other)
 
 
 def gather_y(x):
@@ -253,14 +252,15 @@
     )
     everyone = lax.all_gather(payload, "z", axis=0, tiled=False)
 
-    early = [(0, 0), (1, 0)]
-    late = [(2, 0), (3, 0)] + [(k, 1) for k in range(NY)]
-    outs = grad_parts(core, early, acts, (after(cotangent, payload),), 1)
+    early = [[(0, 0)], [(1, 0)]]
+    late = [[(2, 0), (3, 0), (0, 1)], [(1, 1), (2, 1), (3, 1)]]
+    outs = grad_parts(core, early, acts, (after(cotangent, payload),), 2**10)
     pieces = add_cores(outs)
     cot_other = after(cot_other, *pieces)
-    outs = grad_parts(core, late, acts, (cotangent, cot_other), 3)
+    outs = grad_parts(core, late, acts, (cotangent, cot_other), 2**10)
     part = jnp.concatenate(add_cores(outs), axis=1)
     part = after(part, everyone)
+    early, late = [(0, 0), (1, 0)], late[0] + late[1]
     late_part = lax.psum_scatter(part, "z", scatter_dimension=0, tiled=False)
 
     blocks = lax.dynamic_slice_in_dim(everyone, z * QB, QB, axis=1).reshape(NY, 2, QB, QB)
@@ -282,7 +282,7 @@
     far_a = shift(down[: NZ // 2], "y", NY, 1)
     far_b = shift(up[NZ // 2 :], "y", NY, -1)
     early_part = z_last(pieces, z, *lax.optimization_barrier((*ways, down, up))[:2])
-    lefts = (own, down, jnp.concatenate([far_a, far_b], axis=0), up)
+    lefts = (own, down, far_a, far_b, up)
 
     sums = {}
     for names, part in ((early, early_part), (late, late_part)):
@@ -298,11 +298,10 @@
     largest = jnp.max(jnp.abs(updated), axis=(2, 3))
     scales = ((largest + epsilon) / scale_limit).astype(BF16)
     quantized = (updated / scales.astype(F32)[:, :, None, None]).astype(BF16)
-    quantized_other, scales_other = swap(quantized, "c"), swap(scales, "c")
-
-    both = jnp.stack([scales, scales_other], axis=1).astype(F32).reshape(2 * NY, 2, 1)
-    both = jnp.broadcast_to(both, (2 * NY, 2, QB)).reshape(2 * NY, 2 * QB)
-    mine, to_lo, to_hi, to_both = project(lefts, quantized, quantized_other, both)
+    right = (quantized.astype(F32) * scales.astype(F32)[:, :, None, None]).astype(BF16)
+    right = right.transpose(0, 2, 1, 3).reshape(NY * QB, 2 * QB)
+
+    mine, to_lo, to_hi, to_both = project(lefts, right, swap(right, "c"))
     out = (
         mine
         + swap(to_lo, "xl").astype(F32)
@@ -310,7 +309,7 @@
         + lax.ppermute(to_both, ("xh", "xl"), [(i, 3 - i) for i in range(4)]).astype(F32)
     ).astype(BF16)
 
-    blocks = grad.astype(BF16)
+    blocks = after(grad.astype(BF16), mine)
     blocks = jnp.stack([pick(blocks, (y - k) % NY) for k in range(NY)], axis=0)
     kept, got = blocks[:, 0], swap(blocks[:, 1], "xl")
     first = jnp.where(xl == 0, kept, got)

time: 191 us -> 189 us (0.990)
  waiting for transfers between devices: 60.3 us -> 62.3 us
    ppermute x14 -> x13, waiting for transfers between devices: 18.7 us -> 23.3 us  [swap(): return lax.ppermute(x, axis, [(0, 1), (1, 0)])]
    ppermute x1, waiting for transfers between devices: 2.51 us -> 0.01 us  [per_device(): lax.ppermute(to_both, ('xh', 'xl'), [(i, 3 - i) for i in range(4)])]
    ppermute x14 -> x13, starting transfers between devices: 19.2 us -> 19 us  [swap(): return lax.ppermute(x, axis, [(0, 1), (1, 0)])]
  transfers between devices with their start and end apart: 33 -> 32, of which waited for: 18 -> 18; matrix products, arithmetic and copies ran while one was open for 10% -> 10% of each run, Pallas kernels for 14% -> 12%
where the time goes in v2:
time: 189 us; the launch traced here: 187 us
  waiting for transfers between devices  62.3 us (33%)
  starting transfers between devices  46.5 us (25%)
  Pallas kernels  25.3 us (13%)
  blocking collectives  16.1 us (9%)
  between operations  14.7 us (8%)
  local copies, waits for them, and re-layouts  14.6 us (8%)
  other arithmetic  7.88 us (4%)
    ppermute x16, waiting for transfers between devices, shift(): return lax.ppermute(x, axis, [(i, (i + step) % size) for i in range(size)])  33.4 us
    ppermute x16, starting transfers between devices, shift(): return lax.ppermute(x, axis, [(i, (i + step) % size) for i in range(size)])  26.1 us
    ppermute x13, waiting for transfers between devices, swap(): return lax.ppermute(x, axis, [(0, 1), (1, 0)])  23.3 us
    ppermute x13, starting transfers between devices, swap(): return lax.ppermute(x, axis, [(0, 1), (1, 0)])  19 us
    all_to_all x1, blocking collectives, per_device(): blocks = lax.all_to_all(blocks, 'z', 0, 0, tiled=True).transpose(1, 0, 2)  16.1 us
    pallas_call x2, Pallas kernels, grad_parts(): pl.pallas_call(functools.partial(grad_kernel, groups, lefts, rights), gri...  13.6 us
    pallas_call x1, Pallas kernels, make_payload(): pl.pallas_call(functools.partial(payload_kernel, steps), grid=(rows // ti...  8.42 us
    reduce_scatter x1, waiting for transfers between devices, per_device(): late_part = lax.psum_scatter(part, 'z', scatter_dimension=0, tiled=False)  5.59 us
  transfers between devices with their start and end apart: 32, of which 18 were waited for; matrix products, arithmetic and copies ran while one was open for 10% of the time, Pallas kernels for 12%

profile of v2, /device:TPU:1, one launch (start us, length us, event | category | flops | bytes accessed | tf_op | source)
XLA Modules:
  0.0 187.5 jit_solution(157083124283292503)
XLA Ops:
  8.9 2.2 %collective-permute-start = (bf16[512,1024]{1,0:T(8,128)(2,1)S(1)}, bf16[512,1024]{1,0:T(8,128)(2,1)}, u32[]{:S(2)}, u32[]{:S(2)}) collective-permute-start(bf16[512,1024]{1,0:T(8,128)(2,1)S(1)} %bitcast.102), channel_id=1, source_target_pairs={{0,2},{2,4},{4,6},{6,0},{1,3},{3,5},{5,7},{7,1},{8,10},{10,12},{12... | collective-permute-start | bytes 3145736 | tf_op jit(solution)/shard_map/ppermute | solution.py:24
  16.6 8.4 %shard_map.104 = bf16[1280,128]{1,0:T(8,128)(2,1)} custom-call(s32[16]{0:T(128)} %len_ref.1, bf16[16,16,128]{2,1,0:T(8,128)(2,1)} %bitcast.124, bf16[16,16,128]{2,1,0:T(8,128)(2,1)} %pad.7.nk_ref, bf16[16,16,128]{2,1,0:T(8,128)(2,1)} %pad.8.nv_ref, bf16[16,512,128]{2,1,0:T(8,128)(2,1)} %bitcast.127, bf16[16,512,128]{2,1,0:T(8,128)(2,1)} %bitcast.128, ...), custom_call_target="tpu_custom_call" | custom-call | flops 17179869184 | bytes 4194304 | tf_op jit(solution)/shard_map/pallas_call | solution.py:89
  25.1 8.4 %collective-permute-done.refs_1_ = bf16[512,1024]{1,0:T(8,128)(2,1)} collective-permute-done((bf16[512,1024]{1,0:T(8,128)(2,1)S(1)}, bf16[512,1024]{1,0:T(8,128)(2,1)}, u32[]{:S(2)}, u32[]{:S(2)}) %collective-permute-start) | collective-permute-done | bytes 1048608 | tf_op jit(solution)/shard_map/ppermute | solution.py:24
  33.5 1.9 %slice.89 = bf16[256,1024]{1,0:T(8,128)(2,1)} slice(bf16[512,1024]{1,0:T(8,128)(2,1)} %collective-permute-done.refs_1_), slice={[0:256], [0:1024]} | slice | bytes 1048576 | tf_op jit(solution)/shard_map/slice | solution.py:194
  37.0 1.9 slice.90
  40.5 4.4 %shard_map.105 = (bf16[8,256,128]{2,1,0:T(8,128)(2,1)S(1)}, bf16[8,256,128]{2,1,0:T(8,128)(2,1)S(1)}, bf16[8,256,128]{2,1,0:T(8,128)(2,1)S(1)}, bf16[8,256,128]{2,1,0:T(8,128)(2,1)S(1)}) custom-call(s32[1]{0:T(128)} %bitcast.10.core_ref, bf16[512,1024]{1,0:T(8,128)(2,1)S(1)} %bitcast.104, bf16[512,1024]{1,0:T(8,128)(2,1)} %collective-permute-done.refs_1_, ...), custom_call_target="tpu_custom_call" | custom-call | flops 1048576 | bytes 1024 | tf_op jit(solution)/shard_map/pallas_call | solution.py:133
  44.8 3.4 %collective-permute-start.6 = (bf16[8,256,128]{2,1,0:T(8,128)(2,1)S(1)}, bf16[8,256,128]{2,1,0:T(8,128)(2,1)S(1)}, u32[]{:S(2)}, u32[]{:S(2)}) collective-permute-start(bf16[8,256,128]{2,1,0:T(8,128)(2,1)S(1)} %get-tuple-element.30), channel_id=1, source_target_pairs={{0,8},{8,0},{1,9},{9,1},{2,10},{10,2},{3,11},{11,3},{4,12},{12,4},... | collective-permute-start | bytes 1572872 | tf_op jit(solution)/shard_map/ppermute | solution.py:28
  48.4 2.2 %collective-permute-done.3 = bf16[256,1024]{1,0:T(8,128)(2,1)} collective-permute-done((bf16[256,1024]{1,0:T(8,128)(2,1)}, bf16[256,1024]{1,0:T(8,128)(2,1)}, u32[]{:S(2)}, u32[]{:S(2)}) %collective-permute-start.3) | collective-permute-done | bytes 524320 | tf_op jit(solution)/shard_map/ppermute | solution.py:24
  53.7 3.7 %collective-permute-done.4.refs_5_ = bf16[1024,1024]{1,0:T(8,128)(2,1)} collective-permute-done((bf16[1024,1024]{1,0:T(8,128)(2,1)S(1)}, bf16[1024,1024]{1,0:T(8,128)(2,1)}, u32[]{:S(2)}, u32[]{:S(2)}) %collective-permute-start.4) | collective-permute-done | bytes 2097184 | tf_op jit(solution)/shard_map/ppermute | solution.py:28
  57.4 9.3 %shard_map.106 = (bf16[8,768,128]{2,1,0:T(8,128)(2,1)S(1)}, bf16[8,768,128]{2,1,0:T(8,128)(2,1)S(1)}, bf16[8,768,128]{2,1,0:T(8,128)(2,1)S(1)}, bf16[8,768,128]{2,1,0:T(8,128)(2,1)S(1)}) custom-call(s32[1]{0:T(128)} %bitcast.10.core_ref, bf16[512,1024]{1,0:T(8,128)(2,1)S(1)} %bitcast.105, bf16[512,1024]{1,0:T(8,128)(2,1)} %collective-permute-done.refs_1_, ...), custom_call_target="tpu_custom_call" | custom-call | flops 1048576 | bytes 1024 | tf_op jit(solution)/shard_map/pallas_call | solution.py:133
  66.7 3.5 %collective-permute-start.7 = (bf16[8,768,128]{2,1,0:T(8,128)(2,1)S(1)}, bf16[8,768,128]{2,1,0:T(8,128)(2,1)S(1)}, u32[]{:S(2)}, u32[]{:S(2)}) collective-permute-start(bf16[8,768,128]{2,1,0:T(8,128)(2,1)S(1)} %get-tuple-element.33), channel_id=1, source_target_pairs={{0,8},{8,0},{1,9},{9,1},{2,10},{10,2},{3,11},{11,3},{4,12},{12,4},... | collective-permute-start | bytes 4718600 | tf_op jit(solution)/shard_map/ppermute | solution.py:28
  70.2 2.9 %collective-permute-done.7 = bf16[8,768,128]{2,1,0:T(8,128)(2,1)S(1)} collective-permute-done((bf16[8,768,128]{2,1,0:T(8,128)(2,1)S(1)}, bf16[8,768,128]{2,1,0:T(8,128)(2,1)S(1)}, u32[]{:S(2)}, u32[]{:S(2)}) %collective-permute-start.7) | collective-permute-done | bytes 1572896 | tf_op jit(solution)/shard_map/ppermute | solution.py:28
  73.6 1.8 collective-permute-done.8
  75.8 1.9 pad_maximum_fusion
  79.1 2.8 %collective-permute-start.9 = (bf16[8,2,64,128]{3,2,1,0:T(8,128)(2,1)S(1)}, bf16[8,2,64,128]{3,2,1,0:T(8,128)(2,1)S(1)}, u32[]{:S(2)}, u32[]{:S(2)}) collective-permute-start(bf16[8,2,64,128]{3,2,1,0:T(8,128)(2,1)S(1)} %get-tuple-element.37), channel_id=1, source_target_pairs={{0,16},{16,0},{1,17},{17,1},{2,18},{18,2},{3,19},{19,3},{4,20},{20... | collective-permute-start | bytes 786440 | tf_op jit(solution)/shard_map/ppermute | solution.py:28
  82.0 5.8 %collective-permute-start.17 = (bf16[256,128]{1,0:T(8,128)(2,1)S(1)}, bf16[256,128]{1,0:T(8,128)(2,1)S(1)}, u32[]{:S(2)}, u32[]{:S(2)}) collective-permute-start(bf16[256,128]{1,0:T(8,128)(2,1)S(1)} %get-tuple-element.61), channel_id=1, source_target_pairs={{0,224},{32,0},{64,32},{96,64},{128,96},{160,128},{192,160},{224,1... | collective-permute-start | bytes 196616 | tf_op jit(solution)/shard_map/ppermute | solution.py:24
  89.2 3.4 %collective-permute-start.18 = (bf16[512,128]{1,0:T(8,128)(2,1)S(1)}, bf16[512,128]{1,0:T(8,128)(2,1)S(1)}, u32[]{:S(2)}, u32[]{:S(2)}) collective-permute-start(bf16[512,128]{1,0:T(8,128)(2,1)S(1)} %pad_maximum_fusion.9), channel_id=1, source_target_pairs={{0,224},{32,0},{64,32},{96,64},{128,96},{160,128},{192,160},{224,1... | collective-permute-start | bytes 393224 | tf_op jit(solution)/shard_map/ppermute | solution.py:24
  92.7 4.1 %collective-permute-done.18 = bf16[512,128]{1,0:T(8,128)(2,1)S(1)} collective-permute-done((bf16[512,128]{1,0:T(8,128)(2,1)S(1)}, bf16[512,128]{1,0:T(8,128)(2,1)S(1)}, u32[]{:S(2)}, u32[]{:S(2)}) %collective-permute-start.18) | collective-permute-done | bytes 131104 | tf_op jit(solution)/shard_map/ppermute | solution.py:24
  96.9 4.7 %collective-permute-done.16 = bf16[512,128]{1,0:T(8,128)(2,1)S(1)} collective-permute-done((bf16[512,128]{1,0:T(8,128)(2,1)S(1)}, bf16[512,128]{1,0:T(8,128)(2,1)S(1)}, u32[]{:S(2)}, u32[]{:S(2)}) %collective-permute-start.16) | collective-permute-done | bytes 131104 | tf_op jit(solution)/shard_map/ppermute | solution.py:24
  101.9 2.7 %collective-permute-start.12 = (bf16[8,2,2,64,128]{4,3,2,1,0:T(8,128)(2,1)S(1)}, bf16[8,2,2,64,128]{4,3,2,1,0:T(8,128)(2,1)S(1)}, u32[]{:S(2)}, u32[]{:S(2)}) collective-permute-start(bf16[8,2,2,64,128]{4,3,2,1,0:T(8,128)(2,1)S(1)} %pad_maximum_fusion.2.refs_0_), channel_id=1, source_target_pairs={{0,6},{2,0},{4,2},{6,4},{1,7},{3,1},{5,3},{7,5},{8,14},{10,8},{12,... | collective-permute-start | bytes 1572872 | tf_op jit(solution)/shard_map/ppermute | solution.py:24
  105.9 3.4 %collective-permute-done.20 = bf16[512,128]{1,0:T(8,128)(2,1)S(1)} collective-permute-done((bf16[512,128]{1,0:T(8,128)(2,1)S(1)}, bf16[512,128]{1,0:T(8,128)(2,1)S(1)}, u32[]{:S(2)}, u32[]{:S(2)}) %collective-permute-start.20) | collective-permute-done | bytes 131104 | tf_op jit(solution)/shard_map/ppermute | solution.py:24
  109.4 3.7 %collective-permute-done.19 = bf16[512,128]{1,0:T(8,128)(2,1)S(1)} collective-permute-done((bf16[512,128]{1,0:T(8,128)(2,1)S(1)}, bf16[512,128]{1,0:T(8,128)(2,1)S(1)}, u32[]{:S(2)}, u32[]{:S(2)}) %collective-permute-start.19) | collective-permute-done | bytes 131104 | tf_op jit(solution)/shard_map/ppermute | solution.py:24
  117.9 4.7 %collective-permute-done.21 = bf16[512,128]{1,0:T(8,128)(2,1)S(1)} collective-permute-done((bf16[512,128]{1,0:T(8,128)(2,1)S(1)}, bf16[512,128]{1,0:T(8,128)(2,1)S(1)}, u32[]{:S(2)}, u32[]{:S(2)}) %collective-permute-start.21) | collective-permute-done | bytes 131104 | tf_op jit(solution)/shard_map/ppermute | solution.py:24
  123.1 2.7 %collective-permute-start.13 = (bf16[4,2,2,64,128]{4,3,2,1,0:T(8,128)(2,1)S(1)}, bf16[4,2,2,64,128]{4,3,2,1,0:T(8,128)(2,1)S(1)}, u32[]{:S(2)}, u32[]{:S(2)}) collective-permute-start(bf16[4,2,2,64,128]{4,3,2,1,0:T(8,128)(2,1)S(1)} %slice.92), channel_id=1, source_target_pairs={{0,6},{2,0},{4,2},{6,4},{1,7},{3,1},{5,3},{7,5},{8,14},{10,8},{12,... | collective-permute-start | bytes 786440 | tf_op jit(solution)/shard_map/ppermute | solution.py:24
  127.5 5.6 %reduce-scatter.2.cloned.1.call-done = bf16[1,1536,128]{2,1,0:T(8,128)(2,1)} async-done(((bf16[8,1536,128]{2,1,0:T(8,128)(2,1)}), bf16[1,1536,128]{2,1,0:T(8,128)(2,1)}) %reduce-scatter.2.cloned.1.call-update) | async-done | bytes 393232 | tf_op jit(solution)/shard_map/reduce_scatter | solution.py:264
  134.0 2.3 %collective-permute-start.24 = (bf16[6,128,128]{2,1,0:T(8,128)(2,1)S(1)}, bf16[6,128,128]{2,1,0:T(8,128)(2,1)S(1)}, u32[]{:S(2)}, u32[]{:S(2)}) collective-permute-start(bf16[6,128,128]{2,1,0:T(8,128)(2,1)S(1)} %dynamic-slice_bitcast_fusion), channel_id=1, source_target_pairs={{0,16},{16,0},{1,17},{17,1},{2,18},{18,2},{3,19},{19,3},{4,20},{20... | collective-permute-start | bytes 589832 | tf_op jit(solution)/shard_map/ppermute | solution.py:28
  136.3 5.2 %collective-permute-done.24 = bf16[6,128,128]{2,1,0:T(8,128)(2,1)S(1)} collective-permute-done((bf16[6,128,128]{2,1,0:T(8,128)(2,1)S(1)}, bf16[6,128,128]{2,1,0:T(8,128)(2,1)S(1)}, u32[]{:S(2)}, u32[]{:S(2)}) %collective-permute-start.24) | collective-permute-done | bytes 196640 | tf_op jit(solution)/shard_map/ppermute | solution.py:28
  146.8 3.2 %shard_map.107 = (f32[8,64,128]{2,1,0:T(8,128)}, bf16[8,64,128]{2,1,0:T(8,128)(2,1)}, bf16[8,64,128]{2,1,0:T(8,128)(2,1)}, bf16[8,64,128]{2,1,0:T(8,128)(2,1)}) custom-call(bf16[8,2,2,64,128]{4,3,2,1,0:T(8,128)(2,1)} %copy-done.3, bf16[8,2,2,64,128]{4,3,2,1,0:T(8,128)(2,1)} %copy-done.4, bf16[4,2,2,64,128]{4,3,2,1,0:T(8,128)(2,1)} %copy-done.7, ...), custom_call_target="tpu_custom_call" | custom-call | flops 536870912 | bytes 4194304 | tf_op jit(solution)/shard_map/pallas_call | solution.py:175
  151.7 2.2 %collective-permute-start.27 = (bf16[8,64,128]{2,1,0:T(8,128)(2,1)}, bf16[8,64,128]{2,1,0:T(8,128)(2,1)S(1)}, u32[]{:S(2)}, u32[]{:S(2)}) collective-permute-start(bf16[8,64,128]{2,1,0:T(8,128)(2,1)} %get-tuple-element.47), channel_id=1, source_target_pairs={{0,16},{16,0},{1,17},{17,1},{2,18},{18,2},{3,19},{19,3},{4,20},{20... | collective-permute-start | bytes 393224 | tf_op jit(solution)/shard_map/ppermute | solution.py:28
  155.4 2.4 %collective-permute-done.26 = bf16[8,64,128]{2,1,0:T(8,128)(2,1)S(1)} collective-permute-done((bf16[8,64,128]{2,1,0:T(8,128)(2,1)}, bf16[8,64,128]{2,1,0:T(8,128)(2,1)S(1)}, u32[]{:S(2)}, u32[]{:S(2)}) %collective-permute-start.26) | collective-permute-done | bytes 131104 | tf_op jit(solution)/shard_map/ppermute | solution.py:28
  157.8 4.6 %collective-permute-done.27 = bf16[8,64,128]{2,1,0:T(8,128)(2,1)S(1)} collective-permute-done((bf16[8,64,128]{2,1,0:T(8,128)(2,1)}, bf16[8,64,128]{2,1,0:T(8,128)(2,1)S(1)}, u32[]{:S(2)}, u32[]{:S(2)}) %collective-permute-start.27) | collective-permute-done | bytes 131104 | tf_op jit(solution)/shard_map/ppermute | solution.py:28
  162.4 16.1 %all_to_all.5 = bf16[8,192,128]{2,1,0:T(8,128)(2,1)S(1)} all-to-all(bf16[8,192,128]{2,1,0:T(8,128)(2,1)S(1)} %pad_maximum_fusion.4), channel_id=1, replica_groups=mesh['z'=8,'xh'=2,'c'=2,'y'=4,'xl'=2] {'z'}, dimensions={0} | all-to-all | bytes 786432 | tf_op jit(solution)/shard_map/all_to_all | solution.py:319
  (125 shorter events, 37.3 us)
Async XLA Ops:
  7.2 70.5 %all-gather.3.cloned.1.call-start = ((), (), s32[]{:S(2)}) async-start(), calls=%async_computation.3 | async-start | bytes 2949120 | tf_op jit(solution)/shard_map/all_gather | solution.py:253
  8.9 24.6 %collective-permute-start = (bf16[512,1024]{1,0:T(8,128)(2,1)S(1)}, bf16[512,1024]{1,0:T(8,128)(2,1)}, u32[]{:S(2)}, u32[]{:S(2)}) collective-permute-start(bf16[512,1024]{1,0:T(8,128)(2,1)S(1)} %bitcast.102), channel_id=1, source_target_pairs={{0,2},{2,4},{4,6},{6,0},{1,3},{3,5},{5,7},{7,1},{8,10},{10,12},{12... | collective-permute-start | bytes 3145736 | tf_op jit(solution)/shard_map/ppermute | solution.py:24
  11.1 25.9 %collective-permute-start.2 = (bf16[512,1024]{1,0:T(8,128)(2,1)S(1)}, bf16[512,1024]{1,0:T(8,128)(2,1)}, u32[]{:S(2)}, u32[]{:S(2)}) collective-permute-start(bf16[512,1024]{1,0:T(8,128)(2,1)S(1)} %bitcast.103), channel_id=1, source_target_pairs={{0,6},{2,0},{4,2},{6,4},{1,7},{3,1},{5,3},{7,5},{8,14},{10,8},{12,... | collective-permute-start | bytes 3145736 | tf_op jit(solution)/shard_map/ppermute | solution.py:24
  12.6 44.8 %collective-permute-start.4 = (bf16[1024,1024]{1,0:T(8,128)(2,1)S(1)}, bf16[1024,1024]{1,0:T(8,128)(2,1)}, u32[]{:S(2)}, u32[]{:S(2)}) collective-permute-start(bf16[1024,1024]{1,0:T(8,128)(2,1)S(1)} %copy-done), channel_id=1, source_target_pairs={{0,1},{1,0},{2,3},{3,2},{4,5},{5,4},{6,7},{7,6},{8,9},{9,8},{10,11... | collective-permute-start | bytes 6291464 | tf_op jit(solution)/shard_map/ppermute | solution.py:28
  25.0 108.0 %reduce-scatter.2.cloned.1.call-start = ((), (), s32[]{:S(2)}) async-start(), calls=%async_computation.2 | async-start | bytes 3538944 | tf_op jit(solution)/shard_map/reduce_scatter | solution.py:264
  35.4 12.9 %collective-permute-start.1 = (bf16[256,1024]{1,0:T(8,128)(2,1)}, bf16[256,1024]{1,0:T(8,128)(2,1)}, u32[]{:S(2)}, u32[]{:S(2)}) collective-permute-start(bf16[256,1024]{1,0:T(8,128)(2,1)} %slice.89), channel_id=1, source_target_pairs={{0,2},{2,4},{4,6},{6,0},{1,3},{3,5},{5,7},{7,1},{8,10},{10,12},{12... | collective-permute-start | bytes 1572872 | tf_op jit(solution)/shard_map/ppermute | solution.py:24
  38.8 11.7 %collective-permute-start.3 = (bf16[256,1024]{1,0:T(8,128)(2,1)}, bf16[256,1024]{1,0:T(8,128)(2,1)}, u32[]{:S(2)}, u32[]{:S(2)}) collective-permute-start(bf16[256,1024]{1,0:T(8,128)(2,1)} %slice.90), channel_id=1, source_target_pairs={{0,6},{2,0},{4,2},{6,4},{1,7},{3,1},{5,3},{7,5},{8,14},{10,8},{12,... | collective-permute-start | bytes 1572872 | tf_op jit(solution)/shard_map/ppermute | solution.py:24
  44.8 7.0 %collective-permute-start.6 = (bf16[8,256,128]{2,1,0:T(8,128)(2,1)S(1)}, bf16[8,256,128]{2,1,0:T(8,128)(2,1)S(1)}, u32[]{:S(2)}, u32[]{:S(2)}) collective-permute-start(bf16[8,256,128]{2,1,0:T(8,128)(2,1)S(1)} %get-tuple-element.30), channel_id=1, source_target_pairs={{0,8},{8,0},{1,9},{9,1},{2,10},{10,2},{3,11},{11,3},{4,12},{12,4},... | collective-permute-start | bytes 1572872 | tf_op jit(solution)/shard_map/ppermute | solution.py:28
  48.2 4.5 %collective-permute-start.5 = (bf16[8,256,128]{2,1,0:T(8,128)(2,1)S(1)}, bf16[8,256,128]{2,1,0:T(8,128)(2,1)S(1)}, u32[]{:S(2)}, u32[]{:S(2)}) collective-permute-start(bf16[8,256,128]{2,1,0:T(8,128)(2,1)S(1)} %get-tuple-element.28), channel_id=1, source_target_pairs={{0,8},{8,0},{1,9},{9,1},{2,10},{10,2},{3,11},{11,3},{4,12},{12,4},... | collective-permute-start | bytes 1572872 | tf_op jit(solution)/shard_map/ppermute | solution.py:28
  66.7 6.5 %collective-permute-start.7 = (bf16[8,768,128]{2,1,0:T(8,128)(2,1)S(1)}, bf16[8,768,128]{2,1,0:T(8,128)(2,1)S(1)}, u32[]{:S(2)}, u32[]{:S(2)}) collective-permute-start(bf16[8,768,128]{2,1,0:T(8,128)(2,1)S(1)} %get-tuple-element.33), channel_id=1, source_target_pairs={{0,8},{8,0},{1,9},{9,1},{2,10},{10,2},{3,11},{11,3},{4,12},{12,4},... | collective-permute-start | bytes 4718600 | tf_op jit(solution)/shard_map/ppermute | solution.py:28
  70.1 5.3 %collective-permute-start.8 = (bf16[8,768,128]{2,1,0:T(8,128)(2,1)S(1)}, bf16[8,768,128]{2,1,0:T(8,128)(2,1)S(1)}, u32[]{:S(2)}, u32[]{:S(2)}) collective-permute-start(bf16[8,768,128]{2,1,0:T(8,128)(2,1)S(1)} %get-tuple-element.35), channel_id=1, source_target_pairs={{0,8},{8,0},{1,9},{9,1},{2,10},{10,2},{3,11},{11,3},{4,12},{12,4},... | collective-permute-start | bytes 4718600 | tf_op jit(solution)/shard_map/ppermute | solution.py:28
  79.1 22.5 %collective-permute-start.9 = (bf16[8,2,64,128]{3,2,1,0:T(8,128)(2,1)S(1)}, bf16[8,2,64,128]{3,2,1,0:T(8,128)(2,1)S(1)}, u32[]{:S(2)}, u32[]{:S(2)}) collective-permute-start(bf16[8,2,64,128]{3,2,1,0:T(8,128)(2,1)S(1)} %get-tuple-element.37), channel_id=1, source_target_pairs={{0,16},{16,0},{1,17},{17,1},{2,18},{18,2},{3,19},{19,3},{4,20},{20... | collective-permute-start | bytes 786440 | tf_op jit(solution)/shard_map/ppermute | solution.py:28
  82.0 7.2 %collective-permute-start.17 = (bf16[256,128]{1,0:T(8,128)(2,1)S(1)}, bf16[256,128]{1,0:T(8,128)(2,1)S(1)}, u32[]{:S(2)}, u32[]{:S(2)}) collective-permute-start(bf16[256,128]{1,0:T(8,128)(2,1)S(1)} %get-tuple-element.61), channel_id=1, source_target_pairs={{0,224},{32,0},{64,32},{96,64},{128,96},{160,128},{192,160},{224,1... | collective-permute-start | bytes 196616 | tf_op jit(solution)/shard_map/ppermute | solution.py:24
  87.9 4.7 %collective-permute-start.15 = (bf16[256,128]{1,0:T(8,128)(2,1)S(1)}, bf16[256,128]{1,0:T(8,128)(2,1)S(1)}, u32[]{:S(2)}, u32[]{:S(2)}) collective-permute-start(bf16[256,128]{1,0:T(8,128)(2,1)S(1)} %get-tuple-element.56), channel_id=1, source_target_pairs={{0,32},{32,64},{64,96},{96,128},{128,160},{160,192},{192,224},{224... | collective-permute-start | bytes 196616 | tf_op jit(solution)/shard_map/ppermute | solution.py:24
  89.2 7.6 %collective-permute-start.18 = (bf16[512,128]{1,0:T(8,128)(2,1)S(1)}, bf16[512,128]{1,0:T(8,128)(2,1)S(1)}, u32[]{:S(2)}, u32[]{:S(2)}) collective-permute-start(bf16[512,128]{1,0:T(8,128)(2,1)S(1)} %pad_maximum_fusion.9), channel_id=1, source_target_pairs={{0,224},{32,0},{64,32},{96,64},{128,96},{160,128},{192,160},{224,1... | collective-permute-start | bytes 393224 | tf_op jit(solution)/shard_map/ppermute | solution.py:24
  92.6 8.9 %collective-permute-start.16 = (bf16[512,128]{1,0:T(8,128)(2,1)S(1)}, bf16[512,128]{1,0:T(8,128)(2,1)S(1)}, u32[]{:S(2)}, u32[]{:S(2)}) collective-permute-start(bf16[512,128]{1,0:T(8,128)(2,1)S(1)} %pad_maximum_fusion.8), channel_id=1, source_target_pairs={{0,32},{32,64},{64,96},{96,128},{128,160},{160,192},{192,224},{224... | collective-permute-start | bytes 393224 | tf_op jit(solution)/shard_map/ppermute | solution.py:24
  101.7 7.7 %collective-permute-start.20 = (bf16[512,128]{1,0:T(8,128)(2,1)S(1)}, bf16[512,128]{1,0:T(8,128)(2,1)S(1)}, u32[]{:S(2)}, u32[]{:S(2)}) collective-permute-start(bf16[512,128]{1,0:T(8,128)(2,1)S(1)} %add_convert_fusion.7), channel_id=1, source_target_pairs={{0,224},{32,0},{64,32},{96,64},{128,96},{160,128},{192,160},{224,1... | collective-permute-start | bytes 393224 | tf_op jit(solution)/shard_map/ppermute | solution.py:24
  101.8 12.3 %collective-permute-start.10 = (bf16[8,2,2,64,128]{4,3,2,1,0:T(8,128)(2,1)S(1)}, bf16[8,2,2,64,128]{4,3,2,1,0:T(8,128)(2,1)S(1)}, u32[]{:S(2)}, u32[]{:S(2)}) collective-permute-start(bf16[8,2,2,64,128]{4,3,2,1,0:T(8,128)(2,1)S(1)} %pad_maximum_fusion.2.refs_0_), channel_id=1, source_target_pairs={{0,2},{2,4},{4,6},{6,0},{1,3},{3,5},{5,7},{7,1},{8,10},{10,12},{12... | collective-permute-start | bytes 1572872 | tf_op jit(solution)/shard_map/ppermute | solution.py:24
  101.9 12.2 %collective-permute-start.12 = (bf16[8,2,2,64,128]{4,3,2,1,0:T(8,128)(2,1)S(1)}, bf16[8,2,2,64,128]{4,3,2,1,0:T(8,128)(2,1)S(1)}, u32[]{:S(2)}, u32[]{:S(2)}) collective-permute-start(bf16[8,2,2,64,128]{4,3,2,1,0:T(8,128)(2,1)S(1)} %pad_maximum_fusion.2.refs_0_), channel_id=1, source_target_pairs={{0,6},{2,0},{4,2},{6,4},{1,7},{3,1},{5,3},{7,5},{8,14},{10,8},{12,... | collective-permute-start | bytes 1572872 | tf_op jit(solution)/shard_map/ppermute | solution.py:24
  104.5 8.6 %collective-permute-start.19 = (bf16[512,128]{1,0:T(8,128)(2,1)S(1)}, bf16[512,128]{1,0:T(8,128)(2,1)S(1)}, u32[]{:S(2)}, u32[]{:S(2)}) collective-permute-start(bf16[512,128]{1,0:T(8,128)(2,1)S(1)} %add_convert_fusion.8), channel_id=1, source_target_pairs={{0,32},{32,64},{64,96},{96,128},{128,160},{160,192},{192,224},{224... | collective-permute-start | bytes 393224 | tf_op jit(solution)/shard_map/ppermute | solution.py:24
  114.1 8.6 %collective-permute-start.21 = (bf16[512,128]{1,0:T(8,128)(2,1)S(1)}, bf16[512,128]{1,0:T(8,128)(2,1)S(1)}, u32[]{:S(2)}, u32[]{:S(2)}) collective-permute-start(bf16[512,128]{1,0:T(8,128)(2,1)S(1)} %add_convert_fusion.6), channel_id=1, source_target_pairs={{0,32},{32,64},{64,96},{96,128},{128,160},{160,192},{192,224},{224... | collective-permute-start | bytes 393224 | tf_op jit(solution)/shard_map/ppermute | solution.py:24
  115.1 7.5 %collective-permute-start.22 = (bf16[512,128]{1,0:T(8,128)(2,1)S(1)}, bf16[512,128]{1,0:T(8,128)(2,1)S(1)}, u32[]{:S(2)}, u32[]{:S(2)}) collective-permute-start(bf16[512,128]{1,0:T(8,128)(2,1)S(1)} %add_convert_fusion.5), channel_id=1, source_target_pairs={{0,224},{32,0},{64,32},{96,64},{128,96},{160,128},{192,160},{224,1... | collective-permute-start | bytes 393224 | tf_op jit(solution)/shard_map/ppermute | solution.py:24
  117.8 5.0 %collective-permute-start.14 = (bf16[4,128,128]{2,1,0:T(8,128)(2,1)S(1)}, bf16[4,128,128]{2,1,0:T(8,128)(2,1)S(1)}, u32[]{:S(2)}, u32[]{:S(2)}) collective-permute-start(bf16[4,128,128]{2,1,0:T(8,128)(2,1)S(1)} %get-tuple-element.86), channel_id=1, source_target_pairs={{0,1},{1,0},{2,3},{3,2},{4,5},{5,4},{6,7},{7,6},{8,9},{9,8},{10,11... | collective-permute-start | bytes 393224 | tf_op jit(solution)/shard_map/ppermute | solution.py:28
  122.7 4.7 %collective-permute-start.23 = (bf16[2,128,128]{2,1,0:T(8,128)(2,1)S(1)}, bf16[2,128,128]{2,1,0:T(8,128)(2,1)S(1)}, u32[]{:S(2)}, u32[]{:S(2)}) collective-permute-start(bf16[2,128,128]{2,1,0:T(8,128)(2,1)S(1)} %fusion.7), channel_id=1, source_target_pairs={{0,16},{16,0},{1,17},{17,1},{2,18},{18,2},{3,19},{19,3},{4,20},{20... | collective-permute-start | bytes 196616 | tf_op jit(solution)/shard_map/ppermute | solution.py:28
  122.9 22.1 %collective-permute-start.11 = (bf16[4,2,2,64,128]{4,3,2,1,0:T(8,128)(2,1)S(1)}, bf16[4,2,2,64,128]{4,3,2,1,0:T(8,128)(2,1)S(1)}, u32[]{:S(2)}, u32[]{:S(2)}) collective-permute-start(bf16[4,2,2,64,128]{4,3,2,1,0:T(8,128)(2,1)S(1)} %slice.91), channel_id=1, source_target_pairs={{0,2},{2,4},{4,6},{6,0},{1,3},{3,5},{5,7},{7,1},{8,10},{10,12},{12... | collective-permute-start | bytes 786440 | tf_op jit(solution)/shard_map/ppermute | solution.py:24
  123.1 22.0 %collective-permute-start.13 = (bf16[4,2,2,64,128]{4,3,2,1,0:T(8,128)(2,1)S(1)}, bf16[4,2,2,64,128]{4,3,2,1,0:T(8,128)(2,1)S(1)}, u32[]{:S(2)}, u32[]{:S(2)}) collective-permute-start(bf16[4,2,2,64,128]{4,3,2,1,0:T(8,128)(2,1)S(1)} %slice.92), channel_id=1, source_target_pairs={{0,6},{2,0},{4,2},{6,4},{1,7},{3,1},{5,3},{7,5},{8,14},{10,8},{12,... | collective-permute-start | bytes 786440 | tf_op jit(solution)/shard_map/ppermute | solution.py:24
  134.0 7.4 %collective-permute-start.24 = (bf16[6,128,128]{2,1,0:T(8,128)(2,1)S(1)}, bf16[6,128,128]{2,1,0:T(8,128)(2,1)S(1)}, u32[]{:S(2)}, u32[]{:S(2)}) collective-permute-start(bf16[6,128,128]{2,1,0:T(8,128)(2,1)S(1)} %dynamic-slice_bitcast_fusion), channel_id=1, source_target_pairs={{0,16},{16,0},{1,17},{17,1},{2,18},{18,2},{3,19},{19,3},{4,20},{20... | collective-permute-start | bytes 589832 | tf_op jit(solution)/shard_map/ppermute | solution.py:28
  143.2 2.9 %collective-permute-start.25 = (bf16[512,256]{1,0:T(8,128)(2,1)S(1)}, bf16[512,256]{1,0:T(8,128)(2,1)S(1)}, u32[]{:S(2)}, u32[]{:S(2)}) collective-permute-start(bf16[512,256]{1,0:T(8,128)(2,1)S(1)} %bitcast.110), channel_id=1, source_target_pairs={{0,8},{8,0},{1,9},{9,1},{2,10},{10,2},{3,11},{11,3},{4,12},{12,4},... | collective-permute-start | bytes 786440 | tf_op jit(solution)/shard_map/ppermute | solution.py:28
  150.2 5.1 %collective-permute-start.29 = (bf16[4,128,128]{2,1,0:T(8,128)(2,1)S(1)}, bf16[4,128,128]{2,1,0:T(8,128)(2,1)S(1)}, u32[]{:S(2)}, u32[]{:S(2)}) collective-permute-start(bf16[4,128,128]{2,1,0:T(8,128)(2,1)S(1)} %slice_bitcast_fusion), channel_id=1, source_target_pairs={{0,1},{1,0},{2,3},{3,2},{4,5},{5,4},{6,7},{7,6},{8,9},{9,8},{10,11... | collective-permute-start | bytes 393224 | tf_op jit(solution)/shard_map/ppermute | solution.py:28
  151.4 6.3 %collective-permute-start.26 = (bf16[8,64,128]{2,1,0:T(8,128)(2,1)}, bf16[8,64,128]{2,1,0:T(8,128)(2,1)S(1)}, u32[]{:S(2)}, u32[]{:S(2)}) collective-permute-start(bf16[8,64,128]{2,1,0:T(8,128)(2,1)} %get-tuple-element.46), channel_id=1, source_target_pairs={{0,1},{1,0},{2,3},{3,2},{4,5},{5,4},{6,7},{7,6},{8,9},{9,8},{10,11... | collective-permute-start | bytes 393224 | tf_op jit(solution)/shard_map/ppermute | solution.py:28
  151.7 10.6 %collective-permute-start.27 = (bf16[8,64,128]{2,1,0:T(8,128)(2,1)}, bf16[8,64,128]{2,1,0:T(8,128)(2,1)S(1)}, u32[]{:S(2)}, u32[]{:S(2)}) collective-permute-start(bf16[8,64,128]{2,1,0:T(8,128)(2,1)} %get-tuple-element.47), channel_id=1, source_target_pairs={{0,16},{16,0},{1,17},{17,1},{2,18},{18,2},{3,19},{19,3},{4,20},{20... | collective-permute-start | bytes 393224 | tf_op jit(solution)/shard_map/ppermute | solution.py:28
  153.9 8.4 %collective-permute-start.28 = (bf16[8,64,128]{2,1,0:T(8,128)(2,1)}, bf16[8,64,128]{2,1,0:T(8,128)(2,1)S(1)}, u32[]{:S(2)}, u32[]{:S(2)}) collective-permute-start(bf16[8,64,128]{2,1,0:T(8,128)(2,1)} %get-tuple-element.48), channel_id=1, source_target_pairs={{0,17},{1,16},{16,1},{17,0},{2,19},{3,18},{18,3},{19,2},{4,21},{5,... | collective-permute-start | bytes 393224 | tf_op jit(solution)/shard_map/ppermute | solution.py:309
  (13 other events, 120.6 us)
Sparse Core Ops, SparseCore 0:
  25.2 41.6 all-gather.2
  77.8 55.1 reduce-scatter.1

commit v3 on v2

--- a/solution.py
+++ b/solution.py
@@ -272,9 +272,9 @@
     heads = everyone[:, NZ * QB :].reshape(NZ, 2, 2, count, QB)
     heads = jnp.stack([pick(heads, core, 2), pick(heads, 1 - core, 2)], axis=2)
     kept, sent = pick(heads, xh, 1), pick(heads, 1 - xh, 1)
-    got = swap(after(sent, part), "xh")
     pieces = lax.optimization_barrier((*pieces, part))[:-1]
     ways = z_first(pieces, z)
+    got = swap(after(sent, *ways), "xh")
     ways = z_next(pieces, z, 2, *ways)
     own = jnp.stack([kept, got], axis=1)
     down, up = shift(own, "y", NY, 1), shift(own, "y", NY, -1)

time: 189 us -> 188 us (level)
  waiting for transfers between devices: 62.3 us -> 55.8 us
  starting transfers between devices: 46.5 us -> 52.4 us
    ppermute x16, waiting for transfers between devices: 33.4 us -> 27.2 us  [shift(): return lax.ppermute(x, axis, [(i, (i + step) % size) for i in range(size)])]
    ppermute x13, starting transfers between devices: 19 us -> 25 us  [swap(): return lax.ppermute(x, axis, [(0, 1), (1, 0)])]
  transfers between devices with their start and end apart: 32 -> 32, of which waited for: 18 -> 19; matrix products, arithmetic and copies ran while one was open for 10% -> 10% of each run, Pallas kernels for 12% -> 12%
where the time goes in v3:
time: 188 us; the launch traced here: 185 us
  waiting for transfers between devices  55.8 us (30%)
  starting transfers between devices  52.4 us (28%)
  Pallas kernels  25.3 us (13%)
  local copies, waits for them, and re-layouts  14.6 us (8%)
  between operations  14.6 us (8%)
  blocking collectives  14.5 us (8%)
  other arithmetic  7.86 us (4%)
    ppermute x16, waiting for transfers between devices, shift(): return lax.ppermute(x, axis, [(i, (i + step) % size) for i in range(size)])  27.2 us
    ppermute x16, starting transfers between devices, shift(): return lax.ppermute(x, axis, [(i, (i + step) % size) for i in range(size)])  26.6 us
    ppermute x13, starting transfers between devices, swap(): return lax.ppermute(x, axis, [(0, 1), (1, 0)])  25 us
    ppermute x13, waiting for transfers between devices, swap(): return lax.ppermute(x, axis, [(0, 1), (1, 0)])  22.3 us
    all_to_all x1, blocking collectives, per_device(): blocks = lax.all_to_all(blocks, 'z', 0, 0, tiled=True).transpose(1, 0, 2)  14.5 us
    pallas_call x2, Pallas kernels, grad_parts(): pl.pallas_call(functools.partial(grad_kernel, groups, lefts, rights), gri...  13.6 us
    pallas_call x1, Pallas kernels, make_payload(): pl.pallas_call(functools.partial(payload_kernel, steps), grid=(rows // ti...  8.42 us
    reduce_scatter x1, waiting for transfers between devices, per_device(): late_part = lax.psum_scatter(part, 'z', scatter_dimension=0, tiled=False)  6.33 us
  transfers between devices with their start and end apart: 32, of which 19 were waited for; matrix products, arithmetic and copies ran while one was open for 10% of the time, Pallas kernels for 12%

profile of v3, /device:TPU:1, one launch (start us, length us, event | category | flops | bytes accessed | tf_op | source)
XLA Modules:
  0.0 185.2 jit_solution(18048454517377334165)
XLA Ops:
  8.9 2.2 %collective-permute-start = (bf16[512,1024]{1,0:T(8,128)(2,1)S(1)}, bf16[512,1024]{1,0:T(8,128)(2,1)}, u32[]{:S(2)}, u32[]{:S(2)}) collective-permute-start(bf16[512,1024]{1,0:T(8,128)(2,1)S(1)} %bitcast.102), channel_id=1, source_target_pairs={{0,2},{2,4},{4,6},{6,0},{1,3},{3,5},{5,7},{7,1},{8,10},{10,12},{12... | collective-permute-start | bytes 3145736 | tf_op jit(solution)/shard_map/ppermute | solution.py:24
  16.6 8.4 %shard_map.104 = bf16[1280,128]{1,0:T(8,128)(2,1)} custom-call(s32[16]{0:T(128)} %len_ref.1, bf16[16,16,128]{2,1,0:T(8,128)(2,1)} %bitcast.124, bf16[16,16,128]{2,1,0:T(8,128)(2,1)} %pad.7.nk_ref, bf16[16,16,128]{2,1,0:T(8,128)(2,1)} %pad.8.nv_ref, bf16[16,512,128]{2,1,0:T(8,128)(2,1)} %bitcast.127, bf16[16,512,128]{2,1,0:T(8,128)(2,1)} %bitcast.128, ...), custom_call_target="tpu_custom_call" | custom-call | flops 17179869184 | bytes 4194304 | tf_op jit(solution)/shard_map/pallas_call | solution.py:89
  25.1 8.4 %collective-permute-done.refs_1_ = bf16[512,1024]{1,0:T(8,128)(2,1)} collective-permute-done((bf16[512,1024]{1,0:T(8,128)(2,1)S(1)}, bf16[512,1024]{1,0:T(8,128)(2,1)}, u32[]{:S(2)}, u32[]{:S(2)}) %collective-permute-start) | collective-permute-done | bytes 1048608 | tf_op jit(solution)/shard_map/ppermute | solution.py:24
  33.5 1.9 %slice.89 = bf16[256,1024]{1,0:T(8,128)(2,1)} slice(bf16[512,1024]{1,0:T(8,128)(2,1)} %collective-permute-done.refs_1_), slice={[0:256], [0:1024]} | slice | bytes 1048576 | tf_op jit(solution)/shard_map/slice | solution.py:194
  37.0 1.9 %slice.90 = bf16[256,1024]{1,0:T(8,128)(2,1)} slice(bf16[512,1024]{1,0:T(8,128)(2,1)} %collective-permute-done.4.refs_3_), slice={[256:512], [0:1024]} | slice | bytes 1048576 | tf_op jit(solution)/shard_map/slice | solution.py:195
  40.5 4.4 %shard_map.105 = (bf16[8,256,128]{2,1,0:T(8,128)(2,1)S(1)}, bf16[8,256,128]{2,1,0:T(8,128)(2,1)S(1)}, bf16[8,256,128]{2,1,0:T(8,128)(2,1)S(1)}, bf16[8,256,128]{2,1,0:T(8,128)(2,1)S(1)}) custom-call(s32[1]{0:T(128)} %bitcast.10.core_ref, bf16[512,1024]{1,0:T(8,128)(2,1)S(1)} %bitcast.104, bf16[512,1024]{1,0:T(8,128)(2,1)} %collective-permute-done.refs_1_, ...), custom_call_target="tpu_custom_call" | custom-call | flops 1048576 | bytes 1024 | tf_op jit(solution)/shard_map/pallas_call | solution.py:133
  44.8 3.4 %collective-permute-start.2 = (bf16[8,256,128]{2,1,0:T(8,128)(2,1)S(1)}, bf16[8,256,128]{2,1,0:T(8,128)(2,1)S(1)}, u32[]{:S(2)}, u32[]{:S(2)}) collective-permute-start(bf16[8,256,128]{2,1,0:T(8,128)(2,1)S(1)} %get-tuple-element.30), channel_id=1, source_target_pairs={{0,8},{8,0},{1,9},{9,1},{2,10},{10,2},{3,11},{11,3},{4,12},{12,4},... | collective-permute-start | bytes 1572872 | tf_op jit(solution)/shard_map/ppermute | solution.py:28
  48.4 2.2 %collective-permute-done.5 = bf16[256,1024]{1,0:T(8,128)(2,1)} collective-permute-done((bf16[256,1024]{1,0:T(8,128)(2,1)}, bf16[256,1024]{1,0:T(8,128)(2,1)}, u32[]{:S(2)}, u32[]{:S(2)}) %collective-permute-start.5) | collective-permute-done | bytes 524320 | tf_op jit(solution)/shard_map/ppermute | solution.py:24
  53.7 3.7 %collective-permute-done.6.refs_5_ = bf16[1024,1024]{1,0:T(8,128)(2,1)} collective-permute-done((bf16[1024,1024]{1,0:T(8,128)(2,1)S(1)}, bf16[1024,1024]{1,0:T(8,128)(2,1)}, u32[]{:S(2)}, u32[]{:S(2)}) %collective-permute-start.6) | collective-permute-done | bytes 2097184 | tf_op jit(solution)/shard_map/ppermute | solution.py:28
  57.4 9.3 %shard_map.106 = (bf16[8,768,128]{2,1,0:T(8,128)(2,1)S(1)}, bf16[8,768,128]{2,1,0:T(8,128)(2,1)S(1)}, bf16[8,768,128]{2,1,0:T(8,128)(2,1)S(1)}, bf16[8,768,128]{2,1,0:T(8,128)(2,1)S(1)}) custom-call(s32[1]{0:T(128)} %bitcast.10.core_ref, bf16[512,1024]{1,0:T(8,128)(2,1)S(1)} %bitcast.105, bf16[512,1024]{1,0:T(8,128)(2,1)} %collective-permute-done.refs_1_, ...), custom_call_target="tpu_custom_call" | custom-call | flops 1048576 | bytes 1024 | tf_op jit(solution)/shard_map/pallas_call | solution.py:133
  66.7 3.5 %collective-permute-start.7 = (bf16[8,768,128]{2,1,0:T(8,128)(2,1)S(1)}, bf16[8,768,128]{2,1,0:T(8,128)(2,1)S(1)}, u32[]{:S(2)}, u32[]{:S(2)}) collective-permute-start(bf16[8,768,128]{2,1,0:T(8,128)(2,1)S(1)} %get-tuple-element.33), channel_id=1, source_target_pairs={{0,8},{8,0},{1,9},{9,1},{2,10},{10,2},{3,11},{11,3},{4,12},{12,4},... | collective-permute-start | bytes 4718600 | tf_op jit(solution)/shard_map/ppermute | solution.py:28
  70.2 2.9 %collective-permute-done.7 = bf16[8,768,128]{2,1,0:T(8,128)(2,1)S(1)} collective-permute-done((bf16[8,768,128]{2,1,0:T(8,128)(2,1)S(1)}, bf16[8,768,128]{2,1,0:T(8,128)(2,1)S(1)}, u32[]{:S(2)}, u32[]{:S(2)}) %collective-permute-start.7) | collective-permute-done | bytes 1572896 | tf_op jit(solution)/shard_map/ppermute | solution.py:28
  79.1 5.6 %collective-permute-start.10 = (bf16[256,128]{1,0:T(8,128)(2,1)S(1)}, bf16[256,128]{1,0:T(8,128)(2,1)S(1)}, u32[]{:S(2)}, u32[]{:S(2)}) collective-permute-start(bf16[256,128]{1,0:T(8,128)(2,1)S(1)} %get-tuple-element.64), channel_id=1, source_target_pairs={{0,224},{32,0},{64,32},{96,64},{128,96},{160,128},{192,160},{224,1... | collective-permute-start | bytes 196616 | tf_op jit(solution)/shard_map/ppermute | solution.py:24
  86.1 3.1 %collective-permute-start.18 = (bf16[512,128]{1,0:T(8,128)(2,1)S(1)}, bf16[512,128]{1,0:T(8,128)(2,1)S(1)}, u32[]{:S(2)}, u32[]{:S(2)}) collective-permute-start(bf16[512,128]{1,0:T(8,128)(2,1)S(1)} %pad_maximum_fusion.9), channel_id=1, source_target_pairs={{0,224},{32,0},{64,32},{96,64},{128,96},{160,128},{192,160},{224,1... | collective-permute-start | bytes 393224 | tf_op jit(solution)/shard_map/ppermute | solution.py:24
  89.5 2.8 %collective-permute-start.11 = (bf16[8,2,64,128]{3,2,1,0:T(8,128)(2,1)S(1)}, bf16[8,2,64,128]{3,2,1,0:T(8,128)(2,1)S(1)}, u32[]{:S(2)}, u32[]{:S(2)}) collective-permute-start(bf16[8,2,64,128]{3,2,1,0:T(8,128)(2,1)S(1)} %get-tuple-element.39), channel_id=1, source_target_pairs={{0,16},{16,0},{1,17},{17,1},{2,18},{18,2},{3,19},{19,3},{4,20},{20... | collective-permute-start | bytes 786440 | tf_op jit(solution)/shard_map/ppermute | solution.py:28
  92.8 3.2 %collective-permute-done.17 = bf16[512,128]{1,0:T(8,128)(2,1)S(1)} collective-permute-done((bf16[512,128]{1,0:T(8,128)(2,1)S(1)}, bf16[512,128]{1,0:T(8,128)(2,1)S(1)}, u32[]{:S(2)}, u32[]{:S(2)}) %collective-permute-start.17) | collective-permute-done | bytes 131104 | tf_op jit(solution)/shard_map/ppermute | solution.py:24
  97.2 2.4 %collective-permute-start.20 = (bf16[512,128]{1,0:T(8,128)(2,1)S(1)}, bf16[512,128]{1,0:T(8,128)(2,1)S(1)}, u32[]{:S(2)}, u32[]{:S(2)}) collective-permute-start(bf16[512,128]{1,0:T(8,128)(2,1)S(1)} %add_convert_fusion.7), channel_id=1, source_target_pairs={{0,224},{32,0},{64,32},{96,64},{128,96},{160,128},{192,160},{224,1... | collective-permute-start | bytes 393224 | tf_op jit(solution)/shard_map/ppermute | solution.py:24
  99.5 2.7 %collective-permute-start.14 = (bf16[8,2,2,64,128]{4,3,2,1,0:T(8,128)(2,1)S(1)}, bf16[8,2,2,64,128]{4,3,2,1,0:T(8,128)(2,1)S(1)}, u32[]{:S(2)}, u32[]{:S(2)}) collective-permute-start(bf16[8,2,2,64,128]{4,3,2,1,0:T(8,128)(2,1)S(1)} %pad_maximum_fusion.2.refs_0_), channel_id=1, source_target_pairs={{0,6},{2,0},{4,2},{6,4},{1,7},{3,1},{5,3},{7,5},{8,14},{10,8},{12,... | collective-permute-start | bytes 1572872 | tf_op jit(solution)/shard_map/ppermute | solution.py:24
  103.9 6.4 %collective-permute-done.19 = bf16[512,128]{1,0:T(8,128)(2,1)S(1)} collective-permute-done((bf16[512,128]{1,0:T(8,128)(2,1)S(1)}, bf16[512,128]{1,0:T(8,128)(2,1)S(1)}, u32[]{:S(2)}, u32[]{:S(2)}) %collective-permute-start.19) | collective-permute-done | bytes 131104 | tf_op jit(solution)/shard_map/ppermute | solution.py:24
  111.1 2.7 %collective-permute-start.22 = (bf16[512,128]{1,0:T(8,128)(2,1)S(1)}, bf16[512,128]{1,0:T(8,128)(2,1)S(1)}, u32[]{:S(2)}, u32[]{:S(2)}) collective-permute-start(bf16[512,128]{1,0:T(8,128)(2,1)S(1)} %add_convert_fusion.5), channel_id=1, source_target_pairs={{0,224},{32,0},{64,32},{96,64},{128,96},{160,128},{192,160},{224,1... | collective-permute-start | bytes 393224 | tf_op jit(solution)/shard_map/ppermute | solution.py:24
  116.2 3.2 %collective-permute-done.21 = bf16[512,128]{1,0:T(8,128)(2,1)S(1)} collective-permute-done((bf16[512,128]{1,0:T(8,128)(2,1)S(1)}, bf16[512,128]{1,0:T(8,128)(2,1)S(1)}, u32[]{:S(2)}, u32[]{:S(2)}) %collective-permute-start.21) | collective-permute-done | bytes 131104 | tf_op jit(solution)/shard_map/ppermute | solution.py:24
  119.5 3.0 %collective-permute-start.23 = (bf16[2,128,128]{2,1,0:T(8,128)(2,1)S(1)}, bf16[2,128,128]{2,1,0:T(8,128)(2,1)S(1)}, u32[]{:S(2)}, u32[]{:S(2)}) collective-permute-start(bf16[2,128,128]{2,1,0:T(8,128)(2,1)S(1)} %fusion.7), channel_id=1, source_target_pairs={{0,16},{16,0},{1,17},{17,1},{2,18},{18,2},{3,19},{19,3},{4,20},{20... | collective-permute-start | bytes 196616 | tf_op jit(solution)/shard_map/ppermute | solution.py:28
  122.8 2.7 %collective-permute-start.15 = (bf16[4,2,2,64,128]{4,3,2,1,0:T(8,128)(2,1)S(1)}, bf16[4,2,2,64,128]{4,3,2,1,0:T(8,128)(2,1)S(1)}, u32[]{:S(2)}, u32[]{:S(2)}) collective-permute-start(bf16[4,2,2,64,128]{4,3,2,1,0:T(8,128)(2,1)S(1)} %slice.92), channel_id=1, source_target_pairs={{0,6},{2,0},{4,2},{6,4},{1,7},{3,1},{5,3},{7,5},{8,14},{10,8},{12,... | collective-permute-start | bytes 786440 | tf_op jit(solution)/shard_map/ppermute | solution.py:24
  125.5 6.3 %reduce-scatter.2.cloned.1.call-done = bf16[1,1536,128]{2,1,0:T(8,128)(2,1)} async-done(((bf16[8,1536,128]{2,1,0:T(8,128)(2,1)}), bf16[1,1536,128]{2,1,0:T(8,128)(2,1)}) %reduce-scatter.2.cloned.1.call-update) | async-done | bytes 393232 | tf_op jit(solution)/shard_map/reduce_scatter | solution.py:264
  132.8 2.9 %collective-permute-start.24 = (bf16[6,128,128]{2,1,0:T(8,128)(2,1)S(1)}, bf16[6,128,128]{2,1,0:T(8,128)(2,1)S(1)}, u32[]{:S(2)}, u32[]{:S(2)}) collective-permute-start(bf16[6,128,128]{2,1,0:T(8,128)(2,1)S(1)} %dynamic-slice_bitcast_fusion), channel_id=1, source_target_pairs={{0,16},{16,0},{1,17},{17,1},{2,18},{18,2},{3,19},{19,3},{4,20},{20... | collective-permute-start | bytes 589832 | tf_op jit(solution)/shard_map/ppermute | solution.py:28
  135.7 4.2 %collective-permute-done.24 = bf16[6,128,128]{2,1,0:T(8,128)(2,1)S(1)} collective-permute-done((bf16[6,128,128]{2,1,0:T(8,128)(2,1)S(1)}, bf16[6,128,128]{2,1,0:T(8,128)(2,1)S(1)}, u32[]{:S(2)}, u32[]{:S(2)}) %collective-permute-start.24) | collective-permute-done | bytes 196640 | tf_op jit(solution)/shard_map/ppermute | solution.py:28
  141.7 2.1 %collective-permute-start.25 = (bf16[512,256]{1,0:T(8,128)(2,1)S(1)}, bf16[512,256]{1,0:T(8,128)(2,1)S(1)}, u32[]{:S(2)}, u32[]{:S(2)}) collective-permute-start(bf16[512,256]{1,0:T(8,128)(2,1)S(1)} %bitcast.110), channel_id=1, source_target_pairs={{0,8},{8,0},{1,9},{9,1},{2,10},{10,2},{3,11},{11,3},{4,12},{12,4},... | collective-permute-start | bytes 786440 | tf_op jit(solution)/shard_map/ppermute | solution.py:28
  145.6 3.2 %shard_map.107 = (f32[8,64,128]{2,1,0:T(8,128)}, bf16[8,64,128]{2,1,0:T(8,128)(2,1)}, bf16[8,64,128]{2,1,0:T(8,128)(2,1)}, bf16[8,64,128]{2,1,0:T(8,128)(2,1)}) custom-call(bf16[8,2,2,64,128]{4,3,2,1,0:T(8,128)(2,1)} %copy-done.3, bf16[8,2,2,64,128]{4,3,2,1,0:T(8,128)(2,1)} %copy-done.4, bf16[4,2,2,64,128]{4,3,2,1,0:T(8,128)(2,1)} %copy-done.7, ...), custom_call_target="tpu_custom_call" | custom-call | flops 536870912 | bytes 4194304 | tf_op jit(solution)/shard_map/pallas_call | solution.py:175
  150.5 2.8 %collective-permute-start.27 = (bf16[8,64,128]{2,1,0:T(8,128)(2,1)}, bf16[8,64,128]{2,1,0:T(8,128)(2,1)S(1)}, u32[]{:S(2)}, u32[]{:S(2)}) collective-permute-start(bf16[8,64,128]{2,1,0:T(8,128)(2,1)} %get-tuple-element.47), channel_id=1, source_target_pairs={{0,16},{16,0},{1,17},{17,1},{2,18},{18,2},{3,19},{19,3},{4,20},{20... | collective-permute-start | bytes 393224 | tf_op jit(solution)/shard_map/ppermute | solution.py:28
  154.2 2.4 %collective-permute-done.26 = bf16[8,64,128]{2,1,0:T(8,128)(2,1)S(1)} collective-permute-done((bf16[8,64,128]{2,1,0:T(8,128)(2,1)}, bf16[8,64,128]{2,1,0:T(8,128)(2,1)S(1)}, u32[]{:S(2)}, u32[]{:S(2)}) %collective-permute-start.26) | collective-permute-done | bytes 131104 | tf_op jit(solution)/shard_map/ppermute | solution.py:28
  156.6 5.1 %collective-permute-done.27 = bf16[8,64,128]{2,1,0:T(8,128)(2,1)S(1)} collective-permute-done((bf16[8,64,128]{2,1,0:T(8,128)(2,1)}, bf16[8,64,128]{2,1,0:T(8,128)(2,1)S(1)}, u32[]{:S(2)}, u32[]{:S(2)}) %collective-permute-start.27) | collective-permute-done | bytes 131104 | tf_op jit(solution)/shard_map/ppermute | solution.py:28
  161.8 14.5 %all_to_all.5 = bf16[8,192,128]{2,1,0:T(8,128)(2,1)S(1)} all-to-all(bf16[8,192,128]{2,1,0:T(8,128)(2,1)S(1)} %pad_maximum_fusion.4), channel_id=1, replica_groups=mesh['z'=8,'xh'=2,'c'=2,'y'=4,'xl'=2] {'z'}, dimensions={0} | all-to-all | bytes 786432 | tf_op jit(solution)/shard_map/all_to_all | solution.py:319
  (125 shorter events, 37.1 us)
Async XLA Ops:
  7.2 70.5 %all-gather.3.cloned.1.call-start = ((), (), s32[]{:S(2)}) async-start(), calls=%async_computation.3 | async-start | bytes 2949120 | tf_op jit(solution)/shard_map/all_gather | solution.py:253
  8.9 24.6 %collective-permute-start = (bf16[512,1024]{1,0:T(8,128)(2,1)S(1)}, bf16[512,1024]{1,0:T(8,128)(2,1)}, u32[]{:S(2)}, u32[]{:S(2)}) collective-permute-start(bf16[512,1024]{1,0:T(8,128)(2,1)S(1)} %bitcast.102), channel_id=1, source_target_pairs={{0,2},{2,4},{4,6},{6,0},{1,3},{3,5},{5,7},{7,1},{8,10},{10,12},{12... | collective-permute-start | bytes 3145736 | tf_op jit(solution)/shard_map/ppermute | solution.py:24
  11.1 25.9 %collective-permute-start.4 = (bf16[512,1024]{1,0:T(8,128)(2,1)S(1)}, bf16[512,1024]{1,0:T(8,128)(2,1)}, u32[]{:S(2)}, u32[]{:S(2)}) collective-permute-start(bf16[512,1024]{1,0:T(8,128)(2,1)S(1)} %bitcast.103), channel_id=1, source_target_pairs={{0,6},{2,0},{4,2},{6,4},{1,7},{3,1},{5,3},{7,5},{8,14},{10,8},{12,... | collective-permute-start | bytes 3145736 | tf_op jit(solution)/shard_map/ppermute | solution.py:24
  12.6 44.8 %collective-permute-start.6 = (bf16[1024,1024]{1,0:T(8,128)(2,1)S(1)}, bf16[1024,1024]{1,0:T(8,128)(2,1)}, u32[]{:S(2)}, u32[]{:S(2)}) collective-permute-start(bf16[1024,1024]{1,0:T(8,128)(2,1)S(1)} %copy-done), channel_id=1, source_target_pairs={{0,1},{1,0},{2,3},{3,2},{4,5},{5,4},{6,7},{7,6},{8,9},{9,8},{10,11... | collective-permute-start | bytes 6291464 | tf_op jit(solution)/shard_map/ppermute | solution.py:28
  25.0 106.8 %reduce-scatter.2.cloned.1.call-start = ((), (), s32[]{:S(2)}) async-start(), calls=%async_computation.2 | async-start | bytes 3538944 | tf_op jit(solution)/shard_map/reduce_scatter | solution.py:264
  35.4 12.9 %collective-permute-start.3 = (bf16[256,1024]{1,0:T(8,128)(2,1)}, bf16[256,1024]{1,0:T(8,128)(2,1)}, u32[]{:S(2)}, u32[]{:S(2)}) collective-permute-start(bf16[256,1024]{1,0:T(8,128)(2,1)} %slice.89), channel_id=1, source_target_pairs={{0,2},{2,4},{4,6},{6,0},{1,3},{3,5},{5,7},{7,1},{8,10},{10,12},{12... | collective-permute-start | bytes 1572872 | tf_op jit(solution)/shard_map/ppermute | solution.py:24
  38.8 11.7 %collective-permute-start.5 = (bf16[256,1024]{1,0:T(8,128)(2,1)}, bf16[256,1024]{1,0:T(8,128)(2,1)}, u32[]{:S(2)}, u32[]{:S(2)}) collective-permute-start(bf16[256,1024]{1,0:T(8,128)(2,1)} %slice.90), channel_id=1, source_target_pairs={{0,6},{2,0},{4,2},{6,4},{1,7},{3,1},{5,3},{7,5},{8,14},{10,8},{12,... | collective-permute-start | bytes 1572872 | tf_op jit(solution)/shard_map/ppermute | solution.py:24
  44.8 7.0 %collective-permute-start.2 = (bf16[8,256,128]{2,1,0:T(8,128)(2,1)S(1)}, bf16[8,256,128]{2,1,0:T(8,128)(2,1)S(1)}, u32[]{:S(2)}, u32[]{:S(2)}) collective-permute-start(bf16[8,256,128]{2,1,0:T(8,128)(2,1)S(1)} %get-tuple-element.30), channel_id=1, source_target_pairs={{0,8},{8,0},{1,9},{9,1},{2,10},{10,2},{3,11},{11,3},{4,12},{12,4},... | collective-permute-start | bytes 1572872 | tf_op jit(solution)/shard_map/ppermute | solution.py:28
  48.2 4.5 %collective-permute-start.1 = (bf16[8,256,128]{2,1,0:T(8,128)(2,1)S(1)}, bf16[8,256,128]{2,1,0:T(8,128)(2,1)S(1)}, u32[]{:S(2)}, u32[]{:S(2)}) collective-permute-start(bf16[8,256,128]{2,1,0:T(8,128)(2,1)S(1)} %get-tuple-element.28), channel_id=1, source_target_pairs={{0,8},{8,0},{1,9},{9,1},{2,10},{10,2},{3,11},{11,3},{4,12},{12,4},... | collective-permute-start | bytes 1572872 | tf_op jit(solution)/shard_map/ppermute | solution.py:28
  66.7 6.5 %collective-permute-start.7 = (bf16[8,768,128]{2,1,0:T(8,128)(2,1)S(1)}, bf16[8,768,128]{2,1,0:T(8,128)(2,1)S(1)}, u32[]{:S(2)}, u32[]{:S(2)}) collective-permute-start(bf16[8,768,128]{2,1,0:T(8,128)(2,1)S(1)} %get-tuple-element.33), channel_id=1, source_target_pairs={{0,8},{8,0},{1,9},{9,1},{2,10},{10,2},{3,11},{11,3},{4,12},{12,4},... | collective-permute-start | bytes 4718600 | tf_op jit(solution)/shard_map/ppermute | solution.py:28
  70.1 5.3 %collective-permute-start.8 = (bf16[8,768,128]{2,1,0:T(8,128)(2,1)S(1)}, bf16[8,768,128]{2,1,0:T(8,128)(2,1)S(1)}, u32[]{:S(2)}, u32[]{:S(2)}) collective-permute-start(bf16[8,768,128]{2,1,0:T(8,128)(2,1)S(1)} %get-tuple-element.35), channel_id=1, source_target_pairs={{0,8},{8,0},{1,9},{9,1},{2,10},{10,2},{3,11},{11,3},{4,12},{12,4},... | collective-permute-start | bytes 4718600 | tf_op jit(solution)/shard_map/ppermute | solution.py:28
  79.1 7.0 %collective-permute-start.10 = (bf16[256,128]{1,0:T(8,128)(2,1)S(1)}, bf16[256,128]{1,0:T(8,128)(2,1)S(1)}, u32[]{:S(2)}, u32[]{:S(2)}) collective-permute-start(bf16[256,128]{1,0:T(8,128)(2,1)S(1)} %get-tuple-element.64), channel_id=1, source_target_pairs={{0,224},{32,0},{64,32},{96,64},{128,96},{160,128},{192,160},{224,1... | collective-permute-start | bytes 196616 | tf_op jit(solution)/shard_map/ppermute | solution.py:24
  84.8 4.6 %collective-permute-start.9 = (bf16[256,128]{1,0:T(8,128)(2,1)S(1)}, bf16[256,128]{1,0:T(8,128)(2,1)S(1)}, u32[]{:S(2)}, u32[]{:S(2)}) collective-permute-start(bf16[256,128]{1,0:T(8,128)(2,1)S(1)} %get-tuple-element.58), channel_id=1, source_target_pairs={{0,32},{32,64},{64,96},{96,128},{128,160},{160,192},{192,224},{224... | collective-permute-start | bytes 196616 | tf_op jit(solution)/shard_map/ppermute | solution.py:24
  86.1 6.7 %collective-permute-start.18 = (bf16[512,128]{1,0:T(8,128)(2,1)S(1)}, bf16[512,128]{1,0:T(8,128)(2,1)S(1)}, u32[]{:S(2)}, u32[]{:S(2)}) collective-permute-start(bf16[512,128]{1,0:T(8,128)(2,1)S(1)} %pad_maximum_fusion.9), channel_id=1, source_target_pairs={{0,224},{32,0},{64,32},{96,64},{128,96},{160,128},{192,160},{224,1... | collective-permute-start | bytes 393224 | tf_op jit(solution)/shard_map/ppermute | solution.py:24
  89.4 6.6 %collective-permute-start.17 = (bf16[512,128]{1,0:T(8,128)(2,1)S(1)}, bf16[512,128]{1,0:T(8,128)(2,1)S(1)}, u32[]{:S(2)}, u32[]{:S(2)}) collective-permute-start(bf16[512,128]{1,0:T(8,128)(2,1)S(1)} %pad_maximum_fusion.8), channel_id=1, source_target_pairs={{0,32},{32,64},{64,96},{96,128},{128,160},{160,192},{192,224},{224... | collective-permute-start | bytes 393224 | tf_op jit(solution)/shard_map/ppermute | solution.py:24
  89.5 7.6 %collective-permute-start.11 = (bf16[8,2,64,128]{3,2,1,0:T(8,128)(2,1)S(1)}, bf16[8,2,64,128]{3,2,1,0:T(8,128)(2,1)S(1)}, u32[]{:S(2)}, u32[]{:S(2)}) collective-permute-start(bf16[8,2,64,128]{3,2,1,0:T(8,128)(2,1)S(1)} %get-tuple-element.39), channel_id=1, source_target_pairs={{0,16},{16,0},{1,17},{17,1},{2,18},{18,2},{3,19},{19,3},{4,20},{20... | collective-permute-start | bytes 786440 | tf_op jit(solution)/shard_map/ppermute | solution.py:28
  97.2 6.7 %collective-permute-start.20 = (bf16[512,128]{1,0:T(8,128)(2,1)S(1)}, bf16[512,128]{1,0:T(8,128)(2,1)S(1)}, u32[]{:S(2)}, u32[]{:S(2)}) collective-permute-start(bf16[512,128]{1,0:T(8,128)(2,1)S(1)} %add_convert_fusion.7), channel_id=1, source_target_pairs={{0,224},{32,0},{64,32},{96,64},{128,96},{160,128},{192,160},{224,1... | collective-permute-start | bytes 393224 | tf_op jit(solution)/shard_map/ppermute | solution.py:24
  99.5 11.4 %collective-permute-start.12 = (bf16[8,2,2,64,128]{4,3,2,1,0:T(8,128)(2,1)S(1)}, bf16[8,2,2,64,128]{4,3,2,1,0:T(8,128)(2,1)S(1)}, u32[]{:S(2)}, u32[]{:S(2)}) collective-permute-start(bf16[8,2,2,64,128]{4,3,2,1,0:T(8,128)(2,1)S(1)} %pad_maximum_fusion.2.refs_0_), channel_id=1, source_target_pairs={{0,2},{2,4},{4,6},{6,0},{1,3},{3,5},{5,7},{7,1},{8,10},{10,12},{12... | collective-permute-start | bytes 1572872 | tf_op jit(solution)/shard_map/ppermute | solution.py:24
  99.5 11.4 %collective-permute-start.14 = (bf16[8,2,2,64,128]{4,3,2,1,0:T(8,128)(2,1)S(1)}, bf16[8,2,2,64,128]{4,3,2,1,0:T(8,128)(2,1)S(1)}, u32[]{:S(2)}, u32[]{:S(2)}) collective-permute-start(bf16[8,2,2,64,128]{4,3,2,1,0:T(8,128)(2,1)S(1)} %pad_maximum_fusion.2.refs_0_), channel_id=1, source_target_pairs={{0,6},{2,0},{4,2},{6,4},{1,7},{3,1},{5,3},{7,5},{8,14},{10,8},{12,... | collective-permute-start | bytes 1572872 | tf_op jit(solution)/shard_map/ppermute | solution.py:24
  102.2 8.1 %collective-permute-start.19 = (bf16[512,128]{1,0:T(8,128)(2,1)S(1)}, bf16[512,128]{1,0:T(8,128)(2,1)S(1)}, u32[]{:S(2)}, u32[]{:S(2)}) collective-permute-start(bf16[512,128]{1,0:T(8,128)(2,1)S(1)} %add_convert_fusion.8), channel_id=1, source_target_pairs={{0,32},{32,64},{64,96},{96,128},{128,160},{160,192},{192,224},{224... | collective-permute-start | bytes 393224 | tf_op jit(solution)/shard_map/ppermute | solution.py:24
  111.0 8.5 %collective-permute-start.21 = (bf16[512,128]{1,0:T(8,128)(2,1)S(1)}, bf16[512,128]{1,0:T(8,128)(2,1)S(1)}, u32[]{:S(2)}, u32[]{:S(2)}) collective-permute-start(bf16[512,128]{1,0:T(8,128)(2,1)S(1)} %add_convert_fusion.6), channel_id=1, source_target_pairs={{0,32},{32,64},{64,96},{96,128},{128,160},{160,192},{192,224},{224... | collective-permute-start | bytes 393224 | tf_op jit(solution)/shard_map/ppermute | solution.py:24
  111.1 8.4 %collective-permute-start.22 = (bf16[512,128]{1,0:T(8,128)(2,1)S(1)}, bf16[512,128]{1,0:T(8,128)(2,1)S(1)}, u32[]{:S(2)}, u32[]{:S(2)}) collective-permute-start(bf16[512,128]{1,0:T(8,128)(2,1)S(1)} %add_convert_fusion.5), channel_id=1, source_target_pairs={{0,224},{32,0},{64,32},{96,64},{128,96},{160,128},{192,160},{224,1... | collective-permute-start | bytes 393224 | tf_op jit(solution)/shard_map/ppermute | solution.py:24
  114.7 7.9 %collective-permute-start.16 = (bf16[4,128,128]{2,1,0:T(8,128)(2,1)S(1)}, bf16[4,128,128]{2,1,0:T(8,128)(2,1)S(1)}, u32[]{:S(2)}, u32[]{:S(2)}) collective-permute-start(bf16[4,128,128]{2,1,0:T(8,128)(2,1)S(1)} %get-tuple-element.86), channel_id=1, source_target_pairs={{0,1},{1,0},{2,3},{3,2},{4,5},{5,4},{6,7},{7,6},{8,9},{9,8},{10,11... | collective-permute-start | bytes 393224 | tf_op jit(solution)/shard_map/ppermute | solution.py:28
  119.5 6.0 %collective-permute-start.23 = (bf16[2,128,128]{2,1,0:T(8,128)(2,1)S(1)}, bf16[2,128,128]{2,1,0:T(8,128)(2,1)S(1)}, u32[]{:S(2)}, u32[]{:S(2)}) collective-permute-start(bf16[2,128,128]{2,1,0:T(8,128)(2,1)S(1)} %fusion.7), channel_id=1, source_target_pairs={{0,16},{16,0},{1,17},{17,1},{2,18},{18,2},{3,19},{19,3},{4,20},{20... | collective-permute-start | bytes 196616 | tf_op jit(solution)/shard_map/ppermute | solution.py:28
  122.6 21.1 %collective-permute-start.13 = (bf16[4,2,2,64,128]{4,3,2,1,0:T(8,128)(2,1)S(1)}, bf16[4,2,2,64,128]{4,3,2,1,0:T(8,128)(2,1)S(1)}, u32[]{:S(2)}, u32[]{:S(2)}) collective-permute-start(bf16[4,2,2,64,128]{4,3,2,1,0:T(8,128)(2,1)S(1)} %slice.91), channel_id=1, source_target_pairs={{0,2},{2,4},{4,6},{6,0},{1,3},{3,5},{5,7},{7,1},{8,10},{10,12},{12... | collective-permute-start | bytes 786440 | tf_op jit(solution)/shard_map/ppermute | solution.py:24
  122.8 21.0 %collective-permute-start.15 = (bf16[4,2,2,64,128]{4,3,2,1,0:T(8,128)(2,1)S(1)}, bf16[4,2,2,64,128]{4,3,2,1,0:T(8,128)(2,1)S(1)}, u32[]{:S(2)}, u32[]{:S(2)}) collective-permute-start(bf16[4,2,2,64,128]{4,3,2,1,0:T(8,128)(2,1)S(1)} %slice.92), channel_id=1, source_target_pairs={{0,6},{2,0},{4,2},{6,4},{1,7},{3,1},{5,3},{7,5},{8,14},{10,8},{12,... | collective-permute-start | bytes 786440 | tf_op jit(solution)/shard_map/ppermute | solution.py:24
  132.8 7.1 %collective-permute-start.24 = (bf16[6,128,128]{2,1,0:T(8,128)(2,1)S(1)}, bf16[6,128,128]{2,1,0:T(8,128)(2,1)S(1)}, u32[]{:S(2)}, u32[]{:S(2)}) collective-permute-start(bf16[6,128,128]{2,1,0:T(8,128)(2,1)S(1)} %dynamic-slice_bitcast_fusion), channel_id=1, source_target_pairs={{0,16},{16,0},{1,17},{17,1},{2,18},{18,2},{3,19},{19,3},{4,20},{20... | collective-permute-start | bytes 589832 | tf_op jit(solution)/shard_map/ppermute | solution.py:28
  141.7 3.2 %collective-permute-start.25 = (bf16[512,256]{1,0:T(8,128)(2,1)S(1)}, bf16[512,256]{1,0:T(8,128)(2,1)S(1)}, u32[]{:S(2)}, u32[]{:S(2)}) collective-permute-start(bf16[512,256]{1,0:T(8,128)(2,1)S(1)} %bitcast.110), channel_id=1, source_target_pairs={{0,8},{8,0},{1,9},{9,1},{2,10},{10,2},{3,11},{11,3},{4,12},{12,4},... | collective-permute-start | bytes 786440 | tf_op jit(solution)/shard_map/ppermute | solution.py:28
  149.0 5.1 %collective-permute-start.29 = (bf16[4,128,128]{2,1,0:T(8,128)(2,1)S(1)}, bf16[4,128,128]{2,1,0:T(8,128)(2,1)S(1)}, u32[]{:S(2)}, u32[]{:S(2)}) collective-permute-start(bf16[4,128,128]{2,1,0:T(8,128)(2,1)S(1)} %slice_bitcast_fusion), channel_id=1, source_target_pairs={{0,1},{1,0},{2,3},{3,2},{4,5},{5,4},{6,7},{7,6},{8,9},{9,8},{10,11... | collective-permute-start | bytes 393224 | tf_op jit(solution)/shard_map/ppermute | solution.py:28
  150.2 6.3 %collective-permute-start.26 = (bf16[8,64,128]{2,1,0:T(8,128)(2,1)}, bf16[8,64,128]{2,1,0:T(8,128)(2,1)S(1)}, u32[]{:S(2)}, u32[]{:S(2)}) collective-permute-start(bf16[8,64,128]{2,1,0:T(8,128)(2,1)} %get-tuple-element.46), channel_id=1, source_target_pairs={{0,1},{1,0},{2,3},{3,2},{4,5},{5,4},{6,7},{7,6},{8,9},{9,8},{10,11... | collective-permute-start | bytes 393224 | tf_op jit(solution)/shard_map/ppermute | solution.py:28
  150.5 11.1 %collective-permute-start.27 = (bf16[8,64,128]{2,1,0:T(8,128)(2,1)}, bf16[8,64,128]{2,1,0:T(8,128)(2,1)S(1)}, u32[]{:S(2)}, u32[]{:S(2)}) collective-permute-start(bf16[8,64,128]{2,1,0:T(8,128)(2,1)} %get-tuple-element.47), channel_id=1, source_target_pairs={{0,16},{16,0},{1,17},{17,1},{2,18},{18,2},{3,19},{19,3},{4,20},{20... | collective-permute-start | bytes 393224 | tf_op jit(solution)/shard_map/ppermute | solution.py:28
  153.3 8.3 %collective-permute-start.28 = (bf16[8,64,128]{2,1,0:T(8,128)(2,1)}, bf16[8,64,128]{2,1,0:T(8,128)(2,1)S(1)}, u32[]{:S(2)}, u32[]{:S(2)}) collective-permute-start(bf16[8,64,128]{2,1,0:T(8,128)(2,1)} %get-tuple-element.48), channel_id=1, source_target_pairs={{0,17},{1,16},{16,1},{17,0},{2,19},{3,18},{18,3},{19,2},{4,21},{5,... | collective-permute-start | bytes 393224 | tf_op jit(solution)/shard_map/ppermute | solution.py:309
  (13 other events, 124.8 us)
Sparse Core Ops, SparseCore 0:
  25.2 41.6 all-gather.2
  77.9 53.9 reduce-scatter.1

commit v4 on v3

--- a/solution.py
+++ b/solution.py
@@ -263,18 +263,13 @@
     early, late = [(0, 0), (1, 0)], late[0] + late[1]
     late_part = lax.psum_scatter(part, "z", scatter_dimension=0, tiled=False)
 
-    blocks = lax.dynamic_slice_in_dim(everyone, z * QB, QB, axis=1).reshape(NY, 2, QB, QB)
-    blocks = after(blocks, part)
-    kept, sent = pick(blocks, xl, 1), pick(blocks, 1 - xl, 1)
-    blocks = jnp.stack([kept, swap(sent, "xl")], axis=1)
-    weight_here = jnp.stack([pick(blocks, (y - k) % NY) for k in range(NY)], axis=0)
-
     heads = everyone[:, NZ * QB :].reshape(NZ, 2, 2, count, QB)
     heads = jnp.stack([pick(heads, core, 2), pick(heads, 1 - core, 2)], axis=2)
     kept, sent = pick(heads, xh, 1), pick(heads, 1 - xh, 1)
     pieces = lax.optimization_barrier((*pieces, part))[:-1]
     ways = z_first(pieces, z)
     got = swap(after(sent, *ways), "xh")
+    first_hop = ways
     ways = z_next(pieces, z, 2, *ways)
     own = jnp.stack([kept, got], axis=1)
     down, up = shift(own, "y", NY, 1), shift(own, "y", NY, -1)
@@ -283,6 +278,12 @@
     far_b = shift(up[NZ // 2 :], "y", NY, -1)
     early_part = z_last(pieces, z, *lax.optimization_barrier((*ways, down, up))[:2])
     lefts = (own, down, far_a, far_b, up)
+
+    blocks = lax.dynamic_slice_in_dim(everyone, z * QB, QB, axis=1).reshape(NY, 2, QB, QB)
+    blocks = after(blocks, *first_hop)
+    kept, sent = pick(blocks, xl, 1), pick(blocks, 1 - xl, 1)
+    blocks = jnp.stack([kept, swap(sent, "xl")], axis=1)
+    weight_here = jnp.stack([pick(blocks, (y - k) % NY) for k in range(NY)], axis=0)
 
     sums = {}
     for names, part in ((early, early_part), (late, late_part)):

time: 188 us -> 188 us (level)
  no operation moved by 1% of the time
where the time goes in v4:
time: 188 us; the launch traced here: 185 us
  waiting for transfers between devices  55.8 us (30%)
  starting transfers between devices  52.4 us (28%)
  Pallas kernels  25.3 us (13%)
  local copies, waits for them, and re-layouts  14.6 us (8%)
  between operations  14.6 us (8%)
  blocking collectives  14.5 us (8%)
  other arithmetic  7.86 us (4%)
    ppermute x16, waiting for transfers between devices, shift(): return lax.ppermute(x, axis, [(i, (i + step) % size) for i in range(size)])  27.2 us
    ppermute x16, starting transfers between devices, shift(): return lax.ppermute(x, axis, [(i, (i + step) % size) for i in range(size)])  26.6 us
    ppermute x13, starting transfers between devices, swap(): return lax.ppermute(x, axis, [(0, 1), (1, 0)])  25 us
    ppermute x13, waiting for transfers between devices, swap(): return lax.ppermute(x, axis, [(0, 1), (1, 0)])  22.3 us
    all_to_all x1, blocking collectives, per_device(): blocks = lax.all_to_all(blocks, 'z', 0, 0, tiled=True).transpose(1, 0, 2)  14.5 us
    pallas_call x2, Pallas kernels, grad_parts(): pl.pallas_call(functools.partial(grad_kernel, groups, lefts, rights), gri...  13.6 us
    pallas_call x1, Pallas kernels, make_payload(): pl.pallas_call(functools.partial(payload_kernel, steps), grid=(rows // ti...  8.42 us
    reduce_scatter x1, waiting for transfers between devices, per_device(): late_part = lax.psum_scatter(part, 'z', scatter_dimension=0, tiled=False)  6.33 us
  transfers between devices with their start and end apart: 32, of which 19 were waited for; matrix products, arithmetic and copies ran while one was open for 10% of the time, Pallas kernels for 12%

profile of v4, /device:TPU:1, one launch (start us, length us, event | category | flops | bytes accessed | tf_op | source)
XLA Modules:
  0.0 185.2 jit_solution(18048454517377334165)
XLA Ops:
  8.9 2.2 %collective-permute-start = (bf16[512,1024]{1,0:T(8,128)(2,1)S(1)}, bf16[512,1024]{1,0:T(8,128)(2,1)}, u32[]{:S(2)}, u32[]{:S(2)}) collective-permute-start(bf16[512,1024]{1,0:T(8,128)(2,1)S(1)} %bitcast.102), channel_id=1, source_target_pairs={{0,2},{2,4},{4,6},{6,0},{1,3},{3,5},{5,7},{7,1},{8,10},{10,12},{12... | collective-permute-start | bytes 3145736 | tf_op jit(solution)/shard_map/ppermute | solution.py:24
  16.6 8.4 %shard_map.104 = bf16[1280,128]{1,0:T(8,128)(2,1)} custom-call(s32[16]{0:T(128)} %len_ref.1, bf16[16,16,128]{2,1,0:T(8,128)(2,1)} %bitcast.124, bf16[16,16,128]{2,1,0:T(8,128)(2,1)} %pad.7.nk_ref, bf16[16,16,128]{2,1,0:T(8,128)(2,1)} %pad.8.nv_ref, bf16[16,512,128]{2,1,0:T(8,128)(2,1)} %bitcast.127, bf16[16,512,128]{2,1,0:T(8,128)(2,1)} %bitcast.128, ...), custom_call_target="tpu_custom_call" | custom-call | flops 17179869184 | bytes 4194304 | tf_op jit(solution)/shard_map/pallas_call | solution.py:89
  25.1 8.4 %collective-permute-done.refs_1_ = bf16[512,1024]{1,0:T(8,128)(2,1)} collective-permute-done((bf16[512,1024]{1,0:T(8,128)(2,1)S(1)}, bf16[512,1024]{1,0:T(8,128)(2,1)}, u32[]{:S(2)}, u32[]{:S(2)}) %collective-permute-start) | collective-permute-done | bytes 1048608 | tf_op jit(solution)/shard_map/ppermute | solution.py:24
  33.5 1.9 %slice.89 = bf16[256,1024]{1,0:T(8,128)(2,1)} slice(bf16[512,1024]{1,0:T(8,128)(2,1)} %collective-permute-done.refs_1_), slice={[0:256], [0:1024]} | slice | bytes 1048576 | tf_op jit(solution)/shard_map/slice | solution.py:194
  37.0 1.9 %slice.90 = bf16[256,1024]{1,0:T(8,128)(2,1)} slice(bf16[512,1024]{1,0:T(8,128)(2,1)} %collective-permute-done.4.refs_3_), slice={[256:512], [0:1024]} | slice | bytes 1048576 | tf_op jit(solution)/shard_map/slice | solution.py:195
  40.5 4.4 %shard_map.105 = (bf16[8,256,128]{2,1,0:T(8,128)(2,1)S(1)}, bf16[8,256,128]{2,1,0:T(8,128)(2,1)S(1)}, bf16[8,256,128]{2,1,0:T(8,128)(2,1)S(1)}, bf16[8,256,128]{2,1,0:T(8,128)(2,1)S(1)}) custom-call(s32[1]{0:T(128)} %bitcast.10.core_ref, bf16[512,1024]{1,0:T(8,128)(2,1)S(1)} %bitcast.104, bf16[512,1024]{1,0:T(8,128)(2,1)} %collective-permute-done.refs_1_, ...), custom_call_target="tpu_custom_call" | custom-call | flops 1048576 | bytes 1024 | tf_op jit(solution)/shard_map/pallas_call | solution.py:133
  44.8 3.4 %collective-permute-start.2 = (bf16[8,256,128]{2,1,0:T(8,128)(2,1)S(1)}, bf16[8,256,128]{2,1,0:T(8,128)(2,1)S(1)}, u32[]{:S(2)}, u32[]{:S(2)}) collective-permute-start(bf16[8,256,128]{2,1,0:T(8,128)(2,1)S(1)} %get-tuple-element.30), channel_id=1, source_target_pairs={{0,8},{8,0},{1,9},{9,1},{2,10},{10,2},{3,11},{11,3},{4,12},{12,4},... | collective-permute-start | bytes 1572872 | tf_op jit(solution)/shard_map/ppermute | solution.py:28
  48.4 2.2 %collective-permute-done.5 = bf16[256,1024]{1,0:T(8,128)(2,1)} collective-permute-done((bf16[256,1024]{1,0:T(8,128)(2,1)}, bf16[256,1024]{1,0:T(8,128)(2,1)}, u32[]{:S(2)}, u32[]{:S(2)}) %collective-permute-start.5) | collective-permute-done | bytes 524320 | tf_op jit(solution)/shard_map/ppermute | solution.py:24
  53.7 3.7 %collective-permute-done.6.refs_5_ = bf16[1024,1024]{1,0:T(8,128)(2,1)} collective-permute-done((bf16[1024,1024]{1,0:T(8,128)(2,1)S(1)}, bf16[1024,1024]{1,0:T(8,128)(2,1)}, u32[]{:S(2)}, u32[]{:S(2)}) %collective-permute-start.6) | collective-permute-done | bytes 2097184 | tf_op jit(solution)/shard_map/ppermute | solution.py:28
  57.4 9.3 %shard_map.106 = (bf16[8,768,128]{2,1,0:T(8,128)(2,1)S(1)}, bf16[8,768,128]{2,1,0:T(8,128)(2,1)S(1)}, bf16[8,768,128]{2,1,0:T(8,128)(2,1)S(1)}, bf16[8,768,128]{2,1,0:T(8,128)(2,1)S(1)}) custom-call(s32[1]{0:T(128)} %bitcast.10.core_ref, bf16[512,1024]{1,0:T(8,128)(2,1)S(1)} %bitcast.105, bf16[512,1024]{1,0:T(8,128)(2,1)} %collective-permute-done.refs_1_, ...), custom_call_target="tpu_custom_call" | custom-call | flops 1048576 | bytes 1024 | tf_op jit(solution)/shard_map/pallas_call | solution.py:133
  66.7 3.5 %collective-permute-start.7 = (bf16[8,768,128]{2,1,0:T(8,128)(2,1)S(1)}, bf16[8,768,128]{2,1,0:T(8,128)(2,1)S(1)}, u32[]{:S(2)}, u32[]{:S(2)}) collective-permute-start(bf16[8,768,128]{2,1,0:T(8,128)(2,1)S(1)} %get-tuple-element.33), channel_id=1, source_target_pairs={{0,8},{8,0},{1,9},{9,1},{2,10},{10,2},{3,11},{11,3},{4,12},{12,4},... | collective-permute-start | bytes 4718600 | tf_op jit(solution)/shard_map/ppermute | solution.py:28
  70.2 2.9 %collective-permute-done.7 = bf16[8,768,128]{2,1,0:T(8,128)(2,1)S(1)} collective-permute-done((bf16[8,768,128]{2,1,0:T(8,128)(2,1)S(1)}, bf16[8,768,128]{2,1,0:T(8,128)(2,1)S(1)}, u32[]{:S(2)}, u32[]{:S(2)}) %collective-permute-start.7) | collective-permute-done | bytes 1572896 | tf_op jit(solution)/shard_map/ppermute | solution.py:28
  79.1 5.6 %collective-permute-start.10 = (bf16[256,128]{1,0:T(8,128)(2,1)S(1)}, bf16[256,128]{1,0:T(8,128)(2,1)S(1)}, u32[]{:S(2)}, u32[]{:S(2)}) collective-permute-start(bf16[256,128]{1,0:T(8,128)(2,1)S(1)} %get-tuple-element.64), channel_id=1, source_target_pairs={{0,224},{32,0},{64,32},{96,64},{128,96},{160,128},{192,160},{224,1... | collective-permute-start | bytes 196616 | tf_op jit(solution)/shard_map/ppermute | solution.py:24
  86.1 3.1 %collective-permute-start.18 = (bf16[512,128]{1,0:T(8,128)(2,1)S(1)}, bf16[512,128]{1,0:T(8,128)(2,1)S(1)}, u32[]{:S(2)}, u32[]{:S(2)}) collective-permute-start(bf16[512,128]{1,0:T(8,128)(2,1)S(1)} %pad_maximum_fusion.9), channel_id=1, source_target_pairs={{0,224},{32,0},{64,32},{96,64},{128,96},{160,128},{192,160},{224,1... | collective-permute-start | bytes 393224 | tf_op jit(solution)/shard_map/ppermute | solution.py:24
  89.5 2.8 %collective-permute-start.11 = (bf16[8,2,64,128]{3,2,1,0:T(8,128)(2,1)S(1)}, bf16[8,2,64,128]{3,2,1,0:T(8,128)(2,1)S(1)}, u32[]{:S(2)}, u32[]{:S(2)}) collective-permute-start(bf16[8,2,64,128]{3,2,1,0:T(8,128)(2,1)S(1)} %get-tuple-element.39), channel_id=1, source_target_pairs={{0,16},{16,0},{1,17},{17,1},{2,18},{18,2},{3,19},{19,3},{4,20},{20... | collective-permute-start | bytes 786440 | tf_op jit(solution)/shard_map/ppermute | solution.py:28
  92.8 3.2 %collective-permute-done.17 = bf16[512,128]{1,0:T(8,128)(2,1)S(1)} collective-permute-done((bf16[512,128]{1,0:T(8,128)(2,1)S(1)}, bf16[512,128]{1,0:T(8,128)(2,1)S(1)}, u32[]{:S(2)}, u32[]{:S(2)}) %collective-permute-start.17) | collective-permute-done | bytes 131104 | tf_op jit(solution)/shard_map/ppermute | solution.py:24
  97.2 2.4 %collective-permute-start.20 = (bf16[512,128]{1,0:T(8,128)(2,1)S(1)}, bf16[512,128]{1,0:T(8,128)(2,1)S(1)}, u32[]{:S(2)}, u32[]{:S(2)}) collective-permute-start(bf16[512,128]{1,0:T(8,128)(2,1)S(1)} %add_convert_fusion.7), channel_id=1, source_target_pairs={{0,224},{32,0},{64,32},{96,64},{128,96},{160,128},{192,160},{224,1... | collective-permute-start | bytes 393224 | tf_op jit(solution)/shard_map/ppermute | solution.py:24
  99.5 2.7 %collective-permute-start.14 = (bf16[8,2,2,64,128]{4,3,2,1,0:T(8,128)(2,1)S(1)}, bf16[8,2,2,64,128]{4,3,2,1,0:T(8,128)(2,1)S(1)}, u32[]{:S(2)}, u32[]{:S(2)}) collective-permute-start(bf16[8,2,2,64,128]{4,3,2,1,0:T(8,128)(2,1)S(1)} %pad_maximum_fusion.2.refs_0_), channel_id=1, source_target_pairs={{0,6},{2,0},{4,2},{6,4},{1,7},{3,1},{5,3},{7,5},{8,14},{10,8},{12,... | collective-permute-start | bytes 1572872 | tf_op jit(solution)/shard_map/ppermute | solution.py:24
  103.9 6.4 %collective-permute-done.19 = bf16[512,128]{1,0:T(8,128)(2,1)S(1)} collective-permute-done((bf16[512,128]{1,0:T(8,128)(2,1)S(1)}, bf16[512,128]{1,0:T(8,128)(2,1)S(1)}, u32[]{:S(2)}, u32[]{:S(2)}) %collective-permute-start.19) | collective-permute-done | bytes 131104 | tf_op jit(solution)/shard_map/ppermute | solution.py:24
  111.1 2.7 %collective-permute-start.22 = (bf16[512,128]{1,0:T(8,128)(2,1)S(1)}, bf16[512,128]{1,0:T(8,128)(2,1)S(1)}, u32[]{:S(2)}, u32[]{:S(2)}) collective-permute-start(bf16[512,128]{1,0:T(8,128)(2,1)S(1)} %add_convert_fusion.5), channel_id=1, source_target_pairs={{0,224},{32,0},{64,32},{96,64},{128,96},{160,128},{192,160},{224,1... | collective-permute-start | bytes 393224 | tf_op jit(solution)/shard_map/ppermute | solution.py:24
  116.2 3.2 %collective-permute-done.21 = bf16[512,128]{1,0:T(8,128)(2,1)S(1)} collective-permute-done((bf16[512,128]{1,0:T(8,128)(2,1)S(1)}, bf16[512,128]{1,0:T(8,128)(2,1)S(1)}, u32[]{:S(2)}, u32[]{:S(2)}) %collective-permute-start.21) | collective-permute-done | bytes 131104 | tf_op jit(solution)/shard_map/ppermute | solution.py:24
  119.5 3.0 %collective-permute-start.23 = (bf16[2,128,128]{2,1,0:T(8,128)(2,1)S(1)}, bf16[2,128,128]{2,1,0:T(8,128)(2,1)S(1)}, u32[]{:S(2)}, u32[]{:S(2)}) collective-permute-start(bf16[2,128,128]{2,1,0:T(8,128)(2,1)S(1)} %fusion.7), channel_id=1, source_target_pairs={{0,16},{16,0},{1,17},{17,1},{2,18},{18,2},{3,19},{19,3},{4,20},{20... | collective-permute-start | bytes 196616 | tf_op jit(solution)/shard_map/ppermute | solution.py:28
  122.8 2.7 %collective-permute-start.15 = (bf16[4,2,2,64,128]{4,3,2,1,0:T(8,128)(2,1)S(1)}, bf16[4,2,2,64,128]{4,3,2,1,0:T(8,128)(2,1)S(1)}, u32[]{:S(2)}, u32[]{:S(2)}) collective-permute-start(bf16[4,2,2,64,128]{4,3,2,1,0:T(8,128)(2,1)S(1)} %slice.92), channel_id=1, source_target_pairs={{0,6},{2,0},{4,2},{6,4},{1,7},{3,1},{5,3},{7,5},{8,14},{10,8},{12,... | collective-permute-start | bytes 786440 | tf_op jit(solution)/shard_map/ppermute | solution.py:24
  125.5 6.3 %reduce-scatter.2.cloned.1.call-done = bf16[1,1536,128]{2,1,0:T(8,128)(2,1)} async-done(((bf16[8,1536,128]{2,1,0:T(8,128)(2,1)}), bf16[1,1536,128]{2,1,0:T(8,128)(2,1)}) %reduce-scatter.2.cloned.1.call-update) | async-done | bytes 393232 | tf_op jit(solution)/shard_map/reduce_scatter | solution.py:264
  132.8 2.9 %collective-permute-start.24 = (bf16[6,128,128]{2,1,0:T(8,128)(2,1)S(1)}, bf16[6,128,128]{2,1,0:T(8,128)(2,1)S(1)}, u32[]{:S(2)}, u32[]{:S(2)}) collective-permute-start(bf16[6,128,128]{2,1,0:T(8,128)(2,1)S(1)} %dynamic-slice_bitcast_fusion), channel_id=1, source_target_pairs={{0,16},{16,0},{1,17},{17,1},{2,18},{18,2},{3,19},{19,3},{4,20},{20... | collective-permute-start | bytes 589832 | tf_op jit(solution)/shard_map/ppermute | solution.py:28
  135.7 4.2 %collective-permute-done.24 = bf16[6,128,128]{2,1,0:T(8,128)(2,1)S(1)} collective-permute-done((bf16[6,128,128]{2,1,0:T(8,128)(2,1)S(1)}, bf16[6,128,128]{2,1,0:T(8,128)(2,1)S(1)}, u32[]{:S(2)}, u32[]{:S(2)}) %collective-permute-start.24) | collective-permute-done | bytes 196640 | tf_op jit(solution)/shard_map/ppermute | solution.py:28
  141.7 2.1 %collective-permute-start.25 = (bf16[512,256]{1,0:T(8,128)(2,1)S(1)}, bf16[512,256]{1,0:T(8,128)(2,1)S(1)}, u32[]{:S(2)}, u32[]{:S(2)}) collective-permute-start(bf16[512,256]{1,0:T(8,128)(2,1)S(1)} %bitcast.110), channel_id=1, source_target_pairs={{0,8},{8,0},{1,9},{9,1},{2,10},{10,2},{3,11},{11,3},{4,12},{12,4},... | collective-permute-start | bytes 786440 | tf_op jit(solution)/shard_map/ppermute | solution.py:28
  145.6 3.2 %shard_map.107 = (f32[8,64,128]{2,1,0:T(8,128)}, bf16[8,64,128]{2,1,0:T(8,128)(2,1)}, bf16[8,64,128]{2,1,0:T(8,128)(2,1)}, bf16[8,64,128]{2,1,0:T(8,128)(2,1)}) custom-call(bf16[8,2,2,64,128]{4,3,2,1,0:T(8,128)(2,1)} %copy-done.3, bf16[8,2,2,64,128]{4,3,2,1,0:T(8,128)(2,1)} %copy-done.4, bf16[4,2,2,64,128]{4,3,2,1,0:T(8,128)(2,1)} %copy-done.7, ...), custom_call_target="tpu_custom_call" | custom-call | flops 536870912 | bytes 4194304 | tf_op jit(solution)/shard_map/pallas_call | solution.py:175
  150.5 2.8 %collective-permute-start.27 = (bf16[8,64,128]{2,1,0:T(8,128)(2,1)}, bf16[8,64,128]{2,1,0:T(8,128)(2,1)S(1)}, u32[]{:S(2)}, u32[]{:S(2)}) collective-permute-start(bf16[8,64,128]{2,1,0:T(8,128)(2,1)} %get-tuple-element.47), channel_id=1, source_target_pairs={{0,16},{16,0},{1,17},{17,1},{2,18},{18,2},{3,19},{19,3},{4,20},{20... | collective-permute-start | bytes 393224 | tf_op jit(solution)/shard_map/ppermute | solution.py:28
  154.2 2.4 %collective-permute-done.26 = bf16[8,64,128]{2,1,0:T(8,128)(2,1)S(1)} collective-permute-done((bf16[8,64,128]{2,1,0:T(8,128)(2,1)}, bf16[8,64,128]{2,1,0:T(8,128)(2,1)S(1)}, u32[]{:S(2)}, u32[]{:S(2)}) %collective-permute-start.26) | collective-permute-done | bytes 131104 | tf_op jit(solution)/shard_map/ppermute | solution.py:28
  156.6 5.1 %collective-permute-done.27 = bf16[8,64,128]{2,1,0:T(8,128)(2,1)S(1)} collective-permute-done((bf16[8,64,128]{2,1,0:T(8,128)(2,1)}, bf16[8,64,128]{2,1,0:T(8,128)(2,1)S(1)}, u32[]{:S(2)}, u32[]{:S(2)}) %collective-permute-start.27) | collective-permute-done | bytes 131104 | tf_op jit(solution)/shard_map/ppermute | solution.py:28
  161.8 14.5 %all_to_all.5 = bf16[8,192,128]{2,1,0:T(8,128)(2,1)S(1)} all-to-all(bf16[8,192,128]{2,1,0:T(8,128)(2,1)S(1)} %pad_maximum_fusion.4), channel_id=1, replica_groups=mesh['z'=8,'xh'=2,'c'=2,'y'=4,'xl'=2] {'z'}, dimensions={0} | all-to-all | bytes 786432 | tf_op jit(solution)/shard_map/all_to_all | solution.py:320
  (125 shorter events, 37.1 us)
Async XLA Ops:
  7.2 70.5 %all-gather.3.cloned.1.call-start = ((), (), s32[]{:S(2)}) async-start(), calls=%async_computation.3 | async-start | bytes 2949120 | tf_op jit(solution)/shard_map/all_gather | solution.py:253
  8.9 24.6 %collective-permute-start = (bf16[512,1024]{1,0:T(8,128)(2,1)S(1)}, bf16[512,1024]{1,0:T(8,128)(2,1)}, u32[]{:S(2)}, u32[]{:S(2)}) collective-permute-start(bf16[512,1024]{1,0:T(8,128)(2,1)S(1)} %bitcast.102), channel_id=1, source_target_pairs={{0,2},{2,4},{4,6},{6,0},{1,3},{3,5},{5,7},{7,1},{8,10},{10,12},{12... | collective-permute-start | bytes 3145736 | tf_op jit(solution)/shard_map/ppermute | solution.py:24
  11.1 25.9 %collective-permute-start.4 = (bf16[512,1024]{1,0:T(8,128)(2,1)S(1)}, bf16[512,1024]{1,0:T(8,128)(2,1)}, u32[]{:S(2)}, u32[]{:S(2)}) collective-permute-start(bf16[512,1024]{1,0:T(8,128)(2,1)S(1)} %bitcast.103), channel_id=1, source_target_pairs={{0,6},{2,0},{4,2},{6,4},{1,7},{3,1},{5,3},{7,5},{8,14},{10,8},{12,... | collective-permute-start | bytes 3145736 | tf_op jit(solution)/shard_map/ppermute | solution.py:24
  12.6 44.8 %collective-permute-start.6 = (bf16[1024,1024]{1,0:T(8,128)(2,1)S(1)}, bf16[1024,1024]{1,0:T(8,128)(2,1)}, u32[]{:S(2)}, u32[]{:S(2)}) collective-permute-start(bf16[1024,1024]{1,0:T(8,128)(2,1)S(1)} %copy-done), channel_id=1, source_target_pairs={{0,1},{1,0},{2,3},{3,2},{4,5},{5,4},{6,7},{7,6},{8,9},{9,8},{10,11... | collective-permute-start | bytes 6291464 | tf_op jit(solution)/shard_map/ppermute | solution.py:28
  25.0 106.8 %reduce-scatter.2.cloned.1.call-start = ((), (), s32[]{:S(2)}) async-start(), calls=%async_computation.2 | async-start | bytes 3538944 | tf_op jit(solution)/shard_map/reduce_scatter | solution.py:264
  35.4 12.9 %collective-permute-start.3 = (bf16[256,1024]{1,0:T(8,128)(2,1)}, bf16[256,1024]{1,0:T(8,128)(2,1)}, u32[]{:S(2)}, u32[]{:S(2)}) collective-permute-start(bf16[256,1024]{1,0:T(8,128)(2,1)} %slice.89), channel_id=1, source_target_pairs={{0,2},{2,4},{4,6},{6,0},{1,3},{3,5},{5,7},{7,1},{8,10},{10,12},{12... | collective-permute-start | bytes 1572872 | tf_op jit(solution)/shard_map/ppermute | solution.py:24
  38.8 11.7 %collective-permute-start.5 = (bf16[256,1024]{1,0:T(8,128)(2,1)}, bf16[256,1024]{1,0:T(8,128)(2,1)}, u32[]{:S(2)}, u32[]{:S(2)}) collective-permute-start(bf16[256,1024]{1,0:T(8,128)(2,1)} %slice.90), channel_id=1, source_target_pairs={{0,6},{2,0},{4,2},{6,4},{1,7},{3,1},{5,3},{7,5},{8,14},{10,8},{12,... | collective-permute-start | bytes 1572872 | tf_op jit(solution)/shard_map/ppermute | solution.py:24
  44.8 7.0 %collective-permute-start.2 = (bf16[8,256,128]{2,1,0:T(8,128)(2,1)S(1)}, bf16[8,256,128]{2,1,0:T(8,128)(2,1)S(1)}, u32[]{:S(2)}, u32[]{:S(2)}) collective-permute-start(bf16[8,256,128]{2,1,0:T(8,128)(2,1)S(1)} %get-tuple-element.30), channel_id=1, source_target_pairs={{0,8},{8,0},{1,9},{9,1},{2,10},{10,2},{3,11},{11,3},{4,12},{12,4},... | collective-permute-start | bytes 1572872 | tf_op jit(solution)/shard_map/ppermute | solution.py:28
  48.2 4.5 %collective-permute-start.1 = (bf16[8,256,128]{2,1,0:T(8,128)(2,1)S(1)}, bf16[8,256,128]{2,1,0:T(8,128)(2,1)S(1)}, u32[]{:S(2)}, u32[]{:S(2)}) collective-permute-start(bf16[8,256,128]{2,1,0:T(8,128)(2,1)S(1)} %get-tuple-element.28), channel_id=1, source_target_pairs={{0,8},{8,0},{1,9},{9,1},{2,10},{10,2},{3,11},{11,3},{4,12},{12,4},... | collective-permute-start | bytes 1572872 | tf_op jit(solution)/shard_map/ppermute | solution.py:28
  66.7 6.5 %collective-permute-start.7 = (bf16[8,768,128]{2,1,0:T(8,128)(2,1)S(1)}, bf16[8,768,128]{2,1,0:T(8,128)(2,1)S(1)}, u32[]{:S(2)}, u32[]{:S(2)}) collective-permute-start(bf16[8,768,128]{2,1,0:T(8,128)(2,1)S(1)} %get-tuple-element.33), channel_id=1, source_target_pairs={{0,8},{8,0},{1,9},{9,1},{2,10},{10,2},{3,11},{11,3},{4,12},{12,4},... | collective-permute-start | bytes 4718600 | tf_op jit(solution)/shard_map/ppermute | solution.py:28
  70.1 5.3 %collective-permute-start.8 = (bf16[8,768,128]{2,1,0:T(8,128)(2,1)S(1)}, bf16[8,768,128]{2,1,0:T(8,128)(2,1)S(1)}, u32[]{:S(2)}, u32[]{:S(2)}) collective-permute-start(bf16[8,768,128]{2,1,0:T(8,128)(2,1)S(1)} %get-tuple-element.35), channel_id=1, source_target_pairs={{0,8},{8,0},{1,9},{9,1},{2,10},{10,2},{3,11},{11,3},{4,12},{12,4},... | collective-permute-start | bytes 4718600 | tf_op jit(solution)/shard_map/ppermute | solution.py:28
  79.1 7.0 %collective-permute-start.10 = (bf16[256,128]{1,0:T(8,128)(2,1)S(1)}, bf16[256,128]{1,0:T(8,128)(2,1)S(1)}, u32[]{:S(2)}, u32[]{:S(2)}) collective-permute-start(bf16[256,128]{1,0:T(8,128)(2,1)S(1)} %get-tuple-element.64), channel_id=1, source_target_pairs={{0,224},{32,0},{64,32},{96,64},{128,96},{160,128},{192,160},{224,1... | collective-permute-start | bytes 196616 | tf_op jit(solution)/shard_map/ppermute | solution.py:24
  84.8 4.6 %collective-permute-start.9 = (bf16[256,128]{1,0:T(8,128)(2,1)S(1)}, bf16[256,128]{1,0:T(8,128)(2,1)S(1)}, u32[]{:S(2)}, u32[]{:S(2)}) collective-permute-start(bf16[256,128]{1,0:T(8,128)(2,1)S(1)} %get-tuple-element.58), channel_id=1, source_target_pairs={{0,32},{32,64},{64,96},{96,128},{128,160},{160,192},{192,224},{224... | collective-permute-start | bytes 196616 | tf_op jit(solution)/shard_map/ppermute | solution.py:24
  86.1 6.7 %collective-permute-start.18 = (bf16[512,128]{1,0:T(8,128)(2,1)S(1)}, bf16[512,128]{1,0:T(8,128)(2,1)S(1)}, u32[]{:S(2)}, u32[]{:S(2)}) collective-permute-start(bf16[512,128]{1,0:T(8,128)(2,1)S(1)} %pad_maximum_fusion.9), channel_id=1, source_target_pairs={{0,224},{32,0},{64,32},{96,64},{128,96},{160,128},{192,160},{224,1... | collective-permute-start | bytes 393224 | tf_op jit(solution)/shard_map/ppermute | solution.py:24
  89.4 6.6 %collective-permute-start.17 = (bf16[512,128]{1,0:T(8,128)(2,1)S(1)}, bf16[512,128]{1,0:T(8,128)(2,1)S(1)}, u32[]{:S(2)}, u32[]{:S(2)}) collective-permute-start(bf16[512,128]{1,0:T(8,128)(2,1)S(1)} %pad_maximum_fusion.8), channel_id=1, source_target_pairs={{0,32},{32,64},{64,96},{96,128},{128,160},{160,192},{192,224},{224... | collective-permute-start | bytes 393224 | tf_op jit(solution)/shard_map/ppermute | solution.py:24
  89.5 7.6 %collective-permute-start.11 = (bf16[8,2,64,128]{3,2,1,0:T(8,128)(2,1)S(1)}, bf16[8,2,64,128]{3,2,1,0:T(8,128)(2,1)S(1)}, u32[]{:S(2)}, u32[]{:S(2)}) collective-permute-start(bf16[8,2,64,128]{3,2,1,0:T(8,128)(2,1)S(1)} %get-tuple-element.39), channel_id=1, source_target_pairs={{0,16},{16,0},{1,17},{17,1},{2,18},{18,2},{3,19},{19,3},{4,20},{20... | collective-permute-start | bytes 786440 | tf_op jit(solution)/shard_map/ppermute | solution.py:28
  97.2 6.7 %collective-permute-start.20 = (bf16[512,128]{1,0:T(8,128)(2,1)S(1)}, bf16[512,128]{1,0:T(8,128)(2,1)S(1)}, u32[]{:S(2)}, u32[]{:S(2)}) collective-permute-start(bf16[512,128]{1,0:T(8,128)(2,1)S(1)} %add_convert_fusion.7), channel_id=1, source_target_pairs={{0,224},{32,0},{64,32},{96,64},{128,96},{160,128},{192,160},{224,1... | collective-permute-start | bytes 393224 | tf_op jit(solution)/shard_map/ppermute | solution.py:24
  99.5 11.4 %collective-permute-start.12 = (bf16[8,2,2,64,128]{4,3,2,1,0:T(8,128)(2,1)S(1)}, bf16[8,2,2,64,128]{4,3,2,1,0:T(8,128)(2,1)S(1)}, u32[]{:S(2)}, u32[]{:S(2)}) collective-permute-start(bf16[8,2,2,64,128]{4,3,2,1,0:T(8,128)(2,1)S(1)} %pad_maximum_fusion.2.refs_0_), channel_id=1, source_target_pairs={{0,2},{2,4},{4,6},{6,0},{1,3},{3,5},{5,7},{7,1},{8,10},{10,12},{12... | collective-permute-start | bytes 1572872 | tf_op jit(solution)/shard_map/ppermute | solution.py:24
  99.5 11.4 %collective-permute-start.14 = (bf16[8,2,2,64,128]{4,3,2,1,0:T(8,128)(2,1)S(1)}, bf16[8,2,2,64,128]{4,3,2,1,0:T(8,128)(2,1)S(1)}, u32[]{:S(2)}, u32[]{:S(2)}) collective-permute-start(bf16[8,2,2,64,128]{4,3,2,1,0:T(8,128)(2,1)S(1)} %pad_maximum_fusion.2.refs_0_), channel_id=1, source_target_pairs={{0,6},{2,0},{4,2},{6,4},{1,7},{3,1},{5,3},{7,5},{8,14},{10,8},{12,... | collective-permute-start | bytes 1572872 | tf_op jit(solution)/shard_map/ppermute | solution.py:24
  102.2 8.1 %collective-permute-start.19 = (bf16[512,128]{1,0:T(8,128)(2,1)S(1)}, bf16[512,128]{1,0:T(8,128)(2,1)S(1)}, u32[]{:S(2)}, u32[]{:S(2)}) collective-permute-start(bf16[512,128]{1,0:T(8,128)(2,1)S(1)} %add_convert_fusion.8), channel_id=1, source_target_pairs={{0,32},{32,64},{64,96},{96,128},{128,160},{160,192},{192,224},{224... | collective-permute-start | bytes 393224 | tf_op jit(solution)/shard_map/ppermute | solution.py:24
  111.0 8.5 %collective-permute-start.21 = (bf16[512,128]{1,0:T(8,128)(2,1)S(1)}, bf16[512,128]{1,0:T(8,128)(2,1)S(1)}, u32[]{:S(2)}, u32[]{:S(2)}) collective-permute-start(bf16[512,128]{1,0:T(8,128)(2,1)S(1)} %add_convert_fusion.6), channel_id=1, source_target_pairs={{0,32},{32,64},{64,96},{96,128},{128,160},{160,192},{192,224},{224... | collective-permute-start | bytes 393224 | tf_op jit(solution)/shard_map/ppermute | solution.py:24
  111.1 8.4 %collective-permute-start.22 = (bf16[512,128]{1,0:T(8,128)(2,1)S(1)}, bf16[512,128]{1,0:T(8,128)(2,1)S(1)}, u32[]{:S(2)}, u32[]{:S(2)}) collective-permute-start(bf16[512,128]{1,0:T(8,128)(2,1)S(1)} %add_convert_fusion.5), channel_id=1, source_target_pairs={{0,224},{32,0},{64,32},{96,64},{128,96},{160,128},{192,160},{224,1... | collective-permute-start | bytes 393224 | tf_op jit(solution)/shard_map/ppermute | solution.py:24
  114.7 7.9 %collective-permute-start.16 = (bf16[4,128,128]{2,1,0:T(8,128)(2,1)S(1)}, bf16[4,128,128]{2,1,0:T(8,128)(2,1)S(1)}, u32[]{:S(2)}, u32[]{:S(2)}) collective-permute-start(bf16[4,128,128]{2,1,0:T(8,128)(2,1)S(1)} %get-tuple-element.86), channel_id=1, source_target_pairs={{0,1},{1,0},{2,3},{3,2},{4,5},{5,4},{6,7},{7,6},{8,9},{9,8},{10,11... | collective-permute-start | bytes 393224 | tf_op jit(solution)/shard_map/ppermute | solution.py:28
  119.5 6.0 %collective-permute-start.23 = (bf16[2,128,128]{2,1,0:T(8,128)(2,1)S(1)}, bf16[2,128,128]{2,1,0:T(8,128)(2,1)S(1)}, u32[]{:S(2)}, u32[]{:S(2)}) collective-permute-start(bf16[2,128,128]{2,1,0:T(8,128)(2,1)S(1)} %fusion.7), channel_id=1, source_target_pairs={{0,16},{16,0},{1,17},{17,1},{2,18},{18,2},{3,19},{19,3},{4,20},{20... | collective-permute-start | bytes 196616 | tf_op jit(solution)/shard_map/ppermute | solution.py:28
  122.6 21.1 %collective-permute-start.13 = (bf16[4,2,2,64,128]{4,3,2,1,0:T(8,128)(2,1)S(1)}, bf16[4,2,2,64,128]{4,3,2,1,0:T(8,128)(2,1)S(1)}, u32[]{:S(2)}, u32[]{:S(2)}) collective-permute-start(bf16[4,2,2,64,128]{4,3,2,1,0:T(8,128)(2,1)S(1)} %slice.91), channel_id=1, source_target_pairs={{0,2},{2,4},{4,6},{6,0},{1,3},{3,5},{5,7},{7,1},{8,10},{10,12},{12... | collective-permute-start | bytes 786440 | tf_op jit(solution)/shard_map/ppermute | solution.py:24
  122.8 21.0 %collective-permute-start.15 = (bf16[4,2,2,64,128]{4,3,2,1,0:T(8,128)(2,1)S(1)}, bf16[4,2,2,64,128]{4,3,2,1,0:T(8,128)(2,1)S(1)}, u32[]{:S(2)}, u32[]{:S(2)}) collective-permute-start(bf16[4,2,2,64,128]{4,3,2,1,0:T(8,128)(2,1)S(1)} %slice.92), channel_id=1, source_target_pairs={{0,6},{2,0},{4,2},{6,4},{1,7},{3,1},{5,3},{7,5},{8,14},{10,8},{12,... | collective-permute-start | bytes 786440 | tf_op jit(solution)/shard_map/ppermute | solution.py:24
  132.8 7.1 %collective-permute-start.24 = (bf16[6,128,128]{2,1,0:T(8,128)(2,1)S(1)}, bf16[6,128,128]{2,1,0:T(8,128)(2,1)S(1)}, u32[]{:S(2)}, u32[]{:S(2)}) collective-permute-start(bf16[6,128,128]{2,1,0:T(8,128)(2,1)S(1)} %dynamic-slice_bitcast_fusion), channel_id=1, source_target_pairs={{0,16},{16,0},{1,17},{17,1},{2,18},{18,2},{3,19},{19,3},{4,20},{20... | collective-permute-start | bytes 589832 | tf_op jit(solution)/shard_map/ppermute | solution.py:28
  141.7 3.2 %collective-permute-start.25 = (bf16[512,256]{1,0:T(8,128)(2,1)S(1)}, bf16[512,256]{1,0:T(8,128)(2,1)S(1)}, u32[]{:S(2)}, u32[]{:S(2)}) collective-permute-start(bf16[512,256]{1,0:T(8,128)(2,1)S(1)} %bitcast.110), channel_id=1, source_target_pairs={{0,8},{8,0},{1,9},{9,1},{2,10},{10,2},{3,11},{11,3},{4,12},{12,4},... | collective-permute-start | bytes 786440 | tf_op jit(solution)/shard_map/ppermute | solution.py:28
  149.0 5.1 %collective-permute-start.29 = (bf16[4,128,128]{2,1,0:T(8,128)(2,1)S(1)}, bf16[4,128,128]{2,1,0:T(8,128)(2,1)S(1)}, u32[]{:S(2)}, u32[]{:S(2)}) collective-permute-start(bf16[4,128,128]{2,1,0:T(8,128)(2,1)S(1)} %slice_bitcast_fusion), channel_id=1, source_target_pairs={{0,1},{1,0},{2,3},{3,2},{4,5},{5,4},{6,7},{7,6},{8,9},{9,8},{10,11... | collective-permute-start | bytes 393224 | tf_op jit(solution)/shard_map/ppermute | solution.py:28
  150.2 6.3 %collective-permute-start.26 = (bf16[8,64,128]{2,1,0:T(8,128)(2,1)}, bf16[8,64,128]{2,1,0:T(8,128)(2,1)S(1)}, u32[]{:S(2)}, u32[]{:S(2)}) collective-permute-start(bf16[8,64,128]{2,1,0:T(8,128)(2,1)} %get-tuple-element.46), channel_id=1, source_target_pairs={{0,1},{1,0},{2,3},{3,2},{4,5},{5,4},{6,7},{7,6},{8,9},{9,8},{10,11... | collective-permute-start | bytes 393224 | tf_op jit(solution)/shard_map/ppermute | solution.py:28
  150.5 11.1 %collective-permute-start.27 = (bf16[8,64,128]{2,1,0:T(8,128)(2,1)}, bf16[8,64,128]{2,1,0:T(8,128)(2,1)S(1)}, u32[]{:S(2)}, u32[]{:S(2)}) collective-permute-start(bf16[8,64,128]{2,1,0:T(8,128)(2,1)} %get-tuple-element.47), channel_id=1, source_target_pairs={{0,16},{16,0},{1,17},{17,1},{2,18},{18,2},{3,19},{19,3},{4,20},{20... | collective-permute-start | bytes 393224 | tf_op jit(solution)/shard_map/ppermute | solution.py:28
  153.3 8.3 %collective-permute-start.28 = (bf16[8,64,128]{2,1,0:T(8,128)(2,1)}, bf16[8,64,128]{2,1,0:T(8,128)(2,1)S(1)}, u32[]{:S(2)}, u32[]{:S(2)}) collective-permute-start(bf16[8,64,128]{2,1,0:T(8,128)(2,1)} %get-tuple-element.48), channel_id=1, source_target_pairs={{0,17},{1,16},{16,1},{17,0},{2,19},{3,18},{18,3},{19,2},{4,21},{5,... | collective-permute-start | bytes 393224 | tf_op jit(solution)/shard_map/ppermute | solution.py:310
  (13 other events, 124.8 us)
Sparse Core Ops, SparseCore 0:
  25.2 41.6 all-gather.2
  77.9 53.9 reduce-scatter.1
